TPU v7x, 32 devices: a whole 2x2x4 slice. The times are simulated.
32 devices in a mesh: slab: 4 (over z), cross: 8 (over y, x, core).
Axes of the slice: x: 2, y: 2, z: 4, core: 2. Of those that a mesh axis runs over, the one named last changes fastest.
Arguments:
- thickness: int32 [4], P('slab'), may hold values from 1 to 4, as said below
- layer_sources: bfloat16 [16, 128, 32768], P('slab', None, 'cross'), may hold values from -6 to 6
- green_down: bfloat16 [4, 1536, 128, 128], P('slab', 'cross'), may hold values from -0.1875 to 0.1875
- column_down: int32 [4, 1536], P('slab', 'cross'), may hold values from 0 to 255, as said below
- green_up: bfloat16 [4, 1536, 128, 128], P('slab', 'cross'), may hold values from -0.1875 to 0.1875
- column_up: int32 [4, 1536], P('slab', 'cross'), may hold values from 0 to 255, as said below
Outputs:
- down_traces: bfloat16 [4, 128, 32768], P('slab', None, 'cross')
- up_traces: bfloat16 [4, 128, 32768], P('slab', None, 'cross')
Inputs may be any that keep to these rules, and one draw needn't show every extreme that they name: `thickness`: each slab has 1 to 4 layers; some slab has exactly 4 and another exactly 1. `column_down`: the 6 columns of block row i are distinct, each equals (i + o) modulo 256 for some o with -4 <= o <= 4, and they include (i + 4) modulo 256. `column_up`: as for column_down.
All inputs are finite; a program needn't handle non-finite values.
Results may differ from a plain program's by a relative error of at most 0.015.
Values may be sent and summed in bfloat16 or wider, within the bound.
No kernel may reach another device: no remote copies, remote signals or barrier semaphores. Data moves between devices by JAX's collectives and lax.ppermute only.
A program may use at most 64 MiB of HBM per device.

v0:
```python
import jax
import jax.numpy as jnp
from jax import lax
from jax.sharding import PartitionSpec as P

HB = 4
MB = 4
BM = 32


def padded(cells, sides, width):
    for axis, dim in sides:
        count = lax.axis_size(axis)
        head = lax.slice_in_dim(cells, 0, width, axis=dim)
        tail = lax.slice_in_dim(cells, cells.shape[dim] - width, cells.shape[dim], axis=dim)
        cells = jnp.concatenate(
            [
                lax.ppermute(tail, axis, [(i, (i + 1) % count) for i in range(count)]),
                cells,
                lax.ppermute(head, axis, [((i + 1) % count, i) for i in range(count)]),
            ],
            axis=dim,
        )
    return cells


def passed_along(block, axis, distance):
    devices = range(lax.axis_size(axis))
    route = [(i - distance, i) for i in devices if i - distance in devices]
    return lax.ppermute(block, axis, route)


def shards(thickness, layer_sources, green_down, column_down, green_up, column_up):
    slabs = lax.axis_size("slab")
    slab_id = lax.axis_index("slab")
    lateral = lax.axis_index("cross")
    depth = layer_sources.shape[0]
    width = layer_sources.shape[2]
    bsize = green_down.shape[-1]
    per_dev = width // bsize
    total_blocks = per_dev * lax.axis_size("cross")
    kcount = green_down.shape[1] // per_dev
    keep = (jnp.arange(depth) < thickness[0]).astype(jnp.float32)
    source = jnp.sum(layer_sources.astype(jnp.float32) * keep[:, None, None], axis=0)
    group = 1
    rows = BM * group
    groups = MB // group
    steps = slabs + groups - 1
    local_down = (column_down[0] - lateral * per_dev + HB) % total_blocks
    local_up = (column_up[0] - lateral * per_dev + HB) % total_blocks

    def product(extended, blocks, local_cols):
        tiles = extended.reshape(rows, per_dev + 2 * HB, bsize)
        picked = jnp.take(tiles, local_cols, axis=1)
        prod = jnp.einsum("mnb,nab->mna", picked, blocks, preferred_element_type=jnp.float32)
        return prod.reshape(rows, per_dev, kcount, bsize).sum(axis=2).reshape(rows, width)

    def finish(extended, blocks, local_cols, which, stored):
        active = jnp.logical_and(which >= 0, which < groups)
        start = jnp.clip(which, 0, groups - 1) * rows
        added = lax.dynamic_slice_in_dim(source, start, rows, 0)
        result = (product(extended, blocks, local_cols) + added).astype(jnp.bfloat16)
        current = lax.dynamic_slice_in_dim(stored, start, rows, 0)
        stored = lax.dynamic_update_slice_in_dim(
            stored, jnp.where(active, result, current), start, 0
        )
        return (result, stored)

    def one_step(step, carry):
        incoming_down, incoming_up, stored_down, stored_up = carry
        ext_down = padded(incoming_down, (("cross", 1),), HB * bsize)
        ext_up = padded(incoming_up, (("cross", 1),), HB * bsize)
        result_down, stored_down = finish(
            ext_down, green_down[0], local_down, step - slab_id, stored_down
        )
        result_up, stored_up = finish(
            ext_up, green_up[0], local_up, step - (slabs - 1 - slab_id), stored_up
        )
        incoming_down = passed_along(result_down, "slab", 1)
        incoming_up = passed_along(result_up, "slab", -1)
        return (incoming_down, incoming_up, stored_down, stored_up)

    empty = jnp.zeros((rows, width), jnp.bfloat16)
    stored = jnp.zeros((layer_sources.shape[1], width), jnp.bfloat16)
    final = lax.fori_loop(0, steps, one_step, (empty, empty, stored, stored))
    return (final[2][None], final[3][None])


def solution(mesh):
    return jax.shard_map(
        shards,
        mesh=mesh,
        in_specs=(
            P("slab"),
            P("slab", None, "cross"),
            P("slab", "cross", None, None),
            P("slab", "cross"),
            P("slab", "cross", None, None),
            P("slab", "cross"),
        ),
        out_specs=(P("slab", None, "cross"), P("slab", None, "cross")),
        check_vma=False,
    )
```

profile of v0, /device:TPU:0, one launch (start us, length us, event | category | flops | bytes accessed | tf_op | source)
XLA Modules:
  0.0 286.7 jit_solution(2195840468649293668)
XLA Ops:
  2.0 4.7 %multiply_reduce_fusion = f32[128,4096]{1,0:T(8,128)} fusion(bf16[4,128,4096]{2,1,0:T(8,128)(2,1)} %param.11, f32[4]{0:T(128)S(1)} %compare_convert_fusion), kind=kLoop, calls=%fused_computation.32 | loop fusion | flops 5767168 | bytes 6291472 | tf_op jit(solution)/shard_map/reduce_sum | solution.py:44
  8.9 277.9 %while.20 = (s32[]{:T(128)}, bf16[32,4096]{1,0:T(8,128)(2,1)S(1)}, bf16[32,4096]{1,0:T(8,128)(2,1)S(1)}, bf16[128,4096]{1,0:T(8,128)(2,1)}, bf16[128,4096]{1,0:T...) while((s32[]{:T(128)}, bf16[32,4096]{1,0:T(8,128)(2,1)S(1)}, ...), condition=%wide.region_4.6_spmd, body=%wide.region_1.5_spmd.sunk | while | flops 408294784 | bytes 43533184 | solution.py:85
  18.9 6.7 %fusion.43 = f32[192,32,128]{2,1,0:T(8,128)S(1)} fusion(bf16[1,192,128,128]{3,2,1,0:T(8,128)(2,1)} %get-tuple-element.424, bf16[192,32,128]{2,1,0:T(8,128)(2,1)} %gather_fusion.1, pred[192]{0:T(512)(128)(4,1)} %get-tuple-element.371), kind=kOutput, calls=%fused_computation.2.clone.1 | convolution fusion | flops 202113024 | bytes 11010240 | tf_op jit(solution)/shard_map/while/body/eval_jaxpr/mnb,nab->mna/dot_general | solution.py:55
  28.8 6.7 %fusion.41 = f32[192,32,128]{2,1,0:T(8,128)S(1)} fusion(bf16[1,192,128,128]{3,2,1,0:T(8,128)(2,1)} %get-tuple-element.420, bf16[192,32,128]{2,1,0:T(8,128)(2,1)} %gather_fusion, pred[192]{0:T(512)(128)(4,1)S(1)} %get-tuple-element.367), kind=kOutput, calls=%fused_computation.4.clone.1 | convolution fusion | flops 202113024 | bytes 11010240 | tf_op jit(solution)/shard_map/while/body/eval_jaxpr/mnb,nab->mna/dot_general | solution.py:55
  39.4 3.5 %collective-permute-start.4 = (bf16[32,4096]{1,0:T(8,128)(2,1)S(1)}, bf16[32,4096]{1,0:T(8,128)(2,1)S(1)}, u32[]{:S(2)}, u32[]{:S(2)}) collective-permute-start(bf16[32,4096]{1,0:T(8,128)(2,1)S(1)} %get-tuple-element.372), channel_id=1, source_target_pairs={{0,8},{8,16},{16,24},{1,9},{9,17},{17,25},{2,10},{10,18},{18,26},{... | collective-permute-start | bytes 786440 | tf_op jit(solution)/shard_map/while/body/eval_jaxpr/ppermute | solution.py:30
  46.7 4.4 %collective-permute-done.5 = bf16[32,4096]{1,0:T(8,128)(2,1)S(1)} collective-permute-done((bf16[32,4096]{1,0:T(8,128)(2,1)S(1)}, bf16[32,4096]{1,0:T(8,128)(2,1)S(1)}, u32[]{:S(2)}, u32[]{:S(2)}) %collective-permute-start.5) | collective-permute-done | bytes 262176 | tf_op jit(solution)/shard_map/while/body/eval_jaxpr/ppermute | solution.py:30
  59.3 6.7 %fusion.43 = f32[192,32,128]{2,1,0:T(8,128)S(1)} fusion(bf16[1,192,128,128]{3,2,1,0:T(8,128)(2,1)} %get-tuple-element.424, bf16[192,32,128]{2,1,0:T(8,128)(2,1)} %gather_fusion.1, pred[192]{0:T(512)(128)(4,1)} %get-tuple-element.371), kind=kOutput, calls=%fused_computation.2.clone.1 | convolution fusion | flops 202113024 | bytes 11010240 | tf_op jit(solution)/shard_map/while/body/eval_jaxpr/mnb,nab->mna/dot_general | solution.py:55
  69.3 6.7 %fusion.41 = f32[192,32,128]{2,1,0:T(8,128)S(1)} fusion(bf16[1,192,128,128]{3,2,1,0:T(8,128)(2,1)} %get-tuple-element.420, bf16[192,32,128]{2,1,0:T(8,128)(2,1)} %gather_fusion, pred[192]{0:T(512)(128)(4,1)S(1)} %get-tuple-element.367), kind=kOutput, calls=%fused_computation.4.clone.1 | convolution fusion | flops 202113024 | bytes 11010240 | tf_op jit(solution)/shard_map/while/body/eval_jaxpr/mnb,nab->mna/dot_general | solution.py:55
  87.1 4.4 %collective-permute-done.5 = bf16[32,4096]{1,0:T(8,128)(2,1)S(1)} collective-permute-done((bf16[32,4096]{1,0:T(8,128)(2,1)S(1)}, bf16[32,4096]{1,0:T(8,128)(2,1)S(1)}, u32[]{:S(2)}, u32[]{:S(2)}) %collective-permute-start.5) | collective-permute-done | bytes 262176 | tf_op jit(solution)/shard_map/while/body/eval_jaxpr/ppermute | solution.py:30
  99.6 6.7 %fusion.43 = f32[192,32,128]{2,1,0:T(8,128)S(1)} fusion(bf16[1,192,128,128]{3,2,1,0:T(8,128)(2,1)} %get-tuple-element.424, bf16[192,32,128]{2,1,0:T(8,128)(2,1)} %gather_fusion.1, pred[192]{0:T(512)(128)(4,1)} %get-tuple-element.371), kind=kOutput, calls=%fused_computation.2.clone.1 | convolution fusion | flops 202113024 | bytes 11010240 | tf_op jit(solution)/shard_map/while/body/eval_jaxpr/mnb,nab->mna/dot_general | solution.py:55
  109.6 6.7 %fusion.41 = f32[192,32,128]{2,1,0:T(8,128)S(1)} fusion(bf16[1,192,128,128]{3,2,1,0:T(8,128)(2,1)} %get-tuple-element.420, bf16[192,32,128]{2,1,0:T(8,128)(2,1)} %gather_fusion, pred[192]{0:T(512)(128)(4,1)S(1)} %get-tuple-element.367), kind=kOutput, calls=%fused_computation.4.clone.1 | convolution fusion | flops 202113024 | bytes 11010240 | tf_op jit(solution)/shard_map/while/body/eval_jaxpr/mnb,nab->mna/dot_general | solution.py:55
  127.4 4.4 %collective-permute-done.5 = bf16[32,4096]{1,0:T(8,128)(2,1)S(1)} collective-permute-done((bf16[32,4096]{1,0:T(8,128)(2,1)S(1)}, bf16[32,4096]{1,0:T(8,128)(2,1)S(1)}, u32[]{:S(2)}, u32[]{:S(2)}) %collective-permute-start.5) | collective-permute-done | bytes 262176 | tf_op jit(solution)/shard_map/while/body/eval_jaxpr/ppermute | solution.py:30
  139.9 6.7 %fusion.43 = f32[192,32,128]{2,1,0:T(8,128)S(1)} fusion(bf16[1,192,128,128]{3,2,1,0:T(8,128)(2,1)} %get-tuple-element.424, bf16[192,32,128]{2,1,0:T(8,128)(2,1)} %gather_fusion.1, pred[192]{0:T(512)(128)(4,1)} %get-tuple-element.371), kind=kOutput, calls=%fused_computation.2.clone.1 | convolution fusion | flops 202113024 | bytes 11010240 | tf_op jit(solution)/shard_map/while/body/eval_jaxpr/mnb,nab->mna/dot_general | solution.py:55
  149.8 6.7 %fusion.41 = f32[192,32,128]{2,1,0:T(8,128)S(1)} fusion(bf16[1,192,128,128]{3,2,1,0:T(8,128)(2,1)} %get-tuple-element.420, bf16[192,32,128]{2,1,0:T(8,128)(2,1)} %gather_fusion, pred[192]{0:T(512)(128)(4,1)S(1)} %get-tuple-element.367), kind=kOutput, calls=%fused_computation.4.clone.1 | convolution fusion | flops 202113024 | bytes 11010240 | tf_op jit(solution)/shard_map/while/body/eval_jaxpr/mnb,nab->mna/dot_general | solution.py:55
  166.2 4.4 %collective-permute-done.5 = bf16[32,4096]{1,0:T(8,128)(2,1)S(1)} collective-permute-done((bf16[32,4096]{1,0:T(8,128)(2,1)S(1)}, bf16[32,4096]{1,0:T(8,128)(2,1)S(1)}, u32[]{:S(2)}, u32[]{:S(2)}) %collective-permute-start.5) | collective-permute-done | bytes 262176 | tf_op jit(solution)/shard_map/while/body/eval_jaxpr/ppermute | solution.py:30
  178.6 6.7 %fusion.43 = f32[192,32,128]{2,1,0:T(8,128)S(1)} fusion(bf16[1,192,128,128]{3,2,1,0:T(8,128)(2,1)} %get-tuple-element.424, bf16[192,32,128]{2,1,0:T(8,128)(2,1)} %gather_fusion.1, pred[192]{0:T(512)(128)(4,1)} %get-tuple-element.371), kind=kOutput, calls=%fused_computation.2.clone.1 | convolution fusion | flops 202113024 | bytes 11010240 | tf_op jit(solution)/shard_map/while/body/eval_jaxpr/mnb,nab->mna/dot_general | solution.py:55
  188.6 6.7 %fusion.41 = f32[192,32,128]{2,1,0:T(8,128)S(1)} fusion(bf16[1,192,128,128]{3,2,1,0:T(8,128)(2,1)} %get-tuple-element.420, bf16[192,32,128]{2,1,0:T(8,128)(2,1)} %gather_fusion, pred[192]{0:T(512)(128)(4,1)S(1)} %get-tuple-element.367), kind=kOutput, calls=%fused_computation.4.clone.1 | convolution fusion | flops 202113024 | bytes 11010240 | tf_op jit(solution)/shard_map/while/body/eval_jaxpr/mnb,nab->mna/dot_general | solution.py:55
  204.9 4.4 %collective-permute-done.5 = bf16[32,4096]{1,0:T(8,128)(2,1)S(1)} collective-permute-done((bf16[32,4096]{1,0:T(8,128)(2,1)S(1)}, bf16[32,4096]{1,0:T(8,128)(2,1)S(1)}, u32[]{:S(2)}, u32[]{:S(2)}) %collective-permute-start.5) | collective-permute-done | bytes 262176 | tf_op jit(solution)/shard_map/while/body/eval_jaxpr/ppermute | solution.py:30
  217.4 6.7 %fusion.43 = f32[192,32,128]{2,1,0:T(8,128)S(1)} fusion(bf16[1,192,128,128]{3,2,1,0:T(8,128)(2,1)} %get-tuple-element.424, bf16[192,32,128]{2,1,0:T(8,128)(2,1)} %gather_fusion.1, pred[192]{0:T(512)(128)(4,1)} %get-tuple-element.371), kind=kOutput, calls=%fused_computation.2.clone.1 | convolution fusion | flops 202113024 | bytes 11010240 | tf_op jit(solution)/shard_map/while/body/eval_jaxpr/mnb,nab->mna/dot_general | solution.py:55
  227.3 6.7 %fusion.41 = f32[192,32,128]{2,1,0:T(8,128)S(1)} fusion(bf16[1,192,128,128]{3,2,1,0:T(8,128)(2,1)} %get-tuple-element.420, bf16[192,32,128]{2,1,0:T(8,128)(2,1)} %gather_fusion, pred[192]{0:T(512)(128)(4,1)S(1)} %get-tuple-element.367), kind=kOutput, calls=%fused_computation.4.clone.1 | convolution fusion | flops 202113024 | bytes 11010240 | tf_op jit(solution)/shard_map/while/body/eval_jaxpr/mnb,nab->mna/dot_general | solution.py:55
  243.6 4.4 %collective-permute-done.5 = bf16[32,4096]{1,0:T(8,128)(2,1)S(1)} collective-permute-done((bf16[32,4096]{1,0:T(8,128)(2,1)S(1)}, bf16[32,4096]{1,0:T(8,128)(2,1)S(1)}, u32[]{:S(2)}, u32[]{:S(2)}) %collective-permute-start.5) | collective-permute-done | bytes 262176 | tf_op jit(solution)/shard_map/while/body/eval_jaxpr/ppermute | solution.py:30
  256.1 6.7 %fusion.43 = f32[192,32,128]{2,1,0:T(8,128)S(1)} fusion(bf16[1,192,128,128]{3,2,1,0:T(8,128)(2,1)} %get-tuple-element.424, bf16[192,32,128]{2,1,0:T(8,128)(2,1)} %gather_fusion.1, pred[192]{0:T(512)(128)(4,1)} %get-tuple-element.371), kind=kOutput, calls=%fused_computation.2.clone.1 | convolution fusion | flops 202113024 | bytes 11010240 | tf_op jit(solution)/shard_map/while/body/eval_jaxpr/mnb,nab->mna/dot_general | solution.py:55
  266.0 6.7 %fusion.41 = f32[192,32,128]{2,1,0:T(8,128)S(1)} fusion(bf16[1,192,128,128]{3,2,1,0:T(8,128)(2,1)} %get-tuple-element.420, bf16[192,32,128]{2,1,0:T(8,128)(2,1)} %gather_fusion, pred[192]{0:T(512)(128)(4,1)S(1)} %get-tuple-element.367), kind=kOutput, calls=%fused_computation.4.clone.1 | convolution fusion | flops 202113024 | bytes 11010240 | tf_op jit(solution)/shard_map/while/body/eval_jaxpr/mnb,nab->mna/dot_general | solution.py:55
  282.3 4.4 %collective-permute-done.5 = bf16[32,4096]{1,0:T(8,128)(2,1)S(1)} collective-permute-done((bf16[32,4096]{1,0:T(8,128)(2,1)S(1)}, bf16[32,4096]{1,0:T(8,128)(2,1)S(1)}, u32[]{:S(2)}, u32[]{:S(2)}) %collective-permute-start.5) | collective-permute-done | bytes 262176 | tf_op jit(solution)/shard_map/while/body/eval_jaxpr/ppermute | solution.py:30
  (175 shorter events, 152.3 us)
Async XLA Ops:
  12.3 14.5 %collective-permute-start = (bf16[32,512]{1,0:T(8,128)(2,1)S(1)}, bf16[32,512]{1,0:T(8,128)(2,1)S(1)}, u32[]{:S(2)}, u32[]{:S(2)}) collective-permute-start(bf16[32,512]{1,0:T(8,128)(2,1)S(1)} %get-tuple-element.364), channel_id=1, source_target_pairs={{1,0},{2,1},{3,2},{4,3},{5,4},{6,5},{7,6},{0,7},{9,8},{10,9},{11,1... | collective-permute-start | bytes 98312 | tf_op jit(solution)/shard_map/while/body/eval_jaxpr/ppermute | solution.py:20
  14.9 11.8 %collective-permute-start.1 = (bf16[32,512]{1,0:T(8,128)(2,1)S(1)}, bf16[32,512]{1,0:T(8,128)(2,1)S(1)}, u32[]{:S(2)}, u32[]{:S(2)}) collective-permute-start(bf16[32,512]{1,0:T(8,128)(2,1)S(1)} %get-tuple-element.365), channel_id=1, source_target_pairs={{0,1},{1,2},{2,3},{3,4},{4,5},{5,6},{6,7},{7,0},{8,9},{9,10},{10,1... | collective-permute-start | bytes 98312 | tf_op jit(solution)/shard_map/while/body/eval_jaxpr/ppermute | solution.py:18
  39.4 7.3 %collective-permute-start.4 = (bf16[32,4096]{1,0:T(8,128)(2,1)S(1)}, bf16[32,4096]{1,0:T(8,128)(2,1)S(1)}, u32[]{:S(2)}, u32[]{:S(2)}) collective-permute-start(bf16[32,4096]{1,0:T(8,128)(2,1)S(1)} %get-tuple-element.372), channel_id=1, source_target_pairs={{0,8},{8,16},{16,24},{1,9},{9,17},{17,25},{2,10},{10,18},{18,26},{... | collective-permute-start | bytes 786440 | tf_op jit(solution)/shard_map/while/body/eval_jaxpr/ppermute | solution.py:30
  42.9 8.3 %collective-permute-start.5 = (bf16[32,4096]{1,0:T(8,128)(2,1)S(1)}, bf16[32,4096]{1,0:T(8,128)(2,1)S(1)}, u32[]{:S(2)}, u32[]{:S(2)}) collective-permute-start(bf16[32,4096]{1,0:T(8,128)(2,1)S(1)} %get-tuple-element.373), channel_id=1, source_target_pairs={{8,0},{16,8},{24,16},{9,1},{17,9},{25,17},{10,2},{18,10},{26,18},{... | collective-permute-start | bytes 786440 | tf_op jit(solution)/shard_map/while/body/eval_jaxpr/ppermute | solution.py:30
  53.0 14.2 %collective-permute-start = (bf16[32,512]{1,0:T(8,128)(2,1)S(1)}, bf16[32,512]{1,0:T(8,128)(2,1)S(1)}, u32[]{:S(2)}, u32[]{:S(2)}) collective-permute-start(bf16[32,512]{1,0:T(8,128)(2,1)S(1)} %get-tuple-element.364), channel_id=1, source_target_pairs={{1,0},{2,1},{3,2},{4,3},{5,4},{6,5},{7,6},{0,7},{9,8},{10,9},{11,1... | collective-permute-start | bytes 98312 | tf_op jit(solution)/shard_map/while/body/eval_jaxpr/ppermute | solution.py:20
  55.7 11.5 %collective-permute-start.1 = (bf16[32,512]{1,0:T(8,128)(2,1)S(1)}, bf16[32,512]{1,0:T(8,128)(2,1)S(1)}, u32[]{:S(2)}, u32[]{:S(2)}) collective-permute-start(bf16[32,512]{1,0:T(8,128)(2,1)S(1)} %get-tuple-element.365), channel_id=1, source_target_pairs={{0,1},{1,2},{2,3},{3,4},{4,5},{5,6},{6,7},{7,0},{8,9},{9,10},{10,1... | collective-permute-start | bytes 98312 | tf_op jit(solution)/shard_map/while/body/eval_jaxpr/ppermute | solution.py:18
  79.8 7.3 %collective-permute-start.4 = (bf16[32,4096]{1,0:T(8,128)(2,1)S(1)}, bf16[32,4096]{1,0:T(8,128)(2,1)S(1)}, u32[]{:S(2)}, u32[]{:S(2)}) collective-permute-start(bf16[32,4096]{1,0:T(8,128)(2,1)S(1)} %get-tuple-element.372), channel_id=1, source_target_pairs={{0,8},{8,16},{16,24},{1,9},{9,17},{17,25},{2,10},{10,18},{18,26},{... | collective-permute-start | bytes 786440 | tf_op jit(solution)/shard_map/while/body/eval_jaxpr/ppermute | solution.py:30
  83.3 8.3 %collective-permute-start.5 = (bf16[32,4096]{1,0:T(8,128)(2,1)S(1)}, bf16[32,4096]{1,0:T(8,128)(2,1)S(1)}, u32[]{:S(2)}, u32[]{:S(2)}) collective-permute-start(bf16[32,4096]{1,0:T(8,128)(2,1)S(1)} %get-tuple-element.373), channel_id=1, source_target_pairs={{8,0},{16,8},{24,16},{9,1},{17,9},{25,17},{10,2},{18,10},{26,18},{... | collective-permute-start | bytes 786440 | tf_op jit(solution)/shard_map/while/body/eval_jaxpr/ppermute | solution.py:30
  93.3 14.2 %collective-permute-start = (bf16[32,512]{1,0:T(8,128)(2,1)S(1)}, bf16[32,512]{1,0:T(8,128)(2,1)S(1)}, u32[]{:S(2)}, u32[]{:S(2)}) collective-permute-start(bf16[32,512]{1,0:T(8,128)(2,1)S(1)} %get-tuple-element.364), channel_id=1, source_target_pairs={{1,0},{2,1},{3,2},{4,3},{5,4},{6,5},{7,6},{0,7},{9,8},{10,9},{11,1... | collective-permute-start | bytes 98312 | tf_op jit(solution)/shard_map/while/body/eval_jaxpr/ppermute | solution.py:20
  96.0 11.5 %collective-permute-start.1 = (bf16[32,512]{1,0:T(8,128)(2,1)S(1)}, bf16[32,512]{1,0:T(8,128)(2,1)S(1)}, u32[]{:S(2)}, u32[]{:S(2)}) collective-permute-start(bf16[32,512]{1,0:T(8,128)(2,1)S(1)} %get-tuple-element.365), channel_id=1, source_target_pairs={{0,1},{1,2},{2,3},{3,4},{4,5},{5,6},{6,7},{7,0},{8,9},{9,10},{10,1... | collective-permute-start | bytes 98312 | tf_op jit(solution)/shard_map/while/body/eval_jaxpr/ppermute | solution.py:18
  120.1 7.3 %collective-permute-start.4 = (bf16[32,4096]{1,0:T(8,128)(2,1)S(1)}, bf16[32,4096]{1,0:T(8,128)(2,1)S(1)}, u32[]{:S(2)}, u32[]{:S(2)}) collective-permute-start(bf16[32,4096]{1,0:T(8,128)(2,1)S(1)} %get-tuple-element.372), channel_id=1, source_target_pairs={{0,8},{8,16},{16,24},{1,9},{9,17},{17,25},{2,10},{10,18},{18,26},{... | collective-permute-start | bytes 786440 | tf_op jit(solution)/shard_map/while/body/eval_jaxpr/ppermute | solution.py:30
  123.6 8.3 %collective-permute-start.5 = (bf16[32,4096]{1,0:T(8,128)(2,1)S(1)}, bf16[32,4096]{1,0:T(8,128)(2,1)S(1)}, u32[]{:S(2)}, u32[]{:S(2)}) collective-permute-start(bf16[32,4096]{1,0:T(8,128)(2,1)S(1)} %get-tuple-element.373), channel_id=1, source_target_pairs={{8,0},{16,8},{24,16},{9,1},{17,9},{25,17},{10,2},{18,10},{26,18},{... | collective-permute-start | bytes 786440 | tf_op jit(solution)/shard_map/while/body/eval_jaxpr/ppermute | solution.py:30
  133.6 14.2 %collective-permute-start = (bf16[32,512]{1,0:T(8,128)(2,1)S(1)}, bf16[32,512]{1,0:T(8,128)(2,1)S(1)}, u32[]{:S(2)}, u32[]{:S(2)}) collective-permute-start(bf16[32,512]{1,0:T(8,128)(2,1)S(1)} %get-tuple-element.364), channel_id=1, source_target_pairs={{1,0},{2,1},{3,2},{4,3},{5,4},{6,5},{7,6},{0,7},{9,8},{10,9},{11,1... | collective-permute-start | bytes 98312 | tf_op jit(solution)/shard_map/while/body/eval_jaxpr/ppermute | solution.py:20
  136.3 11.5 %collective-permute-start.1 = (bf16[32,512]{1,0:T(8,128)(2,1)S(1)}, bf16[32,512]{1,0:T(8,128)(2,1)S(1)}, u32[]{:S(2)}, u32[]{:S(2)}) collective-permute-start(bf16[32,512]{1,0:T(8,128)(2,1)S(1)} %get-tuple-element.365), channel_id=1, source_target_pairs={{0,1},{1,2},{2,3},{3,4},{4,5},{5,6},{6,7},{7,0},{8,9},{9,10},{10,1... | collective-permute-start | bytes 98312 | tf_op jit(solution)/shard_map/while/body/eval_jaxpr/ppermute | solution.py:18
  162.3 8.3 %collective-permute-start.5 = (bf16[32,4096]{1,0:T(8,128)(2,1)S(1)}, bf16[32,4096]{1,0:T(8,128)(2,1)S(1)}, u32[]{:S(2)}, u32[]{:S(2)}) collective-permute-start(bf16[32,4096]{1,0:T(8,128)(2,1)S(1)} %get-tuple-element.373), channel_id=1, source_target_pairs={{8,0},{16,8},{24,16},{9,1},{17,9},{25,17},{10,2},{18,10},{26,18},{... | collective-permute-start | bytes 786440 | tf_op jit(solution)/shard_map/while/body/eval_jaxpr/ppermute | solution.py:30
  172.4 14.2 %collective-permute-start = (bf16[32,512]{1,0:T(8,128)(2,1)S(1)}, bf16[32,512]{1,0:T(8,128)(2,1)S(1)}, u32[]{:S(2)}, u32[]{:S(2)}) collective-permute-start(bf16[32,512]{1,0:T(8,128)(2,1)S(1)} %get-tuple-element.364), channel_id=1, source_target_pairs={{1,0},{2,1},{3,2},{4,3},{5,4},{6,5},{7,6},{0,7},{9,8},{10,9},{11,1... | collective-permute-start | bytes 98312 | tf_op jit(solution)/shard_map/while/body/eval_jaxpr/ppermute | solution.py:20
  175.0 11.5 %collective-permute-start.1 = (bf16[32,512]{1,0:T(8,128)(2,1)S(1)}, bf16[32,512]{1,0:T(8,128)(2,1)S(1)}, u32[]{:S(2)}, u32[]{:S(2)}) collective-permute-start(bf16[32,512]{1,0:T(8,128)(2,1)S(1)} %get-tuple-element.365), channel_id=1, source_target_pairs={{0,1},{1,2},{2,3},{3,4},{4,5},{5,6},{6,7},{7,0},{8,9},{9,10},{10,1... | collective-permute-start | bytes 98312 | tf_op jit(solution)/shard_map/while/body/eval_jaxpr/ppermute | solution.py:18
  201.0 8.3 %collective-permute-start.5 = (bf16[32,4096]{1,0:T(8,128)(2,1)S(1)}, bf16[32,4096]{1,0:T(8,128)(2,1)S(1)}, u32[]{:S(2)}, u32[]{:S(2)}) collective-permute-start(bf16[32,4096]{1,0:T(8,128)(2,1)S(1)} %get-tuple-element.373), channel_id=1, source_target_pairs={{8,0},{16,8},{24,16},{9,1},{17,9},{25,17},{10,2},{18,10},{26,18},{... | collective-permute-start | bytes 786440 | tf_op jit(solution)/shard_map/while/body/eval_jaxpr/ppermute | solution.py:30
  211.1 14.2 %collective-permute-start = (bf16[32,512]{1,0:T(8,128)(2,1)S(1)}, bf16[32,512]{1,0:T(8,128)(2,1)S(1)}, u32[]{:S(2)}, u32[]{:S(2)}) collective-permute-start(bf16[32,512]{1,0:T(8,128)(2,1)S(1)} %get-tuple-element.364), channel_id=1, source_target_pairs={{1,0},{2,1},{3,2},{4,3},{5,4},{6,5},{7,6},{0,7},{9,8},{10,9},{11,1... | collective-permute-start | bytes 98312 | tf_op jit(solution)/shard_map/while/body/eval_jaxpr/ppermute | solution.py:20
  213.7 11.5 %collective-permute-start.1 = (bf16[32,512]{1,0:T(8,128)(2,1)S(1)}, bf16[32,512]{1,0:T(8,128)(2,1)S(1)}, u32[]{:S(2)}, u32[]{:S(2)}) collective-permute-start(bf16[32,512]{1,0:T(8,128)(2,1)S(1)} %get-tuple-element.365), channel_id=1, source_target_pairs={{0,1},{1,2},{2,3},{3,4},{4,5},{5,6},{6,7},{7,0},{8,9},{9,10},{10,1... | collective-permute-start | bytes 98312 | tf_op jit(solution)/shard_map/while/body/eval_jaxpr/ppermute | solution.py:18
  239.8 8.3 %collective-permute-start.5 = (bf16[32,4096]{1,0:T(8,128)(2,1)S(1)}, bf16[32,4096]{1,0:T(8,128)(2,1)S(1)}, u32[]{:S(2)}, u32[]{:S(2)}) collective-permute-start(bf16[32,4096]{1,0:T(8,128)(2,1)S(1)} %get-tuple-element.373), channel_id=1, source_target_pairs={{8,0},{16,8},{24,16},{9,1},{17,9},{25,17},{10,2},{18,10},{26,18},{... | collective-permute-start | bytes 786440 | tf_op jit(solution)/shard_map/while/body/eval_jaxpr/ppermute | solution.py:30
  249.8 14.2 %collective-permute-start = (bf16[32,512]{1,0:T(8,128)(2,1)S(1)}, bf16[32,512]{1,0:T(8,128)(2,1)S(1)}, u32[]{:S(2)}, u32[]{:S(2)}) collective-permute-start(bf16[32,512]{1,0:T(8,128)(2,1)S(1)} %get-tuple-element.364), channel_id=1, source_target_pairs={{1,0},{2,1},{3,2},{4,3},{5,4},{6,5},{7,6},{0,7},{9,8},{10,9},{11,1... | collective-permute-start | bytes 98312 | tf_op jit(solution)/shard_map/while/body/eval_jaxpr/ppermute | solution.py:20
  252.4 11.5 %collective-permute-start.1 = (bf16[32,512]{1,0:T(8,128)(2,1)S(1)}, bf16[32,512]{1,0:T(8,128)(2,1)S(1)}, u32[]{:S(2)}, u32[]{:S(2)}) collective-permute-start(bf16[32,512]{1,0:T(8,128)(2,1)S(1)} %get-tuple-element.365), channel_id=1, source_target_pairs={{0,1},{1,2},{2,3},{3,4},{4,5},{5,6},{6,7},{7,0},{8,9},{9,10},{10,1... | collective-permute-start | bytes 98312 | tf_op jit(solution)/shard_map/while/body/eval_jaxpr/ppermute | solution.py:18
  278.5 8.3 %collective-permute-start.5 = (bf16[32,4096]{1,0:T(8,128)(2,1)S(1)}, bf16[32,4096]{1,0:T(8,128)(2,1)S(1)}, u32[]{:S(2)}, u32[]{:S(2)}) collective-permute-start(bf16[32,4096]{1,0:T(8,128)(2,1)S(1)} %get-tuple-element.373), channel_id=1, source_target_pairs={{8,0},{16,8},{24,16},{9,1},{17,9},{25,17},{10,2},{18,10},{26,18},{... | collective-permute-start | bytes 786440 | tf_op jit(solution)/shard_map/while/body/eval_jaxpr/ppermute | solution.py:30
  (18 other events, 90.3 us)
where the time goes:
time: 288 us; the launch traced here: 287 us
  matrix products  93.6 us (32%)
  starting transfers between devices  59.8 us (21%)
  waiting for transfers between devices  55.6 us (19%)
  other arithmetic  45.7 us (16%)
  local copies, waits for them, and re-layouts  30.2 us (10%)
    dot_general x14, matrix products, product(): jnp.einsum('mnb,nab->mna', picked, blocks, preferred_element_type=jnp.flo...  93.6 us
    ppermute x14, waiting for transfers between devices, passed_along(): return lax.ppermute(block, axis, route)  48.7 us
    ppermute x14, starting transfers between devices, padded(): lax.ppermute(head, axis, [((i + 1) % count, i) for i in range(count)])  32.6 us
    gather x14, local copies, waits for them, and re-layouts, product(): picked = jnp.take(tiles, local_cols, axis=1)  27.9 us
    ppermute x14, starting transfers between devices, passed_along(): return lax.ppermute(block, axis, route)  27.1 us
    dynamic_update_slice x7, other arithmetic, finish(): lax.dynamic_update_slice_in_dim(stored, jnp.where(active, result, current...  18.5 us
    reduce_sum x14, other arithmetic, product(): prod.reshape(rows, per_dev, kcount, bsize).sum(axis=2).reshape(rows, width)  16.7 us
    ppermute x14, waiting for transfers between devices, padded(): lax.ppermute(tail, axis, [(i, (i + 1) % count) for i in range(count)])  6.83 us
  transfers between devices with their start and end apart: 42, of which 21 were waited for; matrix products, arithmetic and copies ran while one was open for 26% of the time, Pallas kernels for 0%

commit v1 on v0

v1 whole, which is shorter than its diff:
```python
import functools

import jax
import jax.numpy as jnp
from jax import lax
from jax.experimental import pallas as pl
from jax.experimental.pallas import tpu as pltpu
from jax.sharding import PartitionSpec as P

HB = 4
CHUNKS = 2
VMEM = pl.BlockSpec(memory_space=pltpu.VMEM)
SMEM = pl.BlockSpec(memory_space=pltpu.SMEM)
ANY = pl.BlockSpec(memory_space=pl.ANY)
HBM = pl.BlockSpec(memory_space=pltpu.HBM)


def params(mib):
    return pltpu.CompilerParams(vmem_limit_bytes=mib << 20)


def source_kernel(row0, halo, thick_ref, layers_ref, total_ref, *rest):
    *outs, buf, sems = rest
    depth, rows, width = buf.shape
    thick = thick_ref[0]

    def copy(k):
        return pltpu.make_async_copy(
            layers_ref.at[k, pl.ds(row0, rows), :], buf.at[k], sems.at[k]
        )

    for k in range(depth):
        pl.when(k < thick)(copy(k).start)
    total_ref[...] = jnp.zeros_like(total_ref)
    for k in range(depth):

        @pl.when(k < thick)
        def _():
            copy(k).wait()
            total_ref[...] += buf[k].astype(jnp.float32)

    put(outs, total_ref[...].astype(jnp.bfloat16), 0, halo)


def put(outs, value, start, halo):
    if len(outs) == 1:
        outs[0][:, start : start + value.shape[1]] = value
        return
    edges, mid = outs
    width = edges.shape[1] + mid.shape[1]
    stop = start + value.shape[1]
    for lo, hi, ref, shift in (
        (0, halo, edges, 0),
        (halo, width - halo, mid, -halo),
        (width - halo, width, edges, 2 * halo - width),
    ):
        a, b = max(lo, start), min(hi, stop)
        if a < b:
            ref[:, a + shift : b + shift] = value[:, a - start : b - start]


def product_kernel(halo, parts, mode_ref, cols_ref, left_ref, right_ref, *rest):
    ins, (down_ref, up_ref, total_ref), outs, ext = (
        rest[:parts],
        rest[parts : parts + 3],
        rest[parts + 3 : -1],
        rest[-1],
    )
    width = total_ref.shape[1]
    bsize = down_ref.shape[-1]
    per_dev = width // bsize
    kcount = down_ref.shape[1] // per_dev

    def apply(green_ref):
        ext[:, :halo] = left_ref[...]
        ext[:, halo + width :] = right_ref[...]
        if parts == 1:
            ext[:, halo : halo + width] = ins[0][...]
        else:
            ext[:, halo : 2 * halo] = ins[0][:, :halo]
            ext[:, 2 * halo : width] = ins[1][...]
            ext[:, width : width + halo] = ins[0][:, halo:]
        for i in range(per_dev):
            picked, blocks = [], []
            for k in range(kcount):
                at = pl.multiple_of(cols_ref[0, i * kcount + k] * bsize, bsize)
                picked.append(ext[:, pl.ds(at, bsize)])
                blocks.append(green_ref[0, i * kcount + k])
            value = lax.dot_general(
                jnp.concatenate(picked, 1),
                jnp.concatenate(blocks, 1),
                (((1,), (1,)), ((), ())),
                preferred_element_type=jnp.float32,
            )
            value = value + total_ref[:, i * bsize : (i + 1) * bsize]
            put(outs, value.astype(jnp.bfloat16), i * bsize, halo)

    pl.when(mode_ref[0] == 1)(lambda: apply(down_ref))
    pl.when(mode_ref[0] == 2)(lambda: apply(up_ref))


def store_kernel(halo, hops, chunks, parts, slab_ref, *rest):
    ins, (down_ref, up_ref), sems = rest[:-3], rest[-3:-1], rest[-1]
    rows = ins[0].shape[0]
    width = down_ref.shape[2]

    def copies(h, out_ref, which):
        made = []
        for j in range(chunks):
            at = (h * chunks + j) * parts
            span = pl.ds(j * rows, rows)
            if parts == 1:
                pieces = [(ins[at], 0, width, 0)]
            else:
                pieces = [
                    (ins[at], 0, halo, 0),
                    (ins[at + 1], 0, width - 2 * halo, halo),
                    (ins[at], halo, halo, width - halo),
                ]
            for src, a, size, b in pieces:
                made.append(
                    pltpu.make_async_copy(
                        src.at[:, pl.ds(a, size)],
                        out_ref.at[0, span, pl.ds(b, size)],
                        sems.at[which, len(made)],
                    )
                )
        return made

    plan = []
    for h in range(hops):
        plan.append((h, down_ref, 0, slab_ref[0] == h))
        plan.append((h, up_ref, 1, slab_ref[0] == hops - 1 - h))
    for h, ref, which, chosen in plan:

        @pl.when(chosen)
        def _():
            for copy in copies(h, ref, which):
                copy.start()

    for h, ref, which, chosen in plan:

        @pl.when(chosen)
        def _():
            for copy in copies(h, ref, which):
                copy.wait()


def shards(thickness, layer_sources, green_down, column_down, green_up, column_up):
    slabs = lax.axis_size("slab")
    cross = lax.axis_size("cross")
    slab_id = lax.axis_index("slab")
    lateral = lax.axis_index("cross")
    depth, sources, width = layer_sources.shape
    bsize = green_down.shape[-1]
    per_dev = width // bsize
    total_blocks = per_dev * cross
    nblocks = green_down.shape[1]
    halo = HB * bsize
    rows = sources // CHUNKS
    split = per_dev > 2 * HB
    parts = 2 if split else 1
    low = slab_id < slabs // 2
    bf16 = lambda cols: jax.ShapeDtypeStruct((rows, cols), jnp.bfloat16)
    pieces = [bf16(2 * halo), bf16(width - 2 * halo)] if split else [bf16(width)]

    def local(first):
        cols = jnp.where(first, column_down, column_up)
        return (cols - lateral * per_dev + HB) % total_blocks

    def source(j):
        total, *out = pl.pallas_call(
            functools.partial(source_kernel, j * rows, halo),
            out_shape=[jax.ShapeDtypeStruct((rows, width), jnp.float32), *pieces],
            in_specs=[SMEM, HBM],
            out_specs=[VMEM] * (1 + parts),
            scratch_shapes=[
                pltpu.VMEM((depth, rows, width), jnp.bfloat16),
                pltpu.SemaphoreType.DMA((depth,)),
            ],
            compiler_params=params(16),
            name="source",
        )(thickness, layer_sources)
        return total, out

    def product(h, cols, left, right, got, total):
        mode = jnp.where(slab_id == h, 1, jnp.where(slab_id == slabs - 1 - h, 2, 0))
        return pl.pallas_call(
            functools.partial(product_kernel, halo, parts),
            out_shape=pieces,
            in_specs=[SMEM, SMEM] + [VMEM] * (5 + parts),
            out_specs=[VMEM] * parts,
            scratch_shapes=[pltpu.VMEM((rows, width + 2 * halo), jnp.bfloat16)],
            compiler_params=params(24),
            cost_estimate=pl.CostEstimate(
                flops=2 * rows * nblocks * bsize * bsize,
                bytes_accessed=nblocks * bsize * bsize * 2,
                transcendentals=0,
            ),
            name="product",
        )(mode.reshape(1), cols, left, right, *got, green_down, green_up, total)

    def hop(x, h):
        route = []
        for a, b in ((h - 1, h), (slabs - h, slabs - 1 - h)):
            route += [(a * cross + c, b * cross + c) for c in range(cross)]
        return lax.ppermute(x, ("slab", "cross"), route)

    def sideways(x, step):
        return lax.ppermute(x, "cross", [(c, (c + step) % cross) for c in range(cross)])

    totals, made = [], {}
    for j in range(CHUNKS):
        total, out = source(j)
        totals.append(total)
        made[0, j] = out
    cols = [local(low), local(jnp.logical_not(low))]
    order = sorted(
        ((h, j) for h in range(1, slabs) for j in range(CHUNKS)),
        key=lambda hj: (hj[0] + hj[1], hj[0]),
    )
    for h, j in order:
        got = [hop(x, h) for x in made[h - 1, j]]
        right = sideways(got[0][:, :halo], -1)
        left = sideways(got[0][:, got[0].shape[1] - halo :], 1)
        late = 0 if h < slabs // 2 else 1
        made[h, j] = product(h, cols[late], left, right, got, totals[j])

    flat = [x for h in range(slabs) for j in range(CHUNKS) for x in made[h, j]]
    return pl.pallas_call(
        functools.partial(store_kernel, halo, slabs, CHUNKS, parts),
        out_shape=[jax.ShapeDtypeStruct((1, sources, width), jnp.bfloat16)] * 2,
        in_specs=[SMEM] + [VMEM] * len(flat),
        out_specs=[ANY, ANY],
        scratch_shapes=[pltpu.SemaphoreType.DMA((2, CHUNKS * (3 if split else 1)))],
        compiler_params=params(16),
        name="store",
    )(slab_id.astype(jnp.int32).reshape(1), *flat)


def solution(mesh):
    return jax.shard_map(
        shards,
        mesh=mesh,
        in_specs=(
            P("slab"),
            P("slab", None, "cross"),
            P("slab", "cross", None, None),
            P("slab", "cross"),
            P("slab", "cross", None, None),
            P("slab", "cross"),
        ),
        out_specs=(P("slab", None, "cross"), P("slab", None, "cross")),
        check_vma=False,
    )
```

time: 288 us -> 103 us (0.36)
  matrix products: 93.6 us -> 0 us
  other arithmetic: 45.7 us -> 0.02 us
  starting transfers between devices: 59.8 us -> 25.6 us
  waiting for transfers between devices: 55.6 us -> 32.2 us
  Pallas kernels: 0 us -> 19.3 us
  local copies, waits for them, and re-layouts: 30.2 us -> 23.4 us
    dot_general x14 -> x0, matrix products: 93.6 us -> none  [product(): jnp.einsum('mnb,nab->mna', picked, blocks, preferred_element_type=jnp.flo...]
    ppermute x42 -> x24, starting transfers between devices: 59.8 us -> 25.6 us  [the longest x12 19 us: hop(): return lax.ppermute(x, ('slab', 'cross'), route)]
    gather x14 -> x0, local copies, waits for them, and re-layouts: 27.9 us -> none  [product(): picked = jnp.take(tiles, local_cols, axis=1)]
    ppermute x42 -> x24, waiting for transfers between devices: 55.6 us -> 32.2 us  [the longest x12 18 us: hop(): return lax.ppermute(x, ('slab', 'cross'), route)]
    reduce_sum x15 -> x0, other arithmetic: 21.4 us -> none  [the longest x14 16.7 us: product(): prod.reshape(rows, per_dev, kcount, bsize).sum(axis=2).reshape(rows, width)]
    unnamed x0 -> x38, local copies, waits for them, and re-layouts: none -> 21.4 us
    pallas_call x0 -> x9, Pallas kernels: none -> 19.3 us  [the longest x6 13.3 us: product(): pl.pallas_call(functools.partial(product_kernel, halo, parts), out_shape=...]
    dynamic_update_slice x7 -> x0, other arithmetic: 18.5 us -> none  [finish(): lax.dynamic_update_slice_in_dim(stored, jnp.where(active, result, current...]
  transfers between devices with their start and end apart: 42 -> 24, of which waited for: 21 -> 10; matrix products, arithmetic and copies ran while one was open for 26% -> 2% of each run, Pallas kernels for 0% -> 11%
where the time goes in v1:
time: 103 us; the launch traced here: 102 us
  waiting for transfers between devices  32.2 us (31%)
  starting transfers between devices  25.6 us (25%)
  local copies, waits for them, and re-layouts  23.4 us (23%)
  Pallas kernels  19.3 us (19%)
  between operations  1.77 us (2%)
    unnamed x38, local copies, waits for them, and re-layouts  21.4 us
    ppermute x12, starting transfers between devices, hop(): return lax.ppermute(x, ('slab', 'cross'), route)  19 us
    ppermute x12, waiting for transfers between devices, hop(): return lax.ppermute(x, ('slab', 'cross'), route)  18 us
    ppermute x12, waiting for transfers between devices, sideways(): lax.ppermute(x, 'cross', [(c, (c + step) % cross) for c in range(cross)])  14.2 us
    pallas_call x6, Pallas kernels, product(): pl.pallas_call(functools.partial(product_kernel, halo, parts), out_shape=...  13.3 us
    ppermute x12, starting transfers between devices, sideways(): lax.ppermute(x, 'cross', [(c, (c + step) % cross) for c in range(cross)])  6.65 us
    pallas_call x1, Pallas kernels, shards(): pl.pallas_call(functools.partial(store_kernel, halo, slabs, CHUNKS, parts...  3.12 us
    pallas_call x2, Pallas kernels, source(): pl.pallas_call(functools.partial(source_kernel, j * rows, halo), out_shap...  2.88 us
  transfers between devices with their start and end apart: 24, of which 10 were waited for; matrix products, arithmetic and copies ran while one was open for 2% of the time, Pallas kernels for 11%

profile of v1, /device:TPU:0, one launch (start us, length us, event | category | flops | bytes accessed | tf_op | source)
XLA Modules:
  0.0 102.2 jit_solution(18259864818356843244)
XLA Ops:
  1.3 2.2 %copy-done.6 = bf16[4,128,4096]{2,1,0:T(8,128)(2,1)S(1)} copy-done((bf16[4,128,4096]{2,1,0:T(8,128)(2,1)S(1)}, bf16[4,128,4096]{2,1,0:T(8,128)(2,1)}, u32[]{:S(2)}) %copy-start.6) | copy-done | bytes 4194328
  4.9 4.9 %collective-permute-start.4 = (bf16[64,1024]{1,0:T(8,128)(2,1)S(1)}, bf16[64,1024]{1,0:T(8,128)(2,1)S(1)}, u32[]{:S(2)}, u32[]{:S(2)}) collective-permute-start(bf16[64,1024]{1,0:T(8,128)(2,1)S(1)} %get-tuple-element.22.rest_2_), channel_id=1, source_target_pairs={{0,8},{1,9},{2,10},{3,11},{4,12},{5,13},{6,14},{7,15},{24,16},{25,... | collective-permute-start | bytes 393224 | tf_op jit(solution)/shard_map/ppermute | solution.py:207
  9.9 2.0 %collective-permute-start.7 = (bf16[64,3072]{1,0:T(8,128)(2,1)}, bf16[64,3072]{1,0:T(8,128)(2,1)}, u32[]{:S(2)}, u32[]{:S(2)}) collective-permute-start(bf16[64,3072]{1,0:T(8,128)(2,1)} %get-tuple-element.23.rest_3_), channel_id=1, source_target_pairs={{0,8},{1,9},{2,10},{3,11},{4,12},{5,13},{6,14},{7,15},{24,16},{25,... | collective-permute-start | bytes 1179656 | tf_op jit(solution)/shard_map/ppermute | solution.py:207
  14.7 2.0 %collective-permute-start.3 = (bf16[64,3072]{1,0:T(8,128)(2,1)}, bf16[64,3072]{1,0:T(8,128)(2,1)}, u32[]{:S(2)}, u32[]{:S(2)}) collective-permute-start(bf16[64,3072]{1,0:T(8,128)(2,1)} %get-tuple-element.21.rest_1_), channel_id=1, source_target_pairs={{0,8},{1,9},{2,10},{3,11},{4,12},{5,13},{6,14},{7,15},{24,16},{25,... | collective-permute-start | bytes 1179656 | tf_op jit(solution)/shard_map/ppermute | solution.py:207
  19.1 2.2 %collective-permute-done.6.right_ref = bf16[64,512]{1,0:T(8,128)(2,1)} collective-permute-done((bf16[64,512]{1,0:T(8,128)(2,1)}, bf16[64,512]{1,0:T(8,128)(2,1)}, u32[]{:S(2)}, u32[]{:S(2)}) %collective-permute-start.6) | collective-permute-done | bytes 65568 | tf_op jit(solution)/shard_map/ppermute | solution.py:210
  21.2 2.7 %collective-permute-done.5.left_ref = bf16[64,512]{1,0:T(8,128)(2,1)} collective-permute-done((bf16[64,512]{1,0:T(8,128)(2,1)}, bf16[64,512]{1,0:T(8,128)(2,1)}, u32[]{:S(2)}, u32[]{:S(2)}) %collective-permute-start.5) | collective-permute-done | bytes 65568 | tf_op jit(solution)/shard_map/ppermute | solution.py:210
  23.9 2.8 %copy-done = bf16[1,192,128,128]{3,2,1,0:T(8,128)(2,1)S(1)} copy-done((bf16[1,192,128,128]{3,2,1,0:T(8,128)(2,1)S(1)}, bf16[1,192,128,128]{3,2,1,0:T(8,128)(2,1)}, u32[]{:S(2)}) %copy-start) | copy-done | bytes 6291480
  26.7 2.8 %copy-done.3 = bf16[1,192,128,128]{3,2,1,0:T(8,128)(2,1)S(1)} copy-done((bf16[1,192,128,128]{3,2,1,0:T(8,128)(2,1)S(1)}, bf16[1,192,128,128]{3,2,1,0:T(8,128)(2,1)}, u32[]{:S(2)}) %copy-start.3) | copy-done | bytes 6291480
  30.7 2.0 %product.7 = (bf16[64,1024]{1,0:T(8,128)(2,1)S(1)}, bf16[64,3072]{1,0:T(8,128)(2,1)}) custom-call(s32[1]{0:T(128)} %bitcast.1.mode_ref, s32[1,192]{1,0:T(1,128)S(1)} %get-tuple-element.51.cols_ref, bf16[64,512]{1,0:T(8,128)(2,1)} %collective-permute-done.5.left_ref, bf16[64,512]{1,0:T(8,128)(2,1)} %collective-permute-done.6.right_ref, ...), custom_call_target="tpu_custom_call" | custom-call | flops 402653184 | bytes 6291456 | tf_op jit(solution)/shard_map/product/pallas_call | solution.py:188
  35.7 2.3 %collective-permute-done.1.left_ref = bf16[64,512]{1,0:T(8,128)(2,1)S(1)} collective-permute-done((bf16[64,512]{1,0:T(8,128)(2,1)S(1)}, bf16[64,512]{1,0:T(8,128)(2,1)S(1)}, u32[]{:S(2)}, u32[]{:S(2)}) %collective-permute-start.1) | collective-permute-done | bytes 65568 | tf_op jit(solution)/shard_map/ppermute | solution.py:210
  38.1 1.8 %product.6 = (bf16[64,1024]{1,0:T(8,128)(2,1)}, bf16[64,3072]{1,0:T(8,128)(2,1)}) custom-call(s32[1]{0:T(128)} %bitcast.1.mode_ref, s32[1,192]{1,0:T(1,128)S(1)} %get-tuple-element.51.cols_ref, bf16[64,512]{1,0:T(8,128)(2,1)S(1)} %collective-permute-done.1.left_ref, bf16[64,512]{1,0:T(8,128)(2,1)S(1)} %collective-permute-done.2.right_ref, ...), custom_call_target="tpu_custom_call" | custom-call | flops 402653184 | bytes 6291456 | tf_op jit(solution)/shard_map/product/pallas_call | solution.py:188
  43.1 2.7 %collective-permute-done.13.left_ref = bf16[64,512]{1,0:T(8,128)(2,1)S(1)} collective-permute-done((bf16[64,512]{1,0:T(8,128)(2,1)S(1)}, bf16[64,512]{1,0:T(8,128)(2,1)S(1)}, u32[]{:S(2)}, u32[]{:S(2)}) %collective-permute-start.13) | collective-permute-done | bytes 65568 | tf_op jit(solution)/shard_map/ppermute | solution.py:210
  45.8 2.8 %copy-done.1 = bf16[1,192,128,128]{3,2,1,0:T(8,128)(2,1)S(1)} copy-done((bf16[1,192,128,128]{3,2,1,0:T(8,128)(2,1)S(1)}, bf16[1,192,128,128]{3,2,1,0:T(8,128)(2,1)}, u32[]{:S(2)}) %copy-start.1) | copy-done | bytes 6291480
  48.5 2.8 %copy-done.4 = bf16[1,192,128,128]{3,2,1,0:T(8,128)(2,1)S(1)} copy-done((bf16[1,192,128,128]{3,2,1,0:T(8,128)(2,1)S(1)}, bf16[1,192,128,128]{3,2,1,0:T(8,128)(2,1)}, u32[]{:S(2)}) %copy-start.4) | copy-done | bytes 6291480
  52.5 1.9 %product.9 = (bf16[64,1024]{1,0:T(8,128)(2,1)S(1)}, bf16[64,3072]{1,0:T(8,128)(2,1)}) custom-call(s32[1]{0:T(128)} %bitcast.2.mode_ref, s32[1,192]{1,0:T(1,128)S(1)} %get-tuple-element.50.cols_ref, bf16[64,512]{1,0:T(8,128)(2,1)S(1)} %collective-permute-done.13.left_ref, bf16[64,512]{1,0:T(8,128)(2,1)S(1)} %collective-permute-done.14.right_ref, ...), custom_call_target="tpu_custom_call" | custom-call | flops 402653184 | bytes 6291456 | tf_op jit(solution)/shard_map/product/pallas_call | solution.py:188
  58.2 2.3 %collective-permute-done.9.left_ref = bf16[64,512]{1,0:T(8,128)(2,1)S(1)} collective-permute-done((bf16[64,512]{1,0:T(8,128)(2,1)S(1)}, bf16[64,512]{1,0:T(8,128)(2,1)S(1)}, u32[]{:S(2)}, u32[]{:S(2)}) %collective-permute-start.9) | collective-permute-done | bytes 65568 | tf_op jit(solution)/shard_map/ppermute | solution.py:210
  64.4 7.3 %collective-permute-done.20.rest_0_ = bf16[64,1024]{1,0:T(8,128)(2,1)S(1)} collective-permute-done((bf16[64,1024]{1,0:T(8,128)(2,1)S(1)}, bf16[64,1024]{1,0:T(8,128)(2,1)S(1)}, u32[]{:S(2)}, u32[]{:S(2)}) %collective-permute-start.20) | collective-permute-done | bytes 131104 | tf_op jit(solution)/shard_map/ppermute | solution.py:207
  73.6 10.7 %collective-permute-done.16.rest_0_ = bf16[64,1024]{1,0:T(8,128)(2,1)S(1)} collective-permute-done((bf16[64,1024]{1,0:T(8,128)(2,1)S(1)}, bf16[64,1024]{1,0:T(8,128)(2,1)S(1)}, u32[]{:S(2)}, u32[]{:S(2)}) %collective-permute-start.16) | collective-permute-done | bytes 131104 | tf_op jit(solution)/shard_map/ppermute | solution.py:207
  84.9 2.1 %collective-permute-start.18 = (bf16[64,512]{1,0:T(8,128)(2,1)}, bf16[64,512]{1,0:T(8,128)(2,1)}, u32[]{:S(2)}, u32[]{:S(2)}) collective-permute-start(bf16[64,512]{1,0:T(8,128)(2,1)} %get-tuple-element.40), channel_id=1, source_target_pairs={{0,7},{1,0},{2,1},{3,2},{4,3},{5,4},{6,5},{7,6},{8,15},{9,8},{10,9... | collective-permute-start | bytes 196616 | tf_op jit(solution)/shard_map/ppermute | solution.py:210
  87.1 2.8 %copy-done.2 = bf16[1,192,128,128]{3,2,1,0:T(8,128)(2,1)S(1)} copy-done((bf16[1,192,128,128]{3,2,1,0:T(8,128)(2,1)S(1)}, bf16[1,192,128,128]{3,2,1,0:T(8,128)(2,1)}, u32[]{:S(2)}) %copy-start.2) | copy-done | bytes 6291480
  89.9 2.8 %copy-done.5 = bf16[1,192,128,128]{3,2,1,0:T(8,128)(2,1)S(1)} copy-done((bf16[1,192,128,128]{3,2,1,0:T(8,128)(2,1)S(1)}, bf16[1,192,128,128]{3,2,1,0:T(8,128)(2,1)}, u32[]{:S(2)}) %copy-start.5) | copy-done | bytes 6291480
  92.6 2.9 %product.11 = (bf16[64,1024]{1,0:T(8,128)(2,1)S(1)}, bf16[64,3072]{1,0:T(8,128)(2,1)S(1)}) custom-call(s32[1]{0:T(128)} %bitcast.3.mode_ref, s32[1,192]{1,0:T(1,128)S(1)} %get-tuple-element.50.cols_ref, bf16[64,512]{1,0:T(8,128)(2,1)S(1)} %collective-permute-done.21.left_ref, bf16[64,512]{1,0:T(8,128)(2,1)S(1)} %collective-permute-done.22.right_ref, ...), custom_call_target="tpu_custom_call" | custom-call | flops 402653184 | bytes 6291456 | tf_op jit(solution)/shard_map/product/pallas_call | solution.py:188
  95.6 3.3 %product.10 = (bf16[64,1024]{1,0:T(8,128)(2,1)S(1)}, bf16[64,3072]{1,0:T(8,128)(2,1)S(1)}) custom-call(s32[1]{0:T(128)} %bitcast.3.mode_ref, s32[1,192]{1,0:T(1,128)S(1)} %get-tuple-element.50.cols_ref, bf16[64,512]{1,0:T(8,128)(2,1)} %collective-permute-done.17.left_ref, bf16[64,512]{1,0:T(8,128)(2,1)} %collective-permute-done.18.right_ref, ...), custom_call_target="tpu_custom_call" | custom-call | flops 402653184 | bytes 6291456 | tf_op jit(solution)/shard_map/product/pallas_call | solution.py:188
  99.0 3.1 %store.1 = (bf16[1,128,4096]{2,1,0:T(8,128)(2,1)}, bf16[1,128,4096]{2,1,0:T(8,128)(2,1)}) custom-call(s32[1]{0:T(128)} %bitcast.slab_ref, bf16[64,1024]{1,0:T(8,128)(2,1)} %get-tuple-element.20.rest_0_, bf16[64,3072]{1,0:T(8,128)(2,1)} %get-tuple-element.21.rest_1_, bf16[64,1024]{1,0:T(8,128)(2,1)S(1)} %get-tuple-element.22.rest_2_, ...), custom_call_target="tpu_custom_call" | custom-call | tf_op jit(solution)/shard_map/store/pallas_call | solution.py:230
  (79 shorter events, 25.2 us)
Async XLA Ops:
  4.9 11.8 %collective-permute-start.4 = (bf16[64,1024]{1,0:T(8,128)(2,1)S(1)}, bf16[64,1024]{1,0:T(8,128)(2,1)S(1)}, u32[]{:S(2)}, u32[]{:S(2)}) collective-permute-start(bf16[64,1024]{1,0:T(8,128)(2,1)S(1)} %get-tuple-element.22.rest_2_), channel_id=1, source_target_pairs={{0,8},{1,9},{2,10},{3,11},{4,12},{5,13},{6,14},{7,15},{24,16},{25,... | collective-permute-start | bytes 393224 | tf_op jit(solution)/shard_map/ppermute | solution.py:207
  9.9 14.1 %collective-permute-start.7 = (bf16[64,3072]{1,0:T(8,128)(2,1)}, bf16[64,3072]{1,0:T(8,128)(2,1)}, u32[]{:S(2)}, u32[]{:S(2)}) collective-permute-start(bf16[64,3072]{1,0:T(8,128)(2,1)} %get-tuple-element.23.rest_3_), channel_id=1, source_target_pairs={{0,8},{1,9},{2,10},{3,11},{4,12},{5,13},{6,14},{7,15},{24,16},{25,... | collective-permute-start | bytes 1179656 | tf_op jit(solution)/shard_map/ppermute | solution.py:207
  13.4 20.0 %collective-permute-start = (bf16[64,1024]{1,0:T(8,128)(2,1)}, bf16[64,1024]{1,0:T(8,128)(2,1)S(1)}, u32[]{:S(2)}, u32[]{:S(2)}) collective-permute-start(bf16[64,1024]{1,0:T(8,128)(2,1)} %get-tuple-element.20.rest_0_), channel_id=1, source_target_pairs={{0,8},{1,9},{2,10},{3,11},{4,12},{5,13},{6,14},{7,15},{24,16},{25,... | collective-permute-start | bytes 393224 | tf_op jit(solution)/shard_map/ppermute | solution.py:207
  14.7 23.4 %collective-permute-start.3 = (bf16[64,3072]{1,0:T(8,128)(2,1)}, bf16[64,3072]{1,0:T(8,128)(2,1)}, u32[]{:S(2)}, u32[]{:S(2)}) collective-permute-start(bf16[64,3072]{1,0:T(8,128)(2,1)} %get-tuple-element.21.rest_1_), channel_id=1, source_target_pairs={{0,8},{1,9},{2,10},{3,11},{4,12},{5,13},{6,14},{7,15},{24,16},{25,... | collective-permute-start | bytes 1179656 | tf_op jit(solution)/shard_map/ppermute | solution.py:207
  17.4 3.8 %collective-permute-start.6 = (bf16[64,512]{1,0:T(8,128)(2,1)}, bf16[64,512]{1,0:T(8,128)(2,1)}, u32[]{:S(2)}, u32[]{:S(2)}) collective-permute-start(bf16[64,512]{1,0:T(8,128)(2,1)} %get-tuple-element.46), channel_id=1, source_target_pairs={{0,7},{1,0},{2,1},{3,2},{4,3},{5,4},{6,5},{7,6},{8,15},{9,8},{10,9... | collective-permute-start | bytes 196616 | tf_op jit(solution)/shard_map/ppermute | solution.py:210
  19.0 4.9 %collective-permute-start.5 = (bf16[64,512]{1,0:T(8,128)(2,1)}, bf16[64,512]{1,0:T(8,128)(2,1)}, u32[]{:S(2)}, u32[]{:S(2)}) collective-permute-start(bf16[64,512]{1,0:T(8,128)(2,1)} %get-tuple-element.47), channel_id=1, source_target_pairs={{0,1},{1,2},{2,3},{3,4},{4,5},{5,6},{6,7},{7,0},{8,9},{9,10},{10,1... | collective-permute-start | bytes 196616 | tf_op jit(solution)/shard_map/ppermute | solution.py:210
  32.7 7.9 %collective-permute-start.12 = (bf16[64,1024]{1,0:T(8,128)(2,1)S(1)}, bf16[64,1024]{1,0:T(8,128)(2,1)S(1)}, u32[]{:S(2)}, u32[]{:S(2)}) collective-permute-start(bf16[64,1024]{1,0:T(8,128)(2,1)S(1)} %get-tuple-element.28.rest_6_), channel_id=1, source_target_pairs={{8,16},{9,17},{10,18},{11,19},{12,20},{13,21},{14,22},{15,23},{16,... | collective-permute-start | bytes 393224 | tf_op jit(solution)/shard_map/ppermute | solution.py:207
  33.4 2.4 %collective-permute-start.2 = (bf16[64,512]{1,0:T(8,128)(2,1)S(1)}, bf16[64,512]{1,0:T(8,128)(2,1)S(1)}, u32[]{:S(2)}, u32[]{:S(2)}) collective-permute-start(bf16[64,512]{1,0:T(8,128)(2,1)S(1)} %get-tuple-element.48), channel_id=1, source_target_pairs={{0,7},{1,0},{2,1},{3,2},{4,3},{5,4},{6,5},{7,6},{8,15},{9,8},{10,9... | collective-permute-start | bytes 196616 | tf_op jit(solution)/shard_map/ppermute | solution.py:210
  33.5 4.6 %collective-permute-start.1 = (bf16[64,512]{1,0:T(8,128)(2,1)S(1)}, bf16[64,512]{1,0:T(8,128)(2,1)S(1)}, u32[]{:S(2)}, u32[]{:S(2)}) collective-permute-start(bf16[64,512]{1,0:T(8,128)(2,1)S(1)} %get-tuple-element.49), channel_id=1, source_target_pairs={{0,1},{1,2},{2,3},{3,4},{4,5},{5,6},{6,7},{7,0},{8,9},{9,10},{10,1... | collective-permute-start | bytes 196616 | tf_op jit(solution)/shard_map/ppermute | solution.py:210
  33.9 11.8 %collective-permute-start.15 = (bf16[64,3072]{1,0:T(8,128)(2,1)}, bf16[64,3072]{1,0:T(8,128)(2,1)}, u32[]{:S(2)}, u32[]{:S(2)}) collective-permute-start(bf16[64,3072]{1,0:T(8,128)(2,1)} %get-tuple-element.29.rest_7_), channel_id=1, source_target_pairs={{8,16},{9,17},{10,18},{11,19},{12,20},{13,21},{14,22},{15,23},{16,... | collective-permute-start | bytes 1179656 | tf_op jit(solution)/shard_map/ppermute | solution.py:207
  39.9 15.8 %collective-permute-start.8 = (bf16[64,1024]{1,0:T(8,128)(2,1)}, bf16[64,1024]{1,0:T(8,128)(2,1)S(1)}, u32[]{:S(2)}, u32[]{:S(2)}) collective-permute-start(bf16[64,1024]{1,0:T(8,128)(2,1)} %get-tuple-element.25.rest_4_), channel_id=1, source_target_pairs={{8,16},{9,17},{10,18},{11,19},{12,20},{13,21},{14,22},{15,23},{16,... | collective-permute-start | bytes 393224 | tf_op jit(solution)/shard_map/ppermute | solution.py:207
  40.6 2.4 %collective-permute-start.14 = (bf16[64,512]{1,0:T(8,128)(2,1)S(1)}, bf16[64,512]{1,0:T(8,128)(2,1)S(1)}, u32[]{:S(2)}, u32[]{:S(2)}) collective-permute-start(bf16[64,512]{1,0:T(8,128)(2,1)S(1)} %get-tuple-element.42), channel_id=1, source_target_pairs={{0,7},{1,0},{2,1},{3,2},{4,3},{5,4},{6,5},{7,6},{8,15},{9,8},{10,9... | collective-permute-start | bytes 196616 | tf_op jit(solution)/shard_map/ppermute | solution.py:210
  41.2 4.6 %collective-permute-start.13 = (bf16[64,512]{1,0:T(8,128)(2,1)S(1)}, bf16[64,512]{1,0:T(8,128)(2,1)S(1)}, u32[]{:S(2)}, u32[]{:S(2)}) collective-permute-start(bf16[64,512]{1,0:T(8,128)(2,1)S(1)} %get-tuple-element.43), channel_id=1, source_target_pairs={{0,1},{1,2},{2,3},{3,4},{4,5},{5,6},{6,7},{7,0},{8,9},{9,10},{10,1... | collective-permute-start | bytes 196616 | tf_op jit(solution)/shard_map/ppermute | solution.py:210
  41.2 19.3 %collective-permute-start.11 = (bf16[64,3072]{1,0:T(8,128)(2,1)}, bf16[64,3072]{1,0:T(8,128)(2,1)S(1)}, u32[]{:S(2)}, u32[]{:S(2)}) collective-permute-start(bf16[64,3072]{1,0:T(8,128)(2,1)} %get-tuple-element.26.rest_5_), channel_id=1, source_target_pairs={{8,16},{9,17},{10,18},{11,19},{12,20},{13,21},{14,22},{15,23},{16,... | collective-permute-start | bytes 1179656 | tf_op jit(solution)/shard_map/ppermute | solution.py:207
  54.5 17.2 %collective-permute-start.20 = (bf16[64,1024]{1,0:T(8,128)(2,1)S(1)}, bf16[64,1024]{1,0:T(8,128)(2,1)S(1)}, u32[]{:S(2)}, u32[]{:S(2)}) collective-permute-start(bf16[64,1024]{1,0:T(8,128)(2,1)S(1)} %get-tuple-element.32.rest_10_), channel_id=1, source_target_pairs={{16,24},{17,25},{18,26},{19,27},{20,28},{21,29},{22,30},{23,31},{8... | collective-permute-start | bytes 393224 | tf_op jit(solution)/shard_map/ppermute | solution.py:207
  55.8 2.4 %collective-permute-start.10 = (bf16[64,512]{1,0:T(8,128)(2,1)S(1)}, bf16[64,512]{1,0:T(8,128)(2,1)S(1)}, u32[]{:S(2)}, u32[]{:S(2)}) collective-permute-start(bf16[64,512]{1,0:T(8,128)(2,1)S(1)} %get-tuple-element.44), channel_id=1, source_target_pairs={{0,7},{1,0},{2,1},{3,2},{4,3},{5,4},{6,5},{7,6},{8,15},{9,8},{10,9... | collective-permute-start | bytes 196616 | tf_op jit(solution)/shard_map/ppermute | solution.py:210
  55.9 4.6 %collective-permute-start.9 = (bf16[64,512]{1,0:T(8,128)(2,1)S(1)}, bf16[64,512]{1,0:T(8,128)(2,1)S(1)}, u32[]{:S(2)}, u32[]{:S(2)}) collective-permute-start(bf16[64,512]{1,0:T(8,128)(2,1)S(1)} %get-tuple-element.45), channel_id=1, source_target_pairs={{0,1},{1,2},{2,3},{3,4},{4,5},{5,6},{6,7},{7,0},{8,9},{9,10},{10,1... | collective-permute-start | bytes 196616 | tf_op jit(solution)/shard_map/ppermute | solution.py:210
  56.4 30.7 %collective-permute-start.23 = (bf16[64,3072]{1,0:T(8,128)(2,1)}, bf16[64,3072]{1,0:T(8,128)(2,1)S(1)}, u32[]{:S(2)}, u32[]{:S(2)}) collective-permute-start(bf16[64,3072]{1,0:T(8,128)(2,1)} %get-tuple-element.33.rest_11_), channel_id=1, source_target_pairs={{16,24},{17,25},{18,26},{19,27},{20,28},{21,29},{22,30},{23,31},{8... | collective-permute-start | bytes 1179656 | tf_op jit(solution)/shard_map/ppermute | solution.py:207
  61.8 22.4 %collective-permute-start.16 = (bf16[64,1024]{1,0:T(8,128)(2,1)S(1)}, bf16[64,1024]{1,0:T(8,128)(2,1)S(1)}, u32[]{:S(2)}, u32[]{:S(2)}) collective-permute-start(bf16[64,1024]{1,0:T(8,128)(2,1)S(1)} %get-tuple-element.30.rest_8_), channel_id=1, source_target_pairs={{16,24},{17,25},{18,26},{19,27},{20,28},{21,29},{22,30},{23,31},{8... | collective-permute-start | bytes 393224 | tf_op jit(solution)/shard_map/ppermute | solution.py:207
  63.1 32.5 %collective-permute-start.19 = (bf16[64,3072]{1,0:T(8,128)(2,1)}, bf16[64,3072]{1,0:T(8,128)(2,1)S(1)}, u32[]{:S(2)}, u32[]{:S(2)}) collective-permute-start(bf16[64,3072]{1,0:T(8,128)(2,1)} %get-tuple-element.31.rest_9_), channel_id=1, source_target_pairs={{16,24},{17,25},{18,26},{19,27},{20,28},{21,29},{22,30},{23,31},{8... | collective-permute-start | bytes 1179656 | tf_op jit(solution)/shard_map/ppermute | solution.py:207
  72.3 14.7 %collective-permute-start.22 = (bf16[64,512]{1,0:T(8,128)(2,1)S(1)}, bf16[64,512]{1,0:T(8,128)(2,1)S(1)}, u32[]{:S(2)}, u32[]{:S(2)}) collective-permute-start(bf16[64,512]{1,0:T(8,128)(2,1)S(1)} %get-tuple-element.38), channel_id=1, source_target_pairs={{0,7},{1,0},{2,1},{3,2},{4,3},{5,4},{6,5},{7,6},{8,15},{9,8},{10,9... | collective-permute-start | bytes 196616 | tf_op jit(solution)/shard_map/ppermute | solution.py:210
  73.6 13.5 %collective-permute-start.21 = (bf16[64,512]{1,0:T(8,128)(2,1)}, bf16[64,512]{1,0:T(8,128)(2,1)S(1)}, u32[]{:S(2)}, u32[]{:S(2)}) collective-permute-start(bf16[64,512]{1,0:T(8,128)(2,1)} %get-tuple-element.39), channel_id=1, source_target_pairs={{0,1},{1,2},{2,3},{3,4},{4,5},{5,6},{6,7},{7,0},{8,9},{9,10},{10,1... | collective-permute-start | bytes 196616 | tf_op jit(solution)/shard_map/ppermute | solution.py:210
  84.9 10.7 %collective-permute-start.18 = (bf16[64,512]{1,0:T(8,128)(2,1)}, bf16[64,512]{1,0:T(8,128)(2,1)}, u32[]{:S(2)}, u32[]{:S(2)}) collective-permute-start(bf16[64,512]{1,0:T(8,128)(2,1)} %get-tuple-element.40), channel_id=1, source_target_pairs={{0,7},{1,0},{2,1},{3,2},{4,3},{5,4},{6,5},{7,6},{8,15},{9,8},{10,9... | collective-permute-start | bytes 196616 | tf_op jit(solution)/shard_map/ppermute | solution.py:210
  87.0 8.6 %collective-permute-start.17 = (bf16[64,512]{1,0:T(8,128)(2,1)}, bf16[64,512]{1,0:T(8,128)(2,1)}, u32[]{:S(2)}, u32[]{:S(2)}) collective-permute-start(bf16[64,512]{1,0:T(8,128)(2,1)} %get-tuple-element.41), channel_id=1, source_target_pairs={{0,1},{1,2},{2,3},{3,4},{4,5},{5,6},{6,7},{7,0},{8,9},{9,10},{10,1... | collective-permute-start | bytes 196616 | tf_op jit(solution)/shard_map/ppermute | solution.py:210
  (19 other events, 149.4 us)

commit v2 on v1

v2 whole, which is shorter than its diff:
```python
import functools

import jax
import jax.numpy as jnp
from jax import lax
from jax.experimental import pallas as pl
from jax.experimental.pallas import tpu as pltpu
from jax.sharding import PartitionSpec as P

HB = 4
CHUNKS = 2
ROW_TILE = 16
VMEM = pl.BlockSpec(memory_space=pltpu.VMEM)
SMEM = pl.BlockSpec(memory_space=pltpu.SMEM)
HBM = pl.BlockSpec(memory_space=pltpu.HBM)
ANY = pl.BlockSpec(memory_space=pl.ANY)


def params(mib):
    return pltpu.CompilerParams(vmem_limit_bytes=mib << 20)


def pinned(x, space):
    return pltpu.with_memory_space_constraint(x, space)


def chunk_rows(sources):
    tiles = sources // ROW_TILE
    count = min(CHUNKS, tiles)
    sizes = [(tiles // count + (j < tiles % count)) * ROW_TILE for j in range(count)]
    return [(sum(sizes[:j]), sizes[j]) for j in range(count)]


def is_even():
    return lax.rem(lax.axis_index("cross"), 2) == 0


def in_low_half():
    return lax.axis_index("slab") < lax.axis_size("slab") // 2


def edge_places(halo):
    even = is_even()
    left = pl.multiple_of(jnp.where(even, 0, halo), halo)
    right = pl.multiple_of(jnp.where(even, halo, 0), halo)
    return left, right


def source_kernel(row0, thick_ref, layers_ref, total_ref, edge_ref, *rest):
    *mid, buf, sems = rest
    depth, rows, width = buf.shape
    halo = edge_ref.shape[1] // 2
    thick = thick_ref[0]

    def copy(k):
        return pltpu.make_async_copy(
            layers_ref.at[k, pl.ds(row0, rows), :], buf.at[k], sems.at[k]
        )

    for k in range(depth):
        pl.when(k < thick)(copy(k).start)
    for k in range(depth):
        pl.when(k < thick)(copy(k).wait)
    value = jnp.zeros((rows, width), jnp.float32)
    for k in range(depth):
        value = value + jnp.where(k < thick, buf[k], jnp.bfloat16(0)).astype(jnp.float32)
    total_ref[...] = value
    value = value.astype(jnp.bfloat16)
    left, right = edge_places(halo)
    edge_ref[:, pl.ds(left, halo)] = value[:, :halo]
    edge_ref[:, pl.ds(right, halo)] = value[:, width - halo :]
    if mid:
        mid[0][...] = value[:, halo : width - halo]


def fetch_kernel(low, down_ref, up_ref, after_ref, out_ref, sem):
    del after_ref

    @pl.when(in_low_half() == low)
    def _():
        copy = pltpu.make_async_copy(down_ref.at[0], out_ref, sem)
        copy.start()
        copy.wait()

    @pl.when(in_low_half() != low)
    def _():
        copy = pltpu.make_async_copy(up_ref.at[0], out_ref, sem)
        copy.start()
        copy.wait()


def product_kernel(hop, parts, cols_ref, far_ref, near_ref, *rest):
    ins, (green_ref, total_ref), outs, ext = (
        rest[:parts],
        rest[parts : parts + 2],
        rest[parts + 2 : -1],
        rest[-1],
    )
    width = total_ref.shape[1]
    halo = far_ref.shape[1]
    bsize = green_ref.shape[-1]
    per_dev = width // bsize
    kcount = green_ref.shape[0] // per_dev
    slab = lax.axis_index("slab")
    active = jnp.logical_or(slab == hop, slab == lax.axis_size("slab") - 1 - hop)

    @pl.when(active)
    def _():
        left, right = edge_places(halo)
        ext[:, pl.ds(halo, halo)] = ins[0][:, pl.ds(left, halo)]
        ext[:, pl.ds(width, halo)] = ins[0][:, pl.ds(right, halo)]
        if parts == 2:
            ext[:, 2 * halo : width] = ins[1][...]

        @pl.when(is_even())
        def _():
            ext[:, :halo] = far_ref[...]
            ext[:, halo + width :] = near_ref[...]

        @pl.when(jnp.logical_not(is_even()))
        def _():
            ext[:, :halo] = near_ref[...]
            ext[:, halo + width :] = far_ref[...]

        for i in range(per_dev):
            picked, blocks = [], []
            for k in range(kcount):
                at = pl.multiple_of(cols_ref[0, i * kcount + k] * bsize, bsize)
                picked.append(ext[:, pl.ds(at, bsize)])
                blocks.append(green_ref[i * kcount + k])
            value = lax.dot_general(
                jnp.concatenate(picked, 1),
                jnp.concatenate(blocks, 1),
                (((1,), (1,)), ((), ())),
                preferred_element_type=jnp.float32,
            )
            value = (value + total_ref[:, i * bsize : (i + 1) * bsize]).astype(jnp.bfloat16)
            at = i * bsize
            if at < halo:
                outs[0][:, pl.ds(pl.multiple_of(left + at, bsize), bsize)] = value
            elif at >= width - halo:
                at = at - (width - halo)
                outs[0][:, pl.ds(pl.multiple_of(right + at, bsize), bsize)] = value
            else:
                outs[1][:, at - halo : at - halo + bsize] = value


def store_kernel(hops, pieces, parts, *rest):
    count = len(hops) * len(pieces) * parts
    ins, (down_ref, up_ref, sems) = rest[:count], rest[-3:]
    width = down_ref.shape[2]
    halo = ins[0].shape[1] // 2
    slab = lax.axis_index("slab")
    last = lax.axis_size("slab") - 1

    def copies(h, out_ref, which):
        left, right = edge_places(halo)
        made = []
        for j, (row0, rows) in enumerate(pieces):
            at = (hops.index(h) * len(pieces) + j) * parts
            span = pl.ds(row0, rows)
            moves = [
                (ins[at].at[:, pl.ds(left, halo)], 0, halo),
                (ins[at].at[:, pl.ds(right, halo)], width - halo, halo),
            ]
            if parts == 2:
                moves.append((ins[at + 1], halo, width - 2 * halo))
            for src, col, size in moves:
                dst = out_ref.at[0, span, pl.ds(col, size)]
                made.append(pltpu.make_async_copy(src, dst, sems.at[which, len(made)]))
        return made

    plan = []
    for h in hops:
        plan.append((h, down_ref, 0, slab == h))
        plan.append((h, up_ref, 1, slab == last - h))
    for h, ref, which, chosen in plan:

        @pl.when(chosen)
        def _():
            for copy in copies(h, ref, which):
                copy.start()

    for h, ref, which, chosen in plan:

        @pl.when(chosen)
        def _():
            for copy in copies(h, ref, which):
                copy.wait()


def shards(thickness, layer_sources, green_down, column_down, green_up, column_up):
    slabs = lax.axis_size("slab")
    cross = lax.axis_size("cross")
    lateral = lax.axis_index("cross")
    depth, sources, width = layer_sources.shape
    bsize = green_down.shape[-1]
    per_dev = width // bsize
    total_blocks = per_dev * cross
    nblocks = green_down.shape[1]
    halo = HB * bsize
    chunks = chunk_rows(sources)
    parts = 2 if per_dev > 2 * HB else 1
    layers = pinned(layer_sources, pltpu.HBM)
    greens = (pinned(green_down, pltpu.HBM), pinned(green_up, pltpu.HBM))

    def trace(rows):
        widths = [2 * halo, width - 2 * halo][:parts]
        return [pltpu.VMEM((rows, w), jnp.bfloat16) for w in widths]

    def local(low):
        cols = jnp.where(in_low_half() == low, column_down, column_up)
        return (cols - lateral * per_dev + HB) % total_blocks

    def fetch(low, after):
        return pl.pallas_call(
            functools.partial(fetch_kernel, low),
            out_shape=pltpu.VMEM(green_down.shape[1:], jnp.bfloat16),
            in_specs=[HBM, HBM, ANY],
            out_specs=VMEM,
            scratch_shapes=[pltpu.SemaphoreType.DMA],
            compiler_params=params(8),
            name="fetch",
        )(*greens, after)

    def source(row0, rows):
        return pl.pallas_call(
            functools.partial(source_kernel, row0),
            out_shape=[pltpu.VMEM((rows, width), jnp.float32), *trace(rows)],
            in_specs=[SMEM, HBM],
            out_specs=[VMEM] * (1 + parts),
            scratch_shapes=[
                pltpu.VMEM((depth, rows, width), jnp.bfloat16),
                pltpu.SemaphoreType.DMA((depth,)),
            ],
            compiler_params=params(8),
            name="source",
        )(thickness, layers)

    def product(h, cols, far, near, got, green, total):
        rows = total.shape[0]
        ins = [pinned(x, pltpu.VMEM) for x in (far, near, *got, green, total)]
        return pl.pallas_call(
            functools.partial(product_kernel, h, parts),
            out_shape=trace(rows),
            in_specs=[SMEM] + [VMEM] * len(ins),
            out_specs=[VMEM] * parts,
            scratch_shapes=[pltpu.VMEM((rows, width + 2 * halo), jnp.bfloat16)],
            compiler_params=params(8),
            cost_estimate=pl.CostEstimate(
                flops=2 * rows * nblocks * bsize * bsize,
                bytes_accessed=nblocks * bsize * bsize * 2,
                transcendentals=0,
            ),
            name="product",
        )(cols, *ins)

    def store(hops, pieces, arrays, into=None):
        ins = [pinned(x, pltpu.VMEM) for x in arrays]
        given = [] if into is None else [pinned(x, pltpu.HBM) for x in into]
        return pl.pallas_call(
            functools.partial(store_kernel, hops, pieces, parts),
            out_shape=[pltpu.HBM((1, sources, width), jnp.bfloat16)] * 2,
            in_specs=[VMEM] * len(ins) + [HBM] * len(given),
            out_specs=[HBM, HBM],
            scratch_shapes=[pltpu.SemaphoreType.DMA((2, len(pieces) * (1 + parts)))],
            input_output_aliases={len(ins) + i: i for i in range(len(given))},
            compiler_params=params(4),
            name="store",
        )(*ins, *given)

    def mate(c):
        return c ^ 1

    def next_chip(c):
        return (c + 1) % cross if c % 2 else (c - 1) % cross

    def hop(x, h):
        there = {s: s for s in range(slabs)}
        for a, b in ((h - 1, h), (slabs - h, slabs - 1 - h)):
            there[a], there[b] = b, a
        route = []
        for s in range(slabs):
            for c in range(cross):
                to = c if there[s] != s else mate(c)
                route.append((s * cross + c, there[s] * cross + to))
        return lax.ppermute(x, ("slab", "cross"), route)

    def to_mate(x):
        return lax.ppermute(x, "cross", [(c, mate(c)) for c in range(cross)])

    def to_next_chip(x, h):
        route = []
        for s in range(slabs):
            for c in range(cross):
                to = next_chip(c) if s in (h, slabs - 1 - h) else mate(c)
                route.append((s * cross + c, s * cross + to))
        return lax.ppermute(x, ("slab", "cross"), route)

    totals, made = [], {}
    for j, (row0, rows) in enumerate(chunks):
        total, *out = source(row0, rows)
        totals.append(total)
        made[0, j] = out
    cols = {low: local(low) for low in (True, False)}
    green = {}
    order = sorted(
        ((h, j) for h in range(1, slabs) for j in range(len(chunks))),
        key=lambda hj: (hj[0] + hj[1], hj[0]),
    )
    for h, j in order:
        got = [hop(x, h) for x in made[h - 1, j]]
        far = to_next_chip(got[0][:, :halo], h)
        near = to_mate(got[0][:, halo:])
        low = h < slabs // 2
        which = (low, h == slabs - 1)
        if which not in green:
            green[which] = fetch(low, got[0])
        made[h, j] = product(h, cols[low], far, near, got, green[which], totals[j])

    early = list(range(slabs - 1))
    outs = store(early, chunks, [x for h in early for j in range(len(chunks)) for x in made[h, j]])
    for j, piece in enumerate(chunks):
        outs = store([slabs - 1], [piece], made[slabs - 1, j], outs)
    return tuple(outs)


def solution(mesh):
    return jax.shard_map(
        shards,
        mesh=mesh,
        in_specs=(
            P("slab"),
            P("slab", None, "cross"),
            P("slab", "cross", None, None),
            P("slab", "cross"),
            P("slab", "cross", None, None),
            P("slab", "cross"),
        ),
        out_specs=(P("slab", None, "cross"), P("slab", None, "cross")),
        check_vma=False,
    )
```

time: 103 us -> 77.9 us (0.76)
  local copies, waits for them, and re-layouts: 23.4 us -> 0.07 us
  waiting for transfers between devices: 32.2 us -> 20.9 us
  Pallas kernels: 19.3 us -> 24.6 us
  starting transfers between devices: 25.6 us -> 30.4 us
    unnamed x38 -> x4, local copies, waits for them, and re-layouts: 21.4 us -> 0.01 us
    ppermute x12, waiting for transfers between devices: 14.2 us -> 1.75 us  [the longest x6 1.42 us: to_mate(): return lax.ppermute(x, 'cross', [(c, mate(c)) for c in range(cross)])]
    ppermute x12, starting transfers between devices: 19 us -> 25.1 us  [hop(): return lax.ppermute(x, ('slab', 'cross'), route)]
    pallas_call x9 -> x14, Pallas kernels: 19.3 us -> 24.6 us  [the longest x3 8.4 us: fetch(): pl.pallas_call(functools.partial(fetch_kernel, low), out_shape=pltpu.VMEM...]
    slice x6, local copies, waits for them, and re-layouts: 1.98 us -> 0.06 us  [shards(): near = to_mate(got[0][:, halo:])]
    ppermute x12, starting transfers between devices: 6.65 us -> 5.3 us  [the longest x6 4.39 us: to_next_chip(): return lax.ppermute(x, ('slab', 'cross'), route)]
    ppermute x12, waiting for transfers between devices: 18 us -> 19.1 us  [hop(): return lax.ppermute(x, ('slab', 'cross'), route)]
  transfers between devices with their start and end apart: 24 -> 24, of which waited for: 10 -> 10; matrix products, arithmetic and copies ran while one was open for 2% -> 0% of each run, Pallas kernels for 11% -> 24%
where the time goes in v2:
time: 77.9 us; the launch traced here: 77.5 us
  starting transfers between devices  30.4 us (39%)
  Pallas kernels  24.6 us (32%)
  waiting for transfers between devices  20.9 us (27%)
  between operations  1.59 us (2%)
    ppermute x12, starting transfers between devices, hop(): return lax.ppermute(x, ('slab', 'cross'), route)  25.1 us
    ppermute x12, waiting for transfers between devices, hop(): return lax.ppermute(x, ('slab', 'cross'), route)  19.1 us
    pallas_call x3, Pallas kernels, fetch(): pl.pallas_call(functools.partial(fetch_kernel, low), out_shape=pltpu.VMEM...  8.4 us
    pallas_call x6, Pallas kernels, product(): pl.pallas_call(functools.partial(product_kernel, h, parts), out_shape=tra...  8.16 us
    ppermute x6, starting transfers between devices, to_next_chip(): return lax.ppermute(x, ('slab', 'cross'), route)  4.39 us
    pallas_call x2, Pallas kernels, source(): pl.pallas_call(functools.partial(source_kernel, row0), out_shape=[pltpu.V...  4.1 us
    pallas_call x3, Pallas kernels, store(): pl.pallas_call(functools.partial(store_kernel, hops, pieces, parts), out_...  3.92 us
  transfers between devices with their start and end apart: 24, of which 10 were waited for; matrix products, arithmetic and copies ran while one was open for 0% of the time, Pallas kernels for 24%

profile of v2, /device:TPU:0, one launch (start us, length us, event | category | flops | bytes accessed | tf_op | source)
XLA Modules:
  0.0 77.5 jit_solution(10771123412735688607)
XLA Ops:
  1.3 2.0 %source.3 = (f32[64,4096]{1,0:T(8,128)S(1)}, bf16[64,1024]{1,0:T(8,128)(2,1)}, bf16[64,3072]{1,0:T(8,128)(2,1)S(1)}) custom-call(s32[1]{0:T(128)S(6)} %copy.16.thick_ref, bf16[4,128,4096]{2,1,0:T(8,128)(2,1)} %layers_ref.3), custom_call_target="tpu_custom_call" | custom-call | tf_op jit(solution)/shard_map/source/pallas_call | solution.py:227
  3.3 3.6 %collective-permute-start.4 = (bf16[64,1024]{1,0:T(8,128)(2,1)}, bf16[64,1024]{1,0:T(8,128)(2,1)S(1)}, u32[]{:S(2)}, u32[]{:S(2)}) collective-permute-start(bf16[64,1024]{1,0:T(8,128)(2,1)} %get-tuple-element.26.rest_0_), channel_id=1, source_target_pairs={{0,8},{1,9},{2,10},{3,11},{4,12},{5,13},{6,14},{7,15},{8,0},{9,1},... | collective-permute-start | bytes 393224 | tf_op jit(solution)/shard_map/ppermute | solution.py:287
  7.0 2.1 %source.2 = (f32[64,4096]{1,0:T(8,128)S(1)}, bf16[64,1024]{1,0:T(8,128)(2,1)}, bf16[64,3072]{1,0:T(8,128)(2,1)}) custom-call(s32[1]{0:T(128)S(6)} %copy.16.thick_ref, bf16[4,128,4096]{2,1,0:T(8,128)(2,1)} %layers_ref.3), custom_call_target="tpu_custom_call" | custom-call | tf_op jit(solution)/shard_map/source/pallas_call | solution.py:227
  9.1 2.5 %collective-permute-start = (bf16[64,1024]{1,0:T(8,128)(2,1)}, bf16[64,1024]{1,0:T(8,128)(2,1)S(1)}, u32[]{:S(2)}, u32[]{:S(2)}) collective-permute-start(bf16[64,1024]{1,0:T(8,128)(2,1)} %get-tuple-element.24.rest_2_), channel_id=1, source_target_pairs={{0,8},{1,9},{2,10},{3,11},{4,12},{5,13},{6,14},{7,15},{8,0},{9,1},... | collective-permute-start | bytes 393224 | tf_op jit(solution)/shard_map/ppermute | solution.py:287
  12.3 2.8 %fetch.3.rest_2_ = bf16[192,128,128]{2,1,0:T(8,128)(2,1)S(1)} custom-call(bf16[1,192,128,128]{3,2,1,0:T(8,128)(2,1)} %down_ref.5, bf16[1,192,128,128]{3,2,1,0:T(8,128)(2,1)} %up_ref.5, bf16[64,1024]{1,0:T(8,128)(2,1)S(1)} %collective-permute-done.4.after_ref.rest_0_), custom_call_target="tpu_custom_call" | custom-call | tf_op jit(solution)/shard_map/fetch/pallas_call | solution.py:216
  15.1 4.8 %collective-permute-done.11.rest_1_ = bf16[64,3072]{1,0:T(8,128)(2,1)S(1)} collective-permute-done((bf16[64,3072]{1,0:T(8,128)(2,1)S(1)}, bf16[64,3072]{1,0:T(8,128)(2,1)S(1)}, u32[]{:S(2)}, u32[]{:S(2)}) %collective-permute-start.11) | collective-permute-done | bytes 393248 | tf_op jit(solution)/shard_map/ppermute | solution.py:287
  20.5 2.2 %collective-permute-done.rest_0_ = bf16[64,1024]{1,0:T(8,128)(2,1)S(1)} collective-permute-done((bf16[64,1024]{1,0:T(8,128)(2,1)}, bf16[64,1024]{1,0:T(8,128)(2,1)S(1)}, u32[]{:S(2)}, u32[]{:S(2)}) %collective-permute-start) | collective-permute-done | bytes 131104 | tf_op jit(solution)/shard_map/ppermute | solution.py:287
  24.1 6.1 %collective-permute-done.3.rest_1_ = bf16[64,3072]{1,0:T(8,128)(2,1)S(1)} collective-permute-done((bf16[64,3072]{1,0:T(8,128)(2,1)}, bf16[64,3072]{1,0:T(8,128)(2,1)S(1)}, u32[]{:S(2)}, u32[]{:S(2)}) %collective-permute-start.3) | collective-permute-done | bytes 393248 | tf_op jit(solution)/shard_map/ppermute | solution.py:287
  32.0 2.8 %fetch.4.rest_2_ = bf16[192,128,128]{2,1,0:T(8,128)(2,1)S(1)} custom-call(bf16[1,192,128,128]{3,2,1,0:T(8,128)(2,1)} %down_ref.5, bf16[1,192,128,128]{3,2,1,0:T(8,128)(2,1)} %up_ref.5, bf16[64,1024]{1,0:T(8,128)(2,1)S(1)} %collective-permute-done.12.after_ref.rest_0_), custom_call_target="tpu_custom_call" | custom-call | tf_op jit(solution)/shard_map/fetch/pallas_call | solution.py:216
  35.4 10.1 %collective-permute-start.20 = (bf16[64,1024]{1,0:T(8,128)(2,1)S(1)}, bf16[64,1024]{1,0:T(8,128)(2,1)S(1)}, u32[]{:S(2)}, u32[]{:S(2)}) collective-permute-start(bf16[64,1024]{1,0:T(8,128)(2,1)S(1)} %get-tuple-element.36.rest_8_), channel_id=1, source_target_pairs={{0,8},{1,9},{2,10},{3,11},{4,12},{5,13},{6,14},{7,15},{8,0},{9,1},... | collective-permute-start | bytes 393224 | tf_op jit(solution)/shard_map/ppermute | solution.py:287
  46.1 0.7 collective-permute-done.7.near_ref
  47.6 6.1 %collective-permute-start.13 = (bf16[64,1024]{1,0:T(8,128)(2,1)S(1)}, bf16[64,1024]{1,0:T(8,128)(2,1)S(1)}, u32[]{:S(2)}, u32[]{:S(2)}) collective-permute-start(bf16[64,1024]{1,0:T(8,128)(2,1)S(1)} %get-tuple-element.33.rest_10_), channel_id=1, source_target_pairs={{0,8},{1,9},{2,10},{3,11},{4,12},{5,13},{6,14},{7,15},{8,0},{9,1},... | collective-permute-start | bytes 393224 | tf_op jit(solution)/shard_map/ppermute | solution.py:287
  53.8 1.9 %collective-permute-start.16 = (bf16[64,3072]{1,0:T(8,128)(2,1)S(1)}, bf16[64,3072]{1,0:T(8,128)(2,1)S(1)}, u32[]{:S(2)}, u32[]{:S(2)}) collective-permute-start(bf16[64,3072]{1,0:T(8,128)(2,1)S(1)} %get-tuple-element.34.rest_11_), channel_id=1, source_target_pairs={{0,8},{1,9},{2,10},{3,11},{4,12},{5,13},{6,14},{7,15},{8,0},{9,1},... | collective-permute-start | bytes 1179656 | tf_op jit(solution)/shard_map/ppermute | solution.py:287
  55.8 1.4 %collective-permute-start.21 = (bf16[64,512]{1,0:T(8,128)(2,1)S(1)}, bf16[64,512]{1,0:T(8,128)(2,1)S(1)}, u32[]{:S(2)}, u32[]{:S(2)}) collective-permute-start(bf16[64,512]{1,0:T(8,128)(2,1)S(1)} %get-tuple-element.47), channel_id=1, source_target_pairs={{0,7},{1,2},{2,1},{3,4},{4,3},{5,6},{6,5},{7,0},{8,9},{9,8},{10,11... | collective-permute-start | bytes 196616 | tf_op jit(solution)/shard_map/ppermute | solution.py:298
  57.2 0.8 %collective-permute-done.13.rest_0_ = bf16[64,1024]{1,0:T(8,128)(2,1)S(1)} collective-permute-done((bf16[64,1024]{1,0:T(8,128)(2,1)S(1)}, bf16[64,1024]{1,0:T(8,128)(2,1)S(1)}, u32[]{:S(2)}, u32[]{:S(2)}) %collective-permute-start.13) | collective-permute-done | bytes 131104 | tf_op jit(solution)/shard_map/ppermute | solution.py:287
  58.2 1.4 %collective-permute-start.14 = (bf16[64,512]{1,0:T(8,128)(2,1)S(1)}, bf16[64,512]{1,0:T(8,128)(2,1)S(1)}, u32[]{:S(2)}, u32[]{:S(2)}) collective-permute-start(bf16[64,512]{1,0:T(8,128)(2,1)S(1)} %get-tuple-element.51), channel_id=1, source_target_pairs={{0,7},{1,2},{2,1},{3,4},{4,3},{5,6},{6,5},{7,0},{8,9},{9,8},{10,11... | collective-permute-start | bytes 196616 | tf_op jit(solution)/shard_map/ppermute | solution.py:298
  59.6 2.2 %store.3 = (bf16[1,128,4096]{2,1,0:T(8,128)(2,1)}, bf16[1,128,4096]{2,1,0:T(8,128)(2,1)}) custom-call(bf16[64,1024]{1,0:T(8,128)(2,1)} %get-tuple-element.26.rest_0_, bf16[64,3072]{1,0:T(8,128)(2,1)S(1)} %get-tuple-element.30.rest_1_, bf16[64,1024]{1,0:T(8,128)(2,1)} %get-tuple-element.24.rest_2_, bf16[64,3072]{1,0:T(8,128)(2,1)} %get-tuple-element.25.rest_3_, ...), custom_call_target="tpu_custom_call" | custom-call | tf_op jit(solution)/shard_map/store/pallas_call | solution.py:261
  61.8 2.8 %fetch.5.rest_2_ = bf16[192,128,128]{2,1,0:T(8,128)(2,1)S(1)} custom-call(bf16[1,192,128,128]{3,2,1,0:T(8,128)(2,1)} %down_ref.5, bf16[1,192,128,128]{3,2,1,0:T(8,128)(2,1)} %up_ref.5, bf16[64,1024]{1,0:T(8,128)(2,1)S(1)} %collective-permute-done.20.after_ref.rest_0_), custom_call_target="tpu_custom_call" | custom-call | tf_op jit(solution)/shard_map/fetch/pallas_call | solution.py:216
  64.6 1.9 %collective-permute-done.23.rest_1_ = bf16[64,3072]{1,0:T(8,128)(2,1)S(1)} collective-permute-done((bf16[64,3072]{1,0:T(8,128)(2,1)S(1)}, bf16[64,3072]{1,0:T(8,128)(2,1)S(1)}, u32[]{:S(2)}, u32[]{:S(2)}) %collective-permute-start.23) | collective-permute-done | bytes 393248 | tf_op jit(solution)/shard_map/ppermute | solution.py:287
  66.5 3.0 %product.11 = (bf16[64,1024]{1,0:T(8,128)(2,1)S(1)}, bf16[64,3072]{1,0:T(8,128)(2,1)S(1)}) custom-call(s32[1,192]{1,0:T(1,128)S(1)} %get-tuple-element.59.cols_ref, bf16[64,512]{1,0:T(8,128)(2,1)S(1)} %collective-permute-done.21.far_ref, bf16[64,512]{1,0:T(8,128)(2,1)S(1)} %collective-permute-done.22.near_ref, ...), custom_call_target="tpu_custom_call" | custom-call | flops 402653184 | bytes 6291456 | tf_op jit(solution)/shard_map/product/pallas_call | solution.py:243
  69.4 0.9 %store.4 = (bf16[1,128,4096]{2,1,0:T(8,128)(2,1)}, bf16[1,128,4096]{2,1,0:T(8,128)(2,1)}) custom-call(bf16[64,1024]{1,0:T(8,128)(2,1)S(1)} %get-tuple-element.40.rest_0_, bf16[64,3072]{1,0:T(8,128)(2,1)S(1)} %get-tuple-element.41.rest_1_, bf16[1,128,4096]{2,1,0:T(8,128)(2,1)} %get-tuple-element.42.rest_2_, ...), custom_call_target="tpu_custom_call", output_to_operand_aliasing={{0}: (2, {}), {1}: (3, {})} | custom-call | tf_op jit(solution)/shard_map/store/pallas_call | solution.py:261
  70.3 3.4 %collective-permute-done.16.rest_1_ = bf16[64,3072]{1,0:T(8,128)(2,1)S(1)} collective-permute-done((bf16[64,3072]{1,0:T(8,128)(2,1)S(1)}, bf16[64,3072]{1,0:T(8,128)(2,1)S(1)}, u32[]{:S(2)}, u32[]{:S(2)}) %collective-permute-start.16) | collective-permute-done | bytes 393248 | tf_op jit(solution)/shard_map/ppermute | solution.py:287
  73.7 3.0 %product.10 = (bf16[64,1024]{1,0:T(8,128)(2,1)S(1)}, bf16[64,3072]{1,0:T(8,128)(2,1)S(1)}) custom-call(s32[1,192]{1,0:T(1,128)S(1)} %get-tuple-element.59.cols_ref, bf16[64,512]{1,0:T(8,128)(2,1)S(1)} %collective-permute-done.14.far_ref, bf16[64,512]{1,0:T(8,128)(2,1)S(1)} %collective-permute-done.15.near_ref, ...), custom_call_target="tpu_custom_call" | custom-call | flops 402653184 | bytes 6291456 | tf_op jit(solution)/shard_map/product/pallas_call | solution.py:243
  76.7 0.9 %store.5 = (bf16[1,128,4096]{2,1,0:T(8,128)(2,1)}, bf16[1,128,4096]{2,1,0:T(8,128)(2,1)}) custom-call(bf16[64,1024]{1,0:T(8,128)(2,1)S(1)} %get-tuple-element.37.rest_0_, bf16[64,3072]{1,0:T(8,128)(2,1)S(1)} %get-tuple-element.38.rest_1_, bf16[1,128,4096]{2,1,0:T(8,128)(2,1)} %get-tuple-element.44.rest_2_, ...), custom_call_target="tpu_custom_call", output_to_operand_aliasing={{0}: (2, {}), {1}: (3, {})} | custom-call | tf_op jit(solution)/shard_map/store/pallas_call | solution.py:261
  (49 shorter events, 6.7 us)
Async XLA Ops:
  3.3 8.3 %collective-permute-start.4 = (bf16[64,1024]{1,0:T(8,128)(2,1)}, bf16[64,1024]{1,0:T(8,128)(2,1)S(1)}, u32[]{:S(2)}, u32[]{:S(2)}) collective-permute-start(bf16[64,1024]{1,0:T(8,128)(2,1)} %get-tuple-element.26.rest_0_), channel_id=1, source_target_pairs={{0,8},{1,9},{2,10},{3,11},{4,12},{5,13},{6,14},{7,15},{8,0},{9,1},... | collective-permute-start | bytes 393224 | tf_op jit(solution)/shard_map/ppermute | solution.py:287
  6.9 13.0 %collective-permute-start.11 = (bf16[64,3072]{1,0:T(8,128)(2,1)S(1)}, bf16[64,3072]{1,0:T(8,128)(2,1)S(1)}, u32[]{:S(2)}, u32[]{:S(2)}) collective-permute-start(bf16[64,3072]{1,0:T(8,128)(2,1)S(1)} %get-tuple-element.30.rest_1_), channel_id=1, source_target_pairs={{0,8},{1,9},{2,10},{3,11},{4,12},{5,13},{6,14},{7,15},{8,0},{9,1},... | collective-permute-start | bytes 1179656 | tf_op jit(solution)/shard_map/ppermute | solution.py:287
  9.1 13.6 %collective-permute-start = (bf16[64,1024]{1,0:T(8,128)(2,1)}, bf16[64,1024]{1,0:T(8,128)(2,1)S(1)}, u32[]{:S(2)}, u32[]{:S(2)}) collective-permute-start(bf16[64,1024]{1,0:T(8,128)(2,1)} %get-tuple-element.24.rest_2_), channel_id=1, source_target_pairs={{0,8},{1,9},{2,10},{3,11},{4,12},{5,13},{6,14},{7,15},{8,0},{9,1},... | collective-permute-start | bytes 393224 | tf_op jit(solution)/shard_map/ppermute | solution.py:287
  11.6 18.7 %collective-permute-start.3 = (bf16[64,3072]{1,0:T(8,128)(2,1)}, bf16[64,3072]{1,0:T(8,128)(2,1)S(1)}, u32[]{:S(2)}, u32[]{:S(2)}) collective-permute-start(bf16[64,3072]{1,0:T(8,128)(2,1)} %get-tuple-element.25.rest_3_), channel_id=1, source_target_pairs={{0,8},{1,9},{2,10},{3,11},{4,12},{5,13},{6,14},{7,15},{8,0},{9,1},... | collective-permute-start | bytes 1179656 | tf_op jit(solution)/shard_map/ppermute | solution.py:287
  11.7 3.4 %collective-permute-start.10 = (bf16[64,512]{1,0:T(8,128)(2,1)S(1)}, bf16[64,512]{1,0:T(8,128)(2,1)S(1)}, u32[]{:S(2)}, u32[]{:S(2)}) collective-permute-start(bf16[64,512]{1,0:T(8,128)(2,1)S(1)} %get-tuple-element.52), channel_id=1, source_target_pairs={{0,1},{1,0},{2,3},{3,2},{4,5},{5,4},{6,7},{7,6},{8,9},{9,8},{10,11... | collective-permute-start | bytes 196616 | tf_op jit(solution)/shard_map/ppermute | solution.py:290
  11.7 3.3 %collective-permute-start.9 = (bf16[64,512]{1,0:T(8,128)(2,1)S(1)}, bf16[64,512]{1,0:T(8,128)(2,1)S(1)}, u32[]{:S(2)}, u32[]{:S(2)}) collective-permute-start(bf16[64,512]{1,0:T(8,128)(2,1)S(1)} %get-tuple-element.53), channel_id=1, source_target_pairs={{0,1},{1,0},{2,3},{3,2},{4,5},{5,4},{6,7},{7,6},{8,15},{9,10},{10,... | collective-permute-start | bytes 196616 | tf_op jit(solution)/shard_map/ppermute | solution.py:298
  20.4 10.5 %collective-permute-start.12 = (bf16[64,1024]{1,0:T(8,128)(2,1)S(1)}, bf16[64,1024]{1,0:T(8,128)(2,1)S(1)}, u32[]{:S(2)}, u32[]{:S(2)}) collective-permute-start(bf16[64,1024]{1,0:T(8,128)(2,1)S(1)} %get-tuple-element.32.rest_4_), channel_id=1, source_target_pairs={{0,1},{1,0},{2,3},{3,2},{4,5},{5,4},{6,7},{7,6},{8,16},{9,17},{10,... | collective-permute-start | bytes 393224 | tf_op jit(solution)/shard_map/ppermute | solution.py:287
  22.7 1.3 %collective-permute-start.2 = (bf16[64,512]{1,0:T(8,128)(2,1)S(1)}, bf16[64,512]{1,0:T(8,128)(2,1)S(1)}, u32[]{:S(2)}, u32[]{:S(2)}) collective-permute-start(bf16[64,512]{1,0:T(8,128)(2,1)S(1)} %get-tuple-element.56), channel_id=1, source_target_pairs={{0,1},{1,0},{2,3},{3,2},{4,5},{5,4},{6,7},{7,6},{8,9},{9,8},{10,11... | collective-permute-start | bytes 196616 | tf_op jit(solution)/shard_map/ppermute | solution.py:290
  22.7 1.4 %collective-permute-start.1 = (bf16[64,512]{1,0:T(8,128)(2,1)S(1)}, bf16[64,512]{1,0:T(8,128)(2,1)S(1)}, u32[]{:S(2)}, u32[]{:S(2)}) collective-permute-start(bf16[64,512]{1,0:T(8,128)(2,1)S(1)} %get-tuple-element.57), channel_id=1, source_target_pairs={{0,1},{1,0},{2,3},{3,2},{4,5},{5,4},{6,7},{7,6},{8,15},{9,10},{10,... | collective-permute-start | bytes 196616 | tf_op jit(solution)/shard_map/ppermute | solution.py:298
  23.2 11.6 %collective-permute-start.19 = (bf16[64,3072]{1,0:T(8,128)(2,1)S(1)}, bf16[64,3072]{1,0:T(8,128)(2,1)S(1)}, u32[]{:S(2)}, u32[]{:S(2)}) collective-permute-start(bf16[64,3072]{1,0:T(8,128)(2,1)S(1)} %get-tuple-element.35.rest_5_), channel_id=1, source_target_pairs={{0,1},{1,0},{2,3},{3,2},{4,5},{5,4},{6,7},{7,6},{8,16},{9,17},{10,... | collective-permute-start | bytes 1179656 | tf_op jit(solution)/shard_map/ppermute | solution.py:287
  30.8 14.7 %collective-permute-start.5 = (bf16[64,1024]{1,0:T(8,128)(2,1)S(1)}, bf16[64,1024]{1,0:T(8,128)(2,1)S(1)}, u32[]{:S(2)}, u32[]{:S(2)}) collective-permute-start(bf16[64,1024]{1,0:T(8,128)(2,1)S(1)} %get-tuple-element.28.rest_6_), channel_id=1, source_target_pairs={{0,1},{1,0},{2,3},{3,2},{4,5},{5,4},{6,7},{7,6},{8,16},{9,17},{10,... | collective-permute-start | bytes 393224 | tf_op jit(solution)/shard_map/ppermute | solution.py:287
  30.9 3.9 %collective-permute-start.18 = (bf16[64,512]{1,0:T(8,128)(2,1)S(1)}, bf16[64,512]{1,0:T(8,128)(2,1)S(1)}, u32[]{:S(2)}, u32[]{:S(2)}) collective-permute-start(bf16[64,512]{1,0:T(8,128)(2,1)S(1)} %get-tuple-element.48), channel_id=1, source_target_pairs={{0,1},{1,0},{2,3},{3,2},{4,5},{5,4},{6,7},{7,6},{8,9},{9,8},{10,11... | collective-permute-start | bytes 196616 | tf_op jit(solution)/shard_map/ppermute | solution.py:290
  31.5 3.3 %collective-permute-start.17 = (bf16[64,512]{1,0:T(8,128)(2,1)S(1)}, bf16[64,512]{1,0:T(8,128)(2,1)S(1)}, u32[]{:S(2)}, u32[]{:S(2)}) collective-permute-start(bf16[64,512]{1,0:T(8,128)(2,1)S(1)} %get-tuple-element.49), channel_id=1, source_target_pairs={{0,1},{1,0},{2,3},{3,2},{4,5},{5,4},{6,7},{7,6},{8,15},{9,10},{10,... | collective-permute-start | bytes 196616 | tf_op jit(solution)/shard_map/ppermute | solution.py:298
  31.6 15.5 %collective-permute-start.8 = (bf16[64,3072]{1,0:T(8,128)(2,1)S(1)}, bf16[64,3072]{1,0:T(8,128)(2,1)S(1)}, u32[]{:S(2)}, u32[]{:S(2)}) collective-permute-start(bf16[64,3072]{1,0:T(8,128)(2,1)S(1)} %get-tuple-element.29.rest_7_), channel_id=1, source_target_pairs={{0,1},{1,0},{2,3},{3,2},{4,5},{5,4},{6,7},{7,6},{8,16},{9,17},{10,... | collective-permute-start | bytes 1179656 | tf_op jit(solution)/shard_map/ppermute | solution.py:287
  35.4 20.3 %collective-permute-start.20 = (bf16[64,1024]{1,0:T(8,128)(2,1)S(1)}, bf16[64,1024]{1,0:T(8,128)(2,1)S(1)}, u32[]{:S(2)}, u32[]{:S(2)}) collective-permute-start(bf16[64,1024]{1,0:T(8,128)(2,1)S(1)} %get-tuple-element.36.rest_8_), channel_id=1, source_target_pairs={{0,8},{1,9},{2,10},{3,11},{4,12},{5,13},{6,14},{7,15},{8,0},{9,1},... | collective-permute-start | bytes 393224 | tf_op jit(solution)/shard_map/ppermute | solution.py:287
  45.6 1.3 %collective-permute-start.7 = (bf16[64,512]{1,0:T(8,128)(2,1)S(1)}, bf16[64,512]{1,0:T(8,128)(2,1)S(1)}, u32[]{:S(2)}, u32[]{:S(2)}) collective-permute-start(bf16[64,512]{1,0:T(8,128)(2,1)S(1)} %get-tuple-element.54), channel_id=1, source_target_pairs={{0,1},{1,0},{2,3},{3,2},{4,5},{5,4},{6,7},{7,6},{8,9},{9,8},{10,11... | collective-permute-start | bytes 196616 | tf_op jit(solution)/shard_map/ppermute | solution.py:290
  45.6 1.4 %collective-permute-start.6 = (bf16[64,512]{1,0:T(8,128)(2,1)S(1)}, bf16[64,512]{1,0:T(8,128)(2,1)S(1)}, u32[]{:S(2)}, u32[]{:S(2)}) collective-permute-start(bf16[64,512]{1,0:T(8,128)(2,1)S(1)} %get-tuple-element.55), channel_id=1, source_target_pairs={{0,1},{1,0},{2,3},{3,2},{4,5},{5,4},{6,7},{7,6},{8,15},{9,10},{10,... | collective-permute-start | bytes 196616 | tf_op jit(solution)/shard_map/ppermute | solution.py:298
  47.6 10.5 %collective-permute-start.13 = (bf16[64,1024]{1,0:T(8,128)(2,1)S(1)}, bf16[64,1024]{1,0:T(8,128)(2,1)S(1)}, u32[]{:S(2)}, u32[]{:S(2)}) collective-permute-start(bf16[64,1024]{1,0:T(8,128)(2,1)S(1)} %get-tuple-element.33.rest_10_), channel_id=1, source_target_pairs={{0,8},{1,9},{2,10},{3,11},{4,12},{5,13},{6,14},{7,15},{8,0},{9,1},... | collective-permute-start | bytes 393224 | tf_op jit(solution)/shard_map/ppermute | solution.py:287
  53.7 12.8 %collective-permute-start.23 = (bf16[64,3072]{1,0:T(8,128)(2,1)S(1)}, bf16[64,3072]{1,0:T(8,128)(2,1)S(1)}, u32[]{:S(2)}, u32[]{:S(2)}) collective-permute-start(bf16[64,3072]{1,0:T(8,128)(2,1)S(1)} %get-tuple-element.39.rest_9_), channel_id=1, source_target_pairs={{0,8},{1,9},{2,10},{3,11},{4,12},{5,13},{6,14},{7,15},{8,0},{9,1},... | collective-permute-start | bytes 1179656 | tf_op jit(solution)/shard_map/ppermute | solution.py:287
  53.8 19.9 %collective-permute-start.16 = (bf16[64,3072]{1,0:T(8,128)(2,1)S(1)}, bf16[64,3072]{1,0:T(8,128)(2,1)S(1)}, u32[]{:S(2)}, u32[]{:S(2)}) collective-permute-start(bf16[64,3072]{1,0:T(8,128)(2,1)S(1)} %get-tuple-element.34.rest_11_), channel_id=1, source_target_pairs={{0,8},{1,9},{2,10},{3,11},{4,12},{5,13},{6,14},{7,15},{8,0},{9,1},... | collective-permute-start | bytes 1179656 | tf_op jit(solution)/shard_map/ppermute | solution.py:287
  55.7 2.4 %collective-permute-start.22 = (bf16[64,512]{1,0:T(8,128)(2,1)S(1)}, bf16[64,512]{1,0:T(8,128)(2,1)S(1)}, u32[]{:S(2)}, u32[]{:S(2)}) collective-permute-start(bf16[64,512]{1,0:T(8,128)(2,1)S(1)} %get-tuple-element.46), channel_id=1, source_target_pairs={{0,1},{1,0},{2,3},{3,2},{4,5},{5,4},{6,7},{7,6},{8,9},{9,8},{10,11... | collective-permute-start | bytes 196616 | tf_op jit(solution)/shard_map/ppermute | solution.py:290
  55.8 8.8 %collective-permute-start.21 = (bf16[64,512]{1,0:T(8,128)(2,1)S(1)}, bf16[64,512]{1,0:T(8,128)(2,1)S(1)}, u32[]{:S(2)}, u32[]{:S(2)}) collective-permute-start(bf16[64,512]{1,0:T(8,128)(2,1)S(1)} %get-tuple-element.47), channel_id=1, source_target_pairs={{0,7},{1,2},{2,1},{3,4},{4,3},{5,6},{6,5},{7,0},{8,9},{9,8},{10,11... | collective-permute-start | bytes 196616 | tf_op jit(solution)/shard_map/ppermute | solution.py:298
  58.1 12.2 %collective-permute-start.15 = (bf16[64,512]{1,0:T(8,128)(2,1)S(1)}, bf16[64,512]{1,0:T(8,128)(2,1)S(1)}, u32[]{:S(2)}, u32[]{:S(2)}) collective-permute-start(bf16[64,512]{1,0:T(8,128)(2,1)S(1)} %get-tuple-element.50), channel_id=1, source_target_pairs={{0,1},{1,0},{2,3},{3,2},{4,5},{5,4},{6,7},{7,6},{8,9},{9,8},{10,11... | collective-permute-start | bytes 196616 | tf_op jit(solution)/shard_map/ppermute | solution.py:290
  58.2 12.2 %collective-permute-start.14 = (bf16[64,512]{1,0:T(8,128)(2,1)S(1)}, bf16[64,512]{1,0:T(8,128)(2,1)S(1)}, u32[]{:S(2)}, u32[]{:S(2)}) collective-permute-start(bf16[64,512]{1,0:T(8,128)(2,1)S(1)} %get-tuple-element.51), channel_id=1, source_target_pairs={{0,7},{1,2},{2,1},{3,4},{4,3},{5,6},{6,5},{7,0},{8,9},{9,8},{10,11... | collective-permute-start | bytes 196616 | tf_op jit(solution)/shard_map/ppermute | solution.py:298
  (2 other events, 23.2 us)

commit v3 on v2

--- a/solution.py
+++ b/solution.py
@@ -9,6 +9,8 @@
 
 HB = 4
 CHUNKS = 2
+CP = 1000
+SPLIT = ((1, 1), (1, 1), (0, 1))
 ROW_TILE = 16
 VMEM = pl.BlockSpec(memory_space=pltpu.VMEM)
 SMEM = pl.BlockSpec(memory_space=pltpu.SMEM)
@@ -46,10 +48,9 @@
     return left, right
 
 
-def source_kernel(row0, thick_ref, layers_ref, total_ref, edge_ref, *rest):
+def source_kernel(row0, halo, thick_ref, layers_ref, total_ref, edge_ref, *rest):
     *mid, buf, sems = rest
     depth, rows, width = buf.shape
-    halo = edge_ref.shape[1] // 2
     thick = thick_ref[0]
 
     def copy(k):
@@ -71,25 +72,28 @@
     edge_ref[:, pl.ds(right, halo)] = value[:, width - halo :]
     if mid:
         mid[0][...] = value[:, halo : width - halo]
-
-
-def fetch_kernel(low, down_ref, up_ref, after_ref, out_ref, sem):
-    del after_ref
-
-    @pl.when(in_low_half() == low)
+    elif width > 2 * halo:
+        edge_ref[:, 2 * halo :] = value[:, halo : width - halo]
+
+
+def fetch_kernel(hops, low, down_ref, up_ref, out_ref, sem):
+    slab, last = lax.axis_index("slab"), lax.axis_size("slab") - 1
+    used = functools.reduce(jnp.logical_or, [(slab == h) | (slab == last - h) for h in hops])
+
+    @pl.when(used & (in_low_half() == low))
     def _():
         copy = pltpu.make_async_copy(down_ref.at[0], out_ref, sem)
         copy.start()
         copy.wait()
 
-    @pl.when(in_low_half() != low)
+    @pl.when(used & (in_low_half() != low))
     def _():
         copy = pltpu.make_async_copy(up_ref.at[0], out_ref, sem)
         copy.start()
         copy.wait()
 
 
-def product_kernel(hop, parts, cols_ref, far_ref, near_ref, *rest):
+def product_kernel(hop, parts, split, cols_ref, far_ref, near_ref, *rest):
     ins, (green_ref, total_ref), outs, ext = (
         rest[:parts],
         rest[parts : parts + 2],
@@ -111,6 +115,8 @@
         ext[:, pl.ds(width, halo)] = ins[0][:, pl.ds(right, halo)]
         if parts == 2:
             ext[:, 2 * halo : width] = ins[1][...]
+        elif width > 2 * halo:
+            ext[:, 2 * halo : width] = ins[0][:, 2 * halo :]
 
         @pl.when(is_even())
         def _():
@@ -141,32 +147,40 @@
             elif at >= width - halo:
                 at = at - (width - halo)
                 outs[0][:, pl.ds(pl.multiple_of(right + at, bsize), bsize)] = value
+            elif split:
+                outs[1][:, at - halo : at - halo + bsize] = value
             else:
-                outs[1][:, at - halo : at - halo + bsize] = value
-
-
-def store_kernel(hops, pieces, parts, *rest):
-    count = len(hops) * len(pieces) * parts
-    ins, (down_ref, up_ref, sems) = rest[:count], rest[-3:]
+                outs[0][:, at + halo : at + halo + bsize] = value
+
+
+def store_kernel(halo, hops, pieces, splits, given, *rest):
+    ins, (down_ref, up_ref, done_ref, sems) = list(rest[: -4 - given]), rest[-4:]
+    done_ref[...] = jnp.zeros_like(done_ref)
     width = down_ref.shape[2]
-    halo = ins[0].shape[1] // 2
     slab = lax.axis_index("slab")
     last = lax.axis_size("slab") - 1
+    traces = {}
+    splits = list(splits)
+    for h in hops:
+        for j in range(len(pieces)):
+            traces[h, j] = [ins.pop(0) for _ in range(1 + splits.pop(0))]
 
     def copies(h, out_ref, which):
         left, right = edge_places(halo)
         made = []
         for j, (row0, rows) in enumerate(pieces):
-            at = (hops.index(h) * len(pieces) + j) * parts
-            span = pl.ds(row0, rows)
+            edge, *mid = traces[h, j]
             moves = [
-                (ins[at].at[:, pl.ds(left, halo)], 0, halo),
-                (ins[at].at[:, pl.ds(right, halo)], width - halo, halo),
+                (edge.at[:, pl.ds(left, halo)], 0, halo),
+                (edge.at[:, pl.ds(right, halo)], width - halo, halo),
             ]
-            if parts == 2:
-                moves.append((ins[at + 1], halo, width - 2 * halo))
+            size = width - 2 * halo
+            if mid:
+                moves.append((mid[0], halo, size))
+            elif size:
+                moves.append((edge.at[:, pl.ds(2 * halo, size)], halo, size))
             for src, col, size in moves:
-                dst = out_ref.at[0, span, pl.ds(col, size)]
+                dst = out_ref.at[0, pl.ds(row0, rows), pl.ds(col, size)]
                 made.append(pltpu.make_async_copy(src, dst, sems.at[which, len(made)]))
         return made
 
@@ -200,74 +214,109 @@
     nblocks = green_down.shape[1]
     halo = HB * bsize
     chunks = chunk_rows(sources)
-    parts = 2 if per_dev > 2 * HB else 1
+
     layers = pinned(layer_sources, pltpu.HBM)
     greens = (pinned(green_down, pltpu.HBM), pinned(green_up, pltpu.HBM))
 
-    def trace(rows):
-        widths = [2 * halo, width - 2 * halo][:parts]
+    def splits(h, j):
+        return int(per_dev > 2 * HB and SPLIT[min(h * 3 // (slabs - 1), 2)][min(j, 1)])
+
+    token = []
+
+    def launch(kernel, ins, in_specs, out_shape, out_specs, scratch, mib, name, aliases=None):
+        count = len(ins)
+        ins, in_specs = [*ins, *token], [*in_specs, *[ANY] * len(token)]
+        given = len(ins)
+
+        def body(*refs):
+            kernel(*refs[:count], *refs[given:])
+
+        out = pl.pallas_call(
+            body,
+            out_shape=out_shape,
+            in_specs=in_specs,
+            out_specs=out_specs,
+            scratch_shapes=scratch,
+            input_output_aliases=aliases or {},
+            compiler_params=params(mib),
+            name=name,
+        )(*ins)
+        token[:] = [out[-1]]
+        return out
+
+    def trace(rows, split):
+        widths = [2 * halo, width - 2 * halo] if split else [width]
         return [pltpu.VMEM((rows, w), jnp.bfloat16) for w in widths]
 
     def local(low):
         cols = jnp.where(in_low_half() == low, column_down, column_up)
         return (cols - lateral * per_dev + HB) % total_blocks
 
-    def fetch(low, after):
-        return pl.pallas_call(
-            functools.partial(fetch_kernel, low),
-            out_shape=pltpu.VMEM(green_down.shape[1:], jnp.bfloat16),
-            in_specs=[HBM, HBM, ANY],
-            out_specs=VMEM,
-            scratch_shapes=[pltpu.SemaphoreType.DMA],
-            compiler_params=params(8),
-            name="fetch",
-        )(*greens, after)
-
-    def source(row0, rows):
-        return pl.pallas_call(
-            functools.partial(source_kernel, row0),
-            out_shape=[pltpu.VMEM((rows, width), jnp.float32), *trace(rows)],
-            in_specs=[SMEM, HBM],
-            out_specs=[VMEM] * (1 + parts),
-            scratch_shapes=[
-                pltpu.VMEM((depth, rows, width), jnp.bfloat16),
-                pltpu.SemaphoreType.DMA((depth,)),
-            ],
-            compiler_params=params(8),
-            name="source",
-        )(thickness, layers)
-
-    def product(h, cols, far, near, got, green, total):
+    def fetch(hops):
+        (block,) = launch(
+            functools.partial(fetch_kernel, hops, hops[0] < slabs // 2),
+            greens,
+            [HBM, HBM],
+            [pltpu.VMEM(green_down.shape[1:], jnp.bfloat16)],
+            [VMEM],
+            [pltpu.SemaphoreType.DMA],
+            8,
+            "fetch",
+        )
+        return block
+
+    def source(j, row0, rows):
+        out_shape = [pltpu.VMEM((rows, width), jnp.float32), *trace(rows, splits(0, j))]
+        total, *out = launch(
+            functools.partial(source_kernel, row0, halo),
+            [thickness, layers],
+            [SMEM, HBM],
+            out_shape,
+            [VMEM] * len(out_shape),
+            [pltpu.VMEM((depth, rows, width), jnp.bfloat16), pltpu.SemaphoreType.DMA((depth,))],
+            8,
+            "source",
+        )
+        return total, *out
+
+    def product(h, j, cols, far, near, got, green, total):
         rows = total.shape[0]
         ins = [pinned(x, pltpu.VMEM) for x in (far, near, *got, green, total)]
-        return pl.pallas_call(
-            functools.partial(product_kernel, h, parts),
-            out_shape=trace(rows),
-            in_specs=[SMEM] + [VMEM] * len(ins),
-            out_specs=[VMEM] * parts,
-            scratch_shapes=[pltpu.VMEM((rows, width + 2 * halo), jnp.bfloat16)],
-            compiler_params=params(8),
-            cost_estimate=pl.CostEstimate(
-                flops=2 * rows * nblocks * bsize * bsize,
-                bytes_accessed=nblocks * bsize * bsize * 2,
-                transcendentals=0,
+        out_shape = trace(rows, splits(h, j))
+        return launch(
+            functools.partial(product_kernel, h, len(got), len(out_shape) == 2),
+            [cols, *ins],
+            [SMEM] + [VMEM] * len(ins),
+            out_shape,
+            [VMEM] * len(out_shape),
+            [pltpu.VMEM((rows, width + 2 * halo), jnp.bfloat16)],
+            8,
+            "product",
+        )
+
+    def store(hops, j0, pieces, arrays, into=()):
+        ins = [pinned(x, pltpu.VMEM) for x in arrays]
+        given = [pinned(x, pltpu.HBM) for x in into]
+        *outs, _ = launch(
+            functools.partial(
+                store_kernel,
+                halo,
+                hops,
+                pieces,
+                [splits(h, j0 + j) for h in hops for j in range(len(pieces))],
+                len(given),
             ),
-            name="product",
-        )(cols, *ins)
-
-    def store(hops, pieces, arrays, into=None):
-        ins = [pinned(x, pltpu.VMEM) for x in arrays]
-        given = [] if into is None else [pinned(x, pltpu.HBM) for x in into]
-        return pl.pallas_call(
-            functools.partial(store_kernel, hops, pieces, parts),
-            out_shape=[pltpu.HBM((1, sources, width), jnp.bfloat16)] * 2,
-            in_specs=[VMEM] * len(ins) + [HBM] * len(given),
-            out_specs=[HBM, HBM],
-            scratch_shapes=[pltpu.SemaphoreType.DMA((2, len(pieces) * (1 + parts)))],
-            input_output_aliases={len(ins) + i: i for i in range(len(given))},
-            compiler_params=params(4),
-            name="store",
-        )(*ins, *given)
+            [*ins, *given],
+            [VMEM] * len(ins) + [HBM] * len(given),
+            [pltpu.HBM((1, sources, width), jnp.bfloat16)] * 2
+            + [pltpu.VMEM((8, 128), jnp.float32)],
+            [HBM, HBM, VMEM],
+            [pltpu.SemaphoreType.DMA((2, len(pieces) * 3))],
+            4,
+            "store",
+            {len(ins) + i: i for i in range(len(given))},
+        )
+        return outs
 
     def mate(c):
         return c ^ 1
@@ -297,9 +346,9 @@
                 route.append((s * cross + c, s * cross + to))
         return lax.ppermute(x, ("slab", "cross"), route)
 
-    totals, made = [], {}
+    totals, made, moved = [], {}, {}
     for j, (row0, rows) in enumerate(chunks):
-        total, *out = source(row0, rows)
+        total, *out = source(j, row0, rows)
         totals.append(total)
         made[0, j] = out
     cols = {low: local(low) for low in (True, False)}
@@ -308,20 +357,44 @@
         ((h, j) for h in range(1, slabs) for j in range(len(chunks))),
         key=lambda hj: (hj[0] + hj[1], hj[0]),
     )
+    early = list(range(slabs - 1))
+    groups = [list(range(1, slabs // 2)), list(range(slabs // 2, slabs - 1)), [slabs - 1]]
+    groups = [g for g in groups if g]
+    group_of = {h: g for g in range(len(groups)) for h in groups[g]}
+    early = list(range(slabs - 1))
+    outs, sides = [], {}
+
+    def lateral(h, j):
+        if (h, j) not in sides:
+            edges = moved[h, j][0][:, : 2 * halo]
+            if h == slabs - 1 and j:
+                edges, _ = lax.optimization_barrier((edges, made[h, j - 1][0]))
+            sides[h, j] = (to_next_chip(edges[:, :halo], h), to_mate(edges[:, halo:]))
+        return sides[h, j]
+
+    def send(h, j):
+        moved[h, j] = [hop(x, h) for x in made[h - 1, j]]
+
+    for j in range(len(chunks)):
+        send(1, j)
     for h, j in order:
-        got = [hop(x, h) for x in made[h - 1, j]]
-        far = to_next_chip(got[0][:, :halo], h)
-        near = to_mate(got[0][:, halo:])
-        low = h < slabs // 2
-        which = (low, h == slabs - 1)
-        if which not in green:
-            green[which] = fetch(low, got[0])
-        made[h, j] = product(h, cols[low], far, near, got, green[which], totals[j])
-
-    early = list(range(slabs - 1))
-    outs = store(early, chunks, [x for h in early for j in range(len(chunks)) for x in made[h, j]])
-    for j, piece in enumerate(chunks):
-        outs = store([slabs - 1], [piece], made[slabs - 1, j], outs)
+        far, near = lateral(h, j)
+        g = group_of[h]
+        for ahead in range(g + 1 + (g + 1 < min(2, len(groups)))):
+            if ahead not in green:
+                green[ahead] = fetch(groups[ahead])
+        if h == slabs - 1 and j == 0:
+            arrays = [x for a in early for b in range(len(chunks)) for x in made[a, b]]
+            outs = store(early, 0, chunks, arrays)
+        made[h, j] = product(
+            h, j, cols[h < slabs // 2], far, near, moved[h, j], green[g], totals[j]
+        )
+        if h < slabs - 1:
+            send(h + 1, j)
+        else:
+            outs = store([h], j, [chunks[j]], made[h, j], outs)
+        if (h, j) == (slabs - 2, 0) and len(groups) - 1 not in green:
+            green[len(groups) - 1] = fetch(groups[-1])
     return tuple(outs)
 
 

time: 77.9 us -> 73.3 us (0.941)
  Pallas kernels: 24.6 us -> 20.1 us
    pallas_call x14, Pallas kernels: 24.6 us -> 20.1 us  [launch(): pl.pallas_call(body, out_shape=out_shape, in_specs=in_specs, out_specs=ou...]
    ppermute x6, starting transfers between devices: 4.39 us -> 0.9 us  [to_next_chip(): return lax.ppermute(x, ('slab', 'cross'), route)]
    ppermute x6, waiting for transfers between devices: 0.33 us -> 3.7 us  [to_next_chip(): return lax.ppermute(x, ('slab', 'cross'), route)]
    ppermute x6, starting transfers between devices: 0.9 us -> 3.55 us  [to_mate(): return lax.ppermute(x, 'cross', [(c, mate(c)) for c in range(cross)])]
    ppermute x12 -> x11, waiting for transfers between devices: 19.1 us -> 17.4 us  [hop(): return lax.ppermute(x, ('slab', 'cross'), route)]
    ppermute x6, waiting for transfers between devices: 1.42 us -> 0.17 us  [to_mate(): return lax.ppermute(x, 'cross', [(c, mate(c)) for c in range(cross)])]
    ppermute x12 -> x11, starting transfers between devices: 25.1 us -> 25.8 us  [hop(): return lax.ppermute(x, ('slab', 'cross'), route)]
  transfers between devices with their start and end apart: 24 -> 23, of which waited for: 10 -> 11; matrix products, arithmetic and copies ran while one was open for 0% -> 0% of each run, Pallas kernels for 24% -> 18%
where the time goes in v3:
time: 73.3 us; the launch traced here: 73.2 us
  starting transfers between devices  30.2 us (41%)
  waiting for transfers between devices  21.2 us (29%)
  Pallas kernels  20.1 us (27%)
  between operations  1.55 us (2%)
    ppermute x11, starting transfers between devices, hop(): return lax.ppermute(x, ('slab', 'cross'), route)  25.8 us
    pallas_call x14, Pallas kernels, launch(): pl.pallas_call(body, out_shape=out_shape, in_specs=in_specs, out_specs=ou...  20.1 us
    ppermute x11, waiting for transfers between devices, hop(): return lax.ppermute(x, ('slab', 'cross'), route)  17.4 us
    ppermute x6, waiting for transfers between devices, to_next_chip(): return lax.ppermute(x, ('slab', 'cross'), route)  3.7 us
    ppermute x6, starting transfers between devices, to_mate(): return lax.ppermute(x, 'cross', [(c, mate(c)) for c in range(cross)])  3.55 us
  transfers between devices with their start and end apart: 23, of which 11 were waited for; matrix products, arithmetic and copies ran while one was open for 0% of the time, Pallas kernels for 18%

profile of v3, /device:TPU:0, one launch (start us, length us, event | category | flops | bytes accessed | tf_op | source)
XLA Modules:
  0.0 73.2 jit_solution(3657114724667438208)
XLA Ops:
  1.3 2.1 %source.2 = (f32[64,4096]{1,0:T(8,128)S(1)}, bf16[64,1024]{1,0:T(8,128)(2,1)}, bf16[64,3072]{1,0:T(8,128)(2,1)S(1)}) custom-call(s32[1]{0:T(128)S(6)} %copy.16.refs_0_, bf16[4,128,4096]{2,1,0:T(8,128)(2,1)} %refs_1_.6), custom_call_target="tpu_custom_call" | custom-call | tf_op jit(solution)/shard_map/source/pallas_call | solution.py:234
  3.5 3.1 %collective-permute-start.4 = (bf16[64,1024]{1,0:T(8,128)(2,1)}, bf16[64,1024]{1,0:T(8,128)(2,1)S(1)}, u32[]{:S(2)}, u32[]{:S(2)}) collective-permute-start(bf16[64,1024]{1,0:T(8,128)(2,1)} %get-tuple-element.29.refs_0_), channel_id=1, source_target_pairs={{0,8},{1,9},{2,10},{3,11},{4,12},{5,13},{6,14},{7,15},{8,0},{9,1},... | collective-permute-start | bytes 393224 | tf_op jit(solution)/shard_map/ppermute | solution.py:336
  6.6 2.1 %source.3 = (f32[64,4096]{1,0:T(8,128)S(1)}, bf16[64,1024]{1,0:T(8,128)(2,1)}, bf16[64,3072]{1,0:T(8,128)(2,1)S(1)}) custom-call(s32[1]{0:T(128)S(6)} %copy.16.refs_0_, bf16[4,128,4096]{2,1,0:T(8,128)(2,1)} %refs_1_.6, bf16[64,3072]{1,0:T(8,128)(2,1)S(1)} %get-tuple-element.25.refs_2_.refs_1_), custom_call_target="tpu_custom_call" | custom-call | tf_op jit(solution)/shard_map/source/pallas_call | solution.py:234
  8.8 2.0 %collective-permute-start = (bf16[64,1024]{1,0:T(8,128)(2,1)}, bf16[64,1024]{1,0:T(8,128)(2,1)S(1)}, u32[]{:S(2)}, u32[]{:S(2)}) collective-permute-start(bf16[64,1024]{1,0:T(8,128)(2,1)} %get-tuple-element.26.refs_2_), channel_id=1, source_target_pairs={{0,8},{1,9},{2,10},{3,11},{4,12},{5,13},{6,14},{7,15},{8,0},{9,1},... | collective-permute-start | bytes 393224 | tf_op jit(solution)/shard_map/ppermute | solution.py:336
  11.8 0.7 collective-permute-done.5.refs_1_
  12.6 6.9 %collective-permute-done.7.refs_4_ = bf16[64,3072]{1,0:T(8,128)(2,1)S(1)} collective-permute-done((bf16[64,3072]{1,0:T(8,128)(2,1)S(1)}, bf16[64,3072]{1,0:T(8,128)(2,1)S(1)}, u32[]{:S(2)}, u32[]{:S(2)}) %collective-permute-start.7) | collective-permute-done | bytes 393248 | tf_op jit(solution)/shard_map/ppermute | solution.py:336
  20.7 1.7 %collective-permute-done.refs_3_ = bf16[64,1024]{1,0:T(8,128)(2,1)S(1)} collective-permute-done((bf16[64,1024]{1,0:T(8,128)(2,1)}, bf16[64,1024]{1,0:T(8,128)(2,1)S(1)}, u32[]{:S(2)}, u32[]{:S(2)}) %collective-permute-start) | collective-permute-done | bytes 131104 | tf_op jit(solution)/shard_map/ppermute | solution.py:336
  23.1 0.6 collective-permute-done.1.refs_1_
  23.8 6.2 %collective-permute-done.3.refs_4_ = bf16[64,3072]{1,0:T(8,128)(2,1)} collective-permute-done((bf16[64,3072]{1,0:T(8,128)(2,1)S(1)}, bf16[64,3072]{1,0:T(8,128)(2,1)}, u32[]{:S(2)}, u32[]{:S(2)}) %collective-permute-start.3) | collective-permute-done | bytes 393248 | tf_op jit(solution)/shard_map/ppermute | solution.py:336
  30.0 1.0 %product.7 = (bf16[64,1024]{1,0:T(8,128)(2,1)S(1)}, bf16[64,3072]{1,0:T(8,128)(2,1)S(1)}) custom-call(s32[1,192]{1,0:T(1,128)S(1)} %get-tuple-element.60.refs_0_, bf16[64,512]{1,0:T(8,128)(2,1)S(1)} %collective-permute-done.1.refs_1_, bf16[64,512]{1,0:T(8,128)(2,1)S(1)} %collective-permute-done.2.refs_2_, bf16[64,1024]{1,0:T(8,128)(2,1)S(1)} %collective-permute-done.refs_3_, ...), custom_call_target="tpu_custom_call" | custom-call | tf_op jit(solution)/shard_map/product/pallas_call | solution.py:234
  31.7 9.0 %collective-permute-start.17 = (bf16[64,4096]{1,0:T(8,128)(2,1)S(1)}, bf16[64,4096]{1,0:T(8,128)(2,1)S(1)}, u32[]{:S(2)}, u32[]{:S(2)}) collective-permute-start(bf16[64,4096]{1,0:T(8,128)(2,1)S(1)} %product.8.refs_2_.refs_8_), channel_id=1, source_target_pairs={{0,8},{1,9},{2,10},{3,11},{4,12},{5,13},{6,14},{7,15},{8,0},{9,1},... | collective-permute-start | bytes 1572872 | tf_op jit(solution)/shard_map/ppermute | solution.py:336
  41.1 0.8 %collective-permute-done.8.refs_3_ = bf16[64,1024]{1,0:T(8,128)(2,1)S(1)} collective-permute-done((bf16[64,1024]{1,0:T(8,128)(2,1)S(1)}, bf16[64,1024]{1,0:T(8,128)(2,1)S(1)}, u32[]{:S(2)}, u32[]{:S(2)}) %collective-permute-start.8) | collective-permute-done | bytes 131104 | tf_op jit(solution)/shard_map/ppermute | solution.py:336
  42.6 2.8 %fetch.5.refs_7_.refs_4_.refs_5_ = bf16[192,128,128]{2,1,0:T(8,128)(2,1)S(1)} custom-call(bf16[1,192,128,128]{3,2,1,0:T(8,128)(2,1)} %refs_0_.7, bf16[1,192,128,128]{3,2,1,0:T(8,128)(2,1)} %refs_1_.9, bf16[64,4096]{1,0:T(8,128)(2,1)S(1)} %product.8.refs_2_.refs_8_), custom_call_target="tpu_custom_call" | custom-call | tf_op jit(solution)/shard_map/fetch/pallas_call | solution.py:234
  46.0 10.4 %collective-permute-start.16 = (bf16[64,1024]{1,0:T(8,128)(2,1)S(1)}, bf16[64,1024]{1,0:T(8,128)(2,1)S(1)}, u32[]{:S(2)}, u32[]{:S(2)}) collective-permute-start(bf16[64,1024]{1,0:T(8,128)(2,1)S(1)} %get-tuple-element.35.refs_9_), channel_id=1, source_target_pairs={{0,8},{1,9},{2,10},{3,11},{4,12},{5,13},{6,14},{7,15},{8,0},{9,1},... | collective-permute-start | bytes 393224 | tf_op jit(solution)/shard_map/ppermute | solution.py:336
  56.5 1.6 %collective-permute-start.19 = (bf16[64,512]{1,0:T(8,128)(2,1)S(1)}, bf16[64,512]{1,0:T(8,128)(2,1)S(1)}, u32[]{:S(2)}, u32[]{:S(2)}) collective-permute-start(bf16[64,512]{1,0:T(8,128)(2,1)S(1)} %get-tuple-element.48), channel_id=1, source_target_pairs={{0,1},{1,0},{2,3},{3,2},{4,5},{5,4},{6,7},{7,6},{8,9},{9,8},{10,11... | collective-permute-start | bytes 196616 | tf_op jit(solution)/shard_map/ppermute | solution.py:339
  58.1 2.0 %store.3 = (bf16[1,128,4096]{2,1,0:T(8,128)(2,1)}, bf16[1,128,4096]{2,1,0:T(8,128)(2,1)}, f32[8,128]{1,0:T(8,128)S(1)}) custom-call(bf16[64,1024]{1,0:T(8,128)(2,1)} %get-tuple-element.29.refs_0_, bf16[64,3072]{1,0:T(8,128)(2,1)S(1)} %get-tuple-element.25.refs_2_.refs_1_, bf16[64,1024]{1,0:T(8,128)(2,1)} %get-tuple-element.26.refs_2_, ...), custom_call_target="tpu_custom_call" | custom-call | tf_op jit(solution)/shard_map/store/pallas_call | solution.py:234
  60.2 0.9 %collective-permute-done.18.refs_1_ = bf16[64,512]{1,0:T(8,128)(2,1)S(1)} collective-permute-done((bf16[64,512]{1,0:T(8,128)(2,1)S(1)}, bf16[64,512]{1,0:T(8,128)(2,1)S(1)}, u32[]{:S(2)}, u32[]{:S(2)}) %collective-permute-start.18) | collective-permute-done | bytes 65568 | tf_op jit(solution)/shard_map/ppermute | solution.py:347
  61.1 3.0 %product.10.refs_0_.refs_3_ = bf16[64,4096]{1,0:T(8,128)(2,1)S(1)} custom-call(s32[1,192]{1,0:T(1,128)S(1)} %get-tuple-element.61.refs_0_, bf16[64,512]{1,0:T(8,128)(2,1)S(1)} %collective-permute-done.18.refs_1_, bf16[64,512]{1,0:T(8,128)(2,1)S(1)} %collective-permute-done.19.refs_2_, bf16[64,4096]{1,0:T(8,128)(2,1)S(1)} %collective-permute-done.17.refs_3_, ...), custom_call_target="tpu_custom_call" | custom-call | tf_op jit(solution)/shard_map/product/pallas_call | solution.py:234
  64.3 0.6 collective-permute-start.21
  64.9 0.8 %store.4 = (bf16[1,128,4096]{2,1,0:T(8,128)(2,1)}, bf16[1,128,4096]{2,1,0:T(8,128)(2,1)}, f32[8,128]{1,0:T(8,128)S(1)}) custom-call(bf16[64,4096]{1,0:T(8,128)(2,1)S(1)} %product.10.refs_0_.refs_3_, bf16[1,128,4096]{2,1,0:T(8,128)(2,1)} %get-tuple-element.39.refs_1_, ...), custom_call_target="tpu_custom_call", output_to_operand_aliasing={{0}: (1, {}), {1}: (2, {})} | custom-call | tf_op jit(solution)/shard_map/store/pallas_call | solution.py:234
  65.7 1.5 %collective-permute-done.22.refs_4_ = bf16[64,3072]{1,0:T(8,128)(2,1)S(1)} collective-permute-done((bf16[64,3072]{1,0:T(8,128)(2,1)S(1)}, bf16[64,3072]{1,0:T(8,128)(2,1)S(1)}, u32[]{:S(2)}, u32[]{:S(2)}) %collective-permute-start.22) | collective-permute-done | bytes 393248 | tf_op jit(solution)/shard_map/ppermute | solution.py:336
  67.2 1.5 %collective-permute-done.20.refs_1_ = bf16[64,512]{1,0:T(8,128)(2,1)S(1)} collective-permute-done((bf16[64,512]{1,0:T(8,128)(2,1)S(1)}, bf16[64,512]{1,0:T(8,128)(2,1)S(1)}, u32[]{:S(2)}, u32[]{:S(2)}) %collective-permute-start.20) | collective-permute-done | bytes 65568 | tf_op jit(solution)/shard_map/ppermute | solution.py:347
  68.8 2.9 %product.11 = (bf16[64,1024]{1,0:T(8,128)(2,1)S(1)}, bf16[64,3072]{1,0:T(8,128)(2,1)S(1)}) custom-call(s32[1,192]{1,0:T(1,128)S(1)} %get-tuple-element.61.refs_0_, bf16[64,512]{1,0:T(8,128)(2,1)S(1)} %collective-permute-done.20.refs_1_, bf16[64,512]{1,0:T(8,128)(2,1)S(1)} %collective-permute-done.21.refs_2_, ...), custom_call_target="tpu_custom_call" | custom-call | tf_op jit(solution)/shard_map/product/pallas_call | solution.py:234
  71.7 1.5 %store.5 = (bf16[1,128,4096]{2,1,0:T(8,128)(2,1)}, bf16[1,128,4096]{2,1,0:T(8,128)(2,1)}, f32[8,128]{1,0:T(8,128)}) custom-call(bf16[64,1024]{1,0:T(8,128)(2,1)S(1)} %get-tuple-element.42.refs_0_, bf16[64,3072]{1,0:T(8,128)(2,1)S(1)} %get-tuple-element.43.refs_1_.refs_4_, ...), custom_call_target="tpu_custom_call", output_to_operand_aliasing={{0}: (2, {}), {1}: (3, {})} | custom-call | tf_op jit(solution)/shard_map/store/pallas_call | solution.py:234
  (47 shorter events, 5.8 us)
Async XLA Ops:
  0.6 11.1 %copy-start.1 = (s32[1,192]{1,0:T(1,128)S(1)}, s32[1,192]{1,0:T(1,128)}, u32[]{:S(2)}) copy-start(s32[1,192]{1,0:T(1,128)} %param.11) | copy-start | bytes 2308
  3.5 7.6 %collective-permute-start.4 = (bf16[64,1024]{1,0:T(8,128)(2,1)}, bf16[64,1024]{1,0:T(8,128)(2,1)S(1)}, u32[]{:S(2)}, u32[]{:S(2)}) collective-permute-start(bf16[64,1024]{1,0:T(8,128)(2,1)} %get-tuple-element.29.refs_0_), channel_id=1, source_target_pairs={{0,8},{1,9},{2,10},{3,11},{4,12},{5,13},{6,14},{7,15},{8,0},{9,1},... | collective-permute-start | bytes 393224 | tf_op jit(solution)/shard_map/ppermute | solution.py:336
  6.6 13.0 %collective-permute-start.7 = (bf16[64,3072]{1,0:T(8,128)(2,1)S(1)}, bf16[64,3072]{1,0:T(8,128)(2,1)S(1)}, u32[]{:S(2)}, u32[]{:S(2)}) collective-permute-start(bf16[64,3072]{1,0:T(8,128)(2,1)S(1)} %get-tuple-element.25.refs_2_.refs_1_), channel_id=1, source_target_pairs={{0,8},{1,9},{2,10},{3,11},{4,12},{5,13},{6,14},{7,15},{8,0},{9,1},... | collective-permute-start | bytes 1179656 | tf_op jit(solution)/shard_map/ppermute | solution.py:336
  8.8 13.5 %collective-permute-start = (bf16[64,1024]{1,0:T(8,128)(2,1)}, bf16[64,1024]{1,0:T(8,128)(2,1)S(1)}, u32[]{:S(2)}, u32[]{:S(2)}) collective-permute-start(bf16[64,1024]{1,0:T(8,128)(2,1)} %get-tuple-element.26.refs_2_), channel_id=1, source_target_pairs={{0,8},{1,9},{2,10},{3,11},{4,12},{5,13},{6,14},{7,15},{8,0},{9,1},... | collective-permute-start | bytes 393224 | tf_op jit(solution)/shard_map/ppermute | solution.py:336
  10.8 19.2 %collective-permute-start.3 = (bf16[64,3072]{1,0:T(8,128)(2,1)S(1)}, bf16[64,3072]{1,0:T(8,128)(2,1)}, u32[]{:S(2)}, u32[]{:S(2)}) collective-permute-start(bf16[64,3072]{1,0:T(8,128)(2,1)S(1)} %get-tuple-element.27.refs_2_.refs_3_), channel_id=1, source_target_pairs={{0,8},{1,9},{2,10},{3,11},{4,12},{5,13},{6,14},{7,15},{8,0},{9,1},... | collective-permute-start | bytes 1179656 | tf_op jit(solution)/shard_map/ppermute | solution.py:336
  11.1 1.3 %collective-permute-start.5 = (bf16[64,512]{1,0:T(8,128)(2,1)S(1)}, bf16[64,512]{1,0:T(8,128)(2,1)S(1)}, u32[]{:S(2)}, u32[]{:S(2)}) collective-permute-start(bf16[64,512]{1,0:T(8,128)(2,1)S(1)} %get-tuple-element.57), channel_id=1, source_target_pairs={{0,1},{1,0},{2,3},{3,2},{4,5},{5,4},{6,7},{7,6},{8,15},{9,10},{10,... | collective-permute-start | bytes 196616 | tf_op jit(solution)/shard_map/ppermute | solution.py:347
  11.2 1.4 %collective-permute-start.6 = (bf16[64,512]{1,0:T(8,128)(2,1)S(1)}, bf16[64,512]{1,0:T(8,128)(2,1)S(1)}, u32[]{:S(2)}, u32[]{:S(2)}) collective-permute-start(bf16[64,512]{1,0:T(8,128)(2,1)S(1)} %get-tuple-element.56), channel_id=1, source_target_pairs={{0,1},{1,0},{2,3},{3,2},{4,5},{5,4},{6,7},{7,6},{8,9},{9,8},{10,11... | collective-permute-start | bytes 196616 | tf_op jit(solution)/shard_map/ppermute | solution.py:339
  20.1 2.8 %collective-permute-start.12 = (bf16[64,1024]{1,0:T(8,128)(2,1)S(1)}, bf16[64,1024]{1,0:T(8,128)(2,1)S(1)}, u32[]{:S(2)}, u32[]{:S(2)}) collective-permute-start(bf16[64,1024]{1,0:T(8,128)(2,1)S(1)} %get-tuple-element.34.refs_4_), channel_id=1, source_target_pairs={{0,1},{1,0},{2,3},{3,2},{4,5},{5,4},{6,7},{7,6},{8,16},{9,17},{10,... | collective-permute-start | bytes 393224 | tf_op jit(solution)/shard_map/ppermute | solution.py:336
  20.2 10.9 %collective-permute-start.15 = (bf16[64,3072]{1,0:T(8,128)(2,1)S(1)}, bf16[64,3072]{1,0:T(8,128)(2,1)S(1)}, u32[]{:S(2)}, u32[]{:S(2)}) collective-permute-start(bf16[64,3072]{1,0:T(8,128)(2,1)S(1)} %get-tuple-element.31.refs_7_.refs_5_), channel_id=1, source_target_pairs={{0,1},{1,0},{2,3},{3,2},{4,5},{5,4},{6,7},{7,6},{8,16},{9,17},{10,... | collective-permute-start | bytes 1179656 | tf_op jit(solution)/shard_map/ppermute | solution.py:336
  22.3 1.3 %collective-permute-start.1 = (bf16[64,512]{1,0:T(8,128)(2,1)S(1)}, bf16[64,512]{1,0:T(8,128)(2,1)S(1)}, u32[]{:S(2)}, u32[]{:S(2)}) collective-permute-start(bf16[64,512]{1,0:T(8,128)(2,1)S(1)} %get-tuple-element.59), channel_id=1, source_target_pairs={{0,1},{1,0},{2,3},{3,2},{4,5},{5,4},{6,7},{7,6},{8,15},{9,10},{10,... | collective-permute-start | bytes 196616 | tf_op jit(solution)/shard_map/ppermute | solution.py:347
  22.4 1.4 %collective-permute-start.2 = (bf16[64,512]{1,0:T(8,128)(2,1)S(1)}, bf16[64,512]{1,0:T(8,128)(2,1)S(1)}, u32[]{:S(2)}, u32[]{:S(2)}) collective-permute-start(bf16[64,512]{1,0:T(8,128)(2,1)S(1)} %get-tuple-element.58), channel_id=1, source_target_pairs={{0,1},{1,0},{2,3},{3,2},{4,5},{5,4},{6,7},{7,6},{8,9},{9,8},{10,11... | collective-permute-start | bytes 196616 | tf_op jit(solution)/shard_map/ppermute | solution.py:339
  22.9 8.1 %collective-permute-start.13 = (bf16[64,512]{1,0:T(8,128)(2,1)S(1)}, bf16[64,512]{1,0:T(8,128)(2,1)S(1)}, u32[]{:S(2)}, u32[]{:S(2)}) collective-permute-start(bf16[64,512]{1,0:T(8,128)(2,1)S(1)} %get-tuple-element.53), channel_id=1, source_target_pairs={{0,1},{1,0},{2,3},{3,2},{4,5},{5,4},{6,7},{7,6},{8,15},{9,10},{10,... | collective-permute-start | bytes 196616 | tf_op jit(solution)/shard_map/ppermute | solution.py:347
  23.7 7.4 %collective-permute-start.14 = (bf16[64,512]{1,0:T(8,128)(2,1)S(1)}, bf16[64,512]{1,0:T(8,128)(2,1)S(1)}, u32[]{:S(2)}, u32[]{:S(2)}) collective-permute-start(bf16[64,512]{1,0:T(8,128)(2,1)S(1)} %get-tuple-element.52), channel_id=1, source_target_pairs={{0,1},{1,0},{2,3},{3,2},{4,5},{5,4},{6,7},{7,6},{8,9},{9,8},{10,11... | collective-permute-start | bytes 196616 | tf_op jit(solution)/shard_map/ppermute | solution.py:339
  31.7 24.8 %collective-permute-start.17 = (bf16[64,4096]{1,0:T(8,128)(2,1)S(1)}, bf16[64,4096]{1,0:T(8,128)(2,1)S(1)}, u32[]{:S(2)}, u32[]{:S(2)}) collective-permute-start(bf16[64,4096]{1,0:T(8,128)(2,1)S(1)} %product.8.refs_2_.refs_8_), channel_id=1, source_target_pairs={{0,8},{1,9},{2,10},{3,11},{4,12},{5,13},{6,14},{7,15},{8,0},{9,1},... | collective-permute-start | bytes 1572872 | tf_op jit(solution)/shard_map/ppermute | solution.py:336
  40.6 1.3 %collective-permute-start.8 = (bf16[64,1024]{1,0:T(8,128)(2,1)S(1)}, bf16[64,1024]{1,0:T(8,128)(2,1)S(1)}, u32[]{:S(2)}, u32[]{:S(2)}) collective-permute-start(bf16[64,1024]{1,0:T(8,128)(2,1)S(1)} %get-tuple-element.32.refs_6_), channel_id=1, source_target_pairs={{0,1},{1,0},{2,3},{3,2},{4,5},{5,4},{6,7},{7,6},{8,16},{9,17},{10,... | collective-permute-start | bytes 393224 | tf_op jit(solution)/shard_map/ppermute | solution.py:336
  40.6 4.8 %collective-permute-start.11 = (bf16[64,3072]{1,0:T(8,128)(2,1)S(1)}, bf16[64,3072]{1,0:T(8,128)(2,1)S(1)}, u32[]{:S(2)}, u32[]{:S(2)}) collective-permute-start(bf16[64,3072]{1,0:T(8,128)(2,1)S(1)} %get-tuple-element.33.refs_7_), channel_id=1, source_target_pairs={{0,1},{1,0},{2,3},{3,2},{4,5},{5,4},{6,7},{7,6},{8,16},{9,17},{10,... | collective-permute-start | bytes 1179656 | tf_op jit(solution)/shard_map/ppermute | solution.py:336
  42.0 3.4 %collective-permute-start.10 = (bf16[64,512]{1,0:T(8,128)(2,1)S(1)}, bf16[64,512]{1,0:T(8,128)(2,1)S(1)}, u32[]{:S(2)}, u32[]{:S(2)}) collective-permute-start(bf16[64,512]{1,0:T(8,128)(2,1)S(1)} %get-tuple-element.54), channel_id=1, source_target_pairs={{0,1},{1,0},{2,3},{3,2},{4,5},{5,4},{6,7},{7,6},{8,9},{9,8},{10,11... | collective-permute-start | bytes 196616 | tf_op jit(solution)/shard_map/ppermute | solution.py:339
  42.2 3.2 %collective-permute-start.9 = (bf16[64,512]{1,0:T(8,128)(2,1)S(1)}, bf16[64,512]{1,0:T(8,128)(2,1)S(1)}, u32[]{:S(2)}, u32[]{:S(2)}) collective-permute-start(bf16[64,512]{1,0:T(8,128)(2,1)S(1)} %get-tuple-element.55), channel_id=1, source_target_pairs={{0,1},{1,0},{2,3},{3,2},{4,5},{5,4},{6,7},{7,6},{8,15},{9,10},{10,... | collective-permute-start | bytes 196616 | tf_op jit(solution)/shard_map/ppermute | solution.py:347
  46.0 18.1 %collective-permute-start.16 = (bf16[64,1024]{1,0:T(8,128)(2,1)S(1)}, bf16[64,1024]{1,0:T(8,128)(2,1)S(1)}, u32[]{:S(2)}, u32[]{:S(2)}) collective-permute-start(bf16[64,1024]{1,0:T(8,128)(2,1)S(1)} %get-tuple-element.35.refs_9_), channel_id=1, source_target_pairs={{0,8},{1,9},{2,10},{3,11},{4,12},{5,13},{6,14},{7,15},{8,0},{9,1},... | collective-permute-start | bytes 393224 | tf_op jit(solution)/shard_map/ppermute | solution.py:336
  56.3 10.9 %collective-permute-start.22 = (bf16[64,3072]{1,0:T(8,128)(2,1)S(1)}, bf16[64,3072]{1,0:T(8,128)(2,1)S(1)}, u32[]{:S(2)}, u32[]{:S(2)}) collective-permute-start(bf16[64,3072]{1,0:T(8,128)(2,1)S(1)} %get-tuple-element.36.refs_10_.refs_11_), channel_id=1, source_target_pairs={{0,8},{1,9},{2,10},{3,11},{4,12},{5,13},{6,14},{7,15},{8,0},{9,1},... | collective-permute-start | bytes 1179656 | tf_op jit(solution)/shard_map/ppermute | solution.py:336
  56.4 4.7 %collective-permute-start.18 = (bf16[64,512]{1,0:T(8,128)(2,1)S(1)}, bf16[64,512]{1,0:T(8,128)(2,1)S(1)}, u32[]{:S(2)}, u32[]{:S(2)}) collective-permute-start(bf16[64,512]{1,0:T(8,128)(2,1)S(1)} %get-tuple-element.49), channel_id=1, source_target_pairs={{0,7},{1,2},{2,1},{3,4},{4,3},{5,6},{6,5},{7,0},{8,9},{9,8},{10,11... | collective-permute-start | bytes 196616 | tf_op jit(solution)/shard_map/ppermute | solution.py:347
  56.5 4.6 %collective-permute-start.19 = (bf16[64,512]{1,0:T(8,128)(2,1)S(1)}, bf16[64,512]{1,0:T(8,128)(2,1)S(1)}, u32[]{:S(2)}, u32[]{:S(2)}) collective-permute-start(bf16[64,512]{1,0:T(8,128)(2,1)S(1)} %get-tuple-element.48), channel_id=1, source_target_pairs={{0,1},{1,0},{2,3},{3,2},{4,5},{5,4},{6,7},{7,6},{8,9},{9,8},{10,11... | collective-permute-start | bytes 196616 | tf_op jit(solution)/shard_map/ppermute | solution.py:339
  64.1 4.7 %collective-permute-start.20 = (bf16[64,512]{1,0:T(8,128)(2,1)S(1)}, bf16[64,512]{1,0:T(8,128)(2,1)S(1)}, u32[]{:S(2)}, u32[]{:S(2)}) collective-permute-start(bf16[64,512]{1,0:T(8,128)(2,1)S(1)} %get-tuple-element.51), channel_id=1, source_target_pairs={{0,7},{1,2},{2,1},{3,4},{4,3},{5,6},{6,5},{7,0},{8,9},{9,8},{10,11... | collective-permute-start | bytes 196616 | tf_op jit(solution)/shard_map/ppermute | solution.py:347
  64.3 4.5 %collective-permute-start.21 = (bf16[64,512]{1,0:T(8,128)(2,1)S(1)}, bf16[64,512]{1,0:T(8,128)(2,1)S(1)}, u32[]{:S(2)}, u32[]{:S(2)}) collective-permute-start(bf16[64,512]{1,0:T(8,128)(2,1)S(1)} %get-tuple-element.50), channel_id=1, source_target_pairs={{0,1},{1,0},{2,3},{3,2},{4,5},{5,4},{6,7},{7,6},{8,9},{9,8},{10,11... | collective-permute-start | bytes 196616 | tf_op jit(solution)/shard_map/ppermute | solution.py:339
  (1 other events, 11.0 us)

commit v4 on v3

--- a/solution.py
+++ b/solution.py
@@ -93,7 +93,36 @@
         copy.wait()
 
 
-def product_kernel(hop, parts, split, cols_ref, far_ref, near_ref, *rest):
+def last_product_kernel(hop, parts, row0, cols_ref, far_ref, near_ref, *rest):
+    ins = rest[: parts + 2]
+    down_ref, up_ref, done_ref, ext, held, sems = rest[parts + 4 :]
+    rows, width = held.shape
+    count = sems.shape[1]
+    size = width // count
+    goes_down = lax.axis_index("slab") == hop
+    goes_up = lax.axis_index("slab") == lax.axis_size("slab") - 1 - hop
+    done_ref[...] = jnp.zeros_like(done_ref)
+
+    def copy(ref, which, n):
+        span = pl.ds(n * size, size)
+        return pltpu.make_async_copy(
+            held.at[:, span], ref.at[0, pl.ds(row0, rows), span], sems.at[which, n]
+        )
+
+    def emit(at, value):
+        held[:, at : at + value.shape[1]] = value
+        n, part = divmod(at + value.shape[1], size)
+        if part == 0:
+            pl.when(goes_down)(copy(down_ref, 0, n - 1).start)
+            pl.when(goes_up)(copy(up_ref, 1, n - 1).start)
+
+    product_kernel(hop, parts, False, cols_ref, far_ref, near_ref, *ins, ext, emit=emit)
+    for n in range(count):
+        pl.when(goes_down)(copy(down_ref, 0, n).wait)
+        pl.when(goes_up)(copy(up_ref, 1, n).wait)
+
+
+def product_kernel(hop, parts, split, cols_ref, far_ref, near_ref, *rest, emit=None):
     ins, (green_ref, total_ref), outs, ext = (
         rest[:parts],
         rest[parts : parts + 2],
@@ -142,7 +171,9 @@
             )
             value = (value + total_ref[:, i * bsize : (i + 1) * bsize]).astype(jnp.bfloat16)
             at = i * bsize
-            if at < halo:
+            if emit:
+                emit(at, value)
+            elif at < halo:
                 outs[0][:, pl.ds(pl.multiple_of(left + at, bsize), bsize)] = value
             elif at >= width - halo:
                 at = at - (width - halo)
@@ -293,6 +324,27 @@
             8,
             "product",
         )
+
+    def last_product(j, cols, far, near, got, green, total, into):
+        rows = total.shape[0]
+        ins = [pinned(x, pltpu.VMEM) for x in (far, near, *got, green, total)]
+        pieces = 4 if per_dev % 4 == 0 else 1
+        return launch(
+            functools.partial(last_product_kernel, slabs - 1, len(got), chunks[j][0]),
+            [cols, *ins, *[pinned(x, pltpu.HBM) for x in into]],
+            [SMEM] + [VMEM] * len(ins) + [HBM] * 2,
+            [pltpu.HBM((1, sources, width), jnp.bfloat16)] * 2
+            + [pltpu.VMEM((8, 128), jnp.float32)],
+            [HBM, HBM, VMEM],
+            [
+                pltpu.VMEM((rows, width + 2 * halo), jnp.bfloat16),
+                pltpu.VMEM((rows, width), jnp.bfloat16),
+                pltpu.SemaphoreType.DMA((2, pieces)),
+            ],
+            8,
+            "product",
+            {len(ins) + 1: 0, len(ins) + 2: 1},
+        )[:2]
 
     def store(hops, j0, pieces, arrays, into=()):
         ins = [pinned(x, pltpu.VMEM) for x in arrays]
@@ -368,7 +420,7 @@
         if (h, j) not in sides:
             edges = moved[h, j][0][:, : 2 * halo]
             if h == slabs - 1 and j:
-                edges, _ = lax.optimization_barrier((edges, made[h, j - 1][0]))
+                edges, _ = lax.optimization_barrier((edges, sides[h, j - 1][0]))
             sides[h, j] = (to_next_chip(edges[:, :halo], h), to_mate(edges[:, halo:]))
         return sides[h, j]
 
@@ -386,13 +438,12 @@
         if h == slabs - 1 and j == 0:
             arrays = [x for a in early for b in range(len(chunks)) for x in made[a, b]]
             outs = store(early, 0, chunks, arrays)
-        made[h, j] = product(
-            h, j, cols[h < slabs // 2], far, near, moved[h, j], green[g], totals[j]
-        )
-        if h < slabs - 1:
+        given = (cols[h < slabs // 2], far, near, moved[h, j], green[g], totals[j])
+        if h == slabs - 1:
+            outs = last_product(j, *given, outs)
+        else:
+            made[h, j] = product(h, j, *given)
             send(h + 1, j)
-        else:
-            outs = store([h], j, [chunks[j]], made[h, j], outs)
         if (h, j) == (slabs - 2, 0) and len(groups) - 1 not in green:
             green[len(groups) - 1] = fetch(groups[-1])
     return tuple(outs)

time: 73.3 us -> 72.7 us (level)
  waiting for transfers between devices: 21.2 us -> 20.1 us
  starting transfers between devices: 30.2 us -> 31.1 us
    ppermute x6, waiting for transfers between devices: 3.7 us -> 1.73 us  [to_next_chip(): return lax.ppermute(x, ('slab', 'cross'), route)]
    ppermute x11, waiting for transfers between devices: 17.4 us -> 18.2 us  [hop(): return lax.ppermute(x, ('slab', 'cross'), route)]
    pallas_call x14 -> x12, Pallas kernels: 20.1 us -> 19.5 us  [launch(): pl.pallas_call(body, out_shape=out_shape, in_specs=in_specs, out_specs=ou...]
  transfers between devices with their start and end apart: 23 -> 23, of which waited for: 11 -> 10; matrix products, arithmetic and copies ran while one was open for 0% -> 0% of each run, Pallas kernels for 18% -> 18%
where the time goes in v4:
time: 72.7 us; the launch traced here: 72.4 us
  starting transfers between devices  31.1 us (43%)
  waiting for transfers between devices  20.1 us (28%)
  Pallas kernels  19.5 us (27%)
  between operations  1.56 us (2%)
    ppermute x11, starting transfers between devices, hop(): return lax.ppermute(x, ('slab', 'cross'), route)  26.2 us
    pallas_call x12, Pallas kernels, launch(): pl.pallas_call(body, out_shape=out_shape, in_specs=in_specs, out_specs=ou...  19.5 us
    ppermute x11, waiting for transfers between devices, hop(): return lax.ppermute(x, ('slab', 'cross'), route)  18.2 us
    ppermute x6, starting transfers between devices, to_mate(): return lax.ppermute(x, 'cross', [(c, mate(c)) for c in range(cross)])  4.18 us
    ppermute x6, waiting for transfers between devices, to_next_chip(): return lax.ppermute(x, ('slab', 'cross'), route)  1.73 us
  transfers between devices with their start and end apart: 23, of which 10 were waited for; matrix products, arithmetic and copies ran while one was open for 0% of the time, Pallas kernels for 18%

profile of v4, /device:TPU:0, one launch (start us, length us, event | category | flops | bytes accessed | tf_op | source)
XLA Modules:
  0.0 72.4 jit_solution(8616322557277930263)
XLA Ops:
  1.3 2.0 %source.2 = (f32[64,4096]{1,0:T(8,128)S(1)}, bf16[64,1024]{1,0:T(8,128)(2,1)}, bf16[64,3072]{1,0:T(8,128)(2,1)S(1)}) custom-call(s32[1]{0:T(128)S(6)} %copy.16.refs_0_, bf16[4,128,4096]{2,1,0:T(8,128)(2,1)} %refs_1_.6), custom_call_target="tpu_custom_call" | custom-call | tf_op jit(solution)/shard_map/source/pallas_call | solution.py:265
  3.3 3.4 %collective-permute-start.4 = (bf16[64,1024]{1,0:T(8,128)(2,1)}, bf16[64,1024]{1,0:T(8,128)(2,1)S(1)}, u32[]{:S(2)}, u32[]{:S(2)}) collective-permute-start(bf16[64,1024]{1,0:T(8,128)(2,1)} %get-tuple-element.27.refs_0_), channel_id=1, source_target_pairs={{0,8},{1,9},{2,10},{3,11},{4,12},{5,13},{6,14},{7,15},{8,0},{9,1},... | collective-permute-start | bytes 393224 | tf_op jit(solution)/shard_map/ppermute | solution.py:388
  6.8 2.0 %source.3 = (f32[64,4096]{1,0:T(8,128)S(1)}, bf16[64,1024]{1,0:T(8,128)(2,1)}, bf16[64,3072]{1,0:T(8,128)(2,1)S(1)}) custom-call(s32[1]{0:T(128)S(6)} %copy.16.refs_0_, bf16[4,128,4096]{2,1,0:T(8,128)(2,1)} %refs_1_.6, bf16[64,3072]{1,0:T(8,128)(2,1)S(1)} %get-tuple-element.23.refs_2_.refs_1_), custom_call_target="tpu_custom_call" | custom-call | tf_op jit(solution)/shard_map/source/pallas_call | solution.py:265
  8.8 2.3 %collective-permute-start = (bf16[64,1024]{1,0:T(8,128)(2,1)}, bf16[64,1024]{1,0:T(8,128)(2,1)S(1)}, u32[]{:S(2)}, u32[]{:S(2)}) collective-permute-start(bf16[64,1024]{1,0:T(8,128)(2,1)} %get-tuple-element.24.refs_2_), channel_id=1, source_target_pairs={{0,8},{1,9},{2,10},{3,11},{4,12},{5,13},{6,14},{7,15},{8,0},{9,1},... | collective-permute-start | bytes 393224 | tf_op jit(solution)/shard_map/ppermute | solution.py:388
  11.9 0.7 collective-permute-done.5.refs_1_
  12.7 6.9 %collective-permute-done.7.refs_4_ = bf16[64,3072]{1,0:T(8,128)(2,1)S(1)} collective-permute-done((bf16[64,3072]{1,0:T(8,128)(2,1)S(1)}, bf16[64,3072]{1,0:T(8,128)(2,1)S(1)}, u32[]{:S(2)}, u32[]{:S(2)}) %collective-permute-start.7) | collective-permute-done | bytes 393248 | tf_op jit(solution)/shard_map/ppermute | solution.py:388
  19.7 0.6 product.6
  20.8 1.7 %collective-permute-done.refs_3_ = bf16[64,1024]{1,0:T(8,128)(2,1)S(1)} collective-permute-done((bf16[64,1024]{1,0:T(8,128)(2,1)}, bf16[64,1024]{1,0:T(8,128)(2,1)S(1)}, u32[]{:S(2)}, u32[]{:S(2)}) %collective-permute-start) | collective-permute-done | bytes 131104 | tf_op jit(solution)/shard_map/ppermute | solution.py:388
  23.2 0.6 collective-permute-done.1.refs_1_
  24.0 6.2 %collective-permute-done.3.refs_4_ = bf16[64,3072]{1,0:T(8,128)(2,1)} collective-permute-done((bf16[64,3072]{1,0:T(8,128)(2,1)S(1)}, bf16[64,3072]{1,0:T(8,128)(2,1)}, u32[]{:S(2)}, u32[]{:S(2)}) %collective-permute-start.3) | collective-permute-done | bytes 393248 | tf_op jit(solution)/shard_map/ppermute | solution.py:388
  30.2 1.0 %product.7 = (bf16[64,1024]{1,0:T(8,128)(2,1)S(1)}, bf16[64,3072]{1,0:T(8,128)(2,1)S(1)}) custom-call(s32[1,192]{1,0:T(1,128)S(1)} %get-tuple-element.56.refs_0_, bf16[64,512]{1,0:T(8,128)(2,1)S(1)} %collective-permute-done.1.refs_1_, bf16[64,512]{1,0:T(8,128)(2,1)S(1)} %collective-permute-done.2.refs_2_, bf16[64,1024]{1,0:T(8,128)(2,1)S(1)} %collective-permute-done.refs_3_, ...), custom_call_target="tpu_custom_call" | custom-call | tf_op jit(solution)/shard_map/product/pallas_call | solution.py:265
  31.2 0.6 product.8.refs_2_.refs_8_
  31.8 8.7 %collective-permute-start.17 = (bf16[64,4096]{1,0:T(8,128)(2,1)S(1)}, bf16[64,4096]{1,0:T(8,128)(2,1)S(1)}, u32[]{:S(2)}, u32[]{:S(2)}) collective-permute-start(bf16[64,4096]{1,0:T(8,128)(2,1)S(1)} %product.8.refs_2_.refs_8_), channel_id=1, source_target_pairs={{0,8},{1,9},{2,10},{3,11},{4,12},{5,13},{6,14},{7,15},{8,0},{9,1},... | collective-permute-start | bytes 1572872 | tf_op jit(solution)/shard_map/ppermute | solution.py:388
  40.6 0.5 collective-permute-start.11
  41.1 0.8 %collective-permute-done.8.refs_3_ = bf16[64,1024]{1,0:T(8,128)(2,1)S(1)} collective-permute-done((bf16[64,1024]{1,0:T(8,128)(2,1)S(1)}, bf16[64,1024]{1,0:T(8,128)(2,1)S(1)}, u32[]{:S(2)}, u32[]{:S(2)}) %collective-permute-start.8) | collective-permute-done | bytes 131104 | tf_op jit(solution)/shard_map/ppermute | solution.py:388
  42.5 2.8 %fetch.5.refs_7_.refs_4_.refs_5_ = bf16[192,128,128]{2,1,0:T(8,128)(2,1)S(1)} custom-call(bf16[1,192,128,128]{3,2,1,0:T(8,128)(2,1)} %refs_0_.7, bf16[1,192,128,128]{3,2,1,0:T(8,128)(2,1)} %refs_1_.9, bf16[64,4096]{1,0:T(8,128)(2,1)S(1)} %product.8.refs_2_.refs_8_), custom_call_target="tpu_custom_call" | custom-call | tf_op jit(solution)/shard_map/fetch/pallas_call | solution.py:265
  45.3 0.6 product.9
  45.9 10.4 %collective-permute-start.16 = (bf16[64,1024]{1,0:T(8,128)(2,1)S(1)}, bf16[64,1024]{1,0:T(8,128)(2,1)S(1)}, u32[]{:S(2)}, u32[]{:S(2)}) collective-permute-start(bf16[64,1024]{1,0:T(8,128)(2,1)S(1)} %get-tuple-element.33.refs_9_), channel_id=1, source_target_pairs={{0,8},{1,9},{2,10},{3,11},{4,12},{5,13},{6,14},{7,15},{8,0},{9,1},... | collective-permute-start | bytes 393224 | tf_op jit(solution)/shard_map/ppermute | solution.py:388
  56.5 1.6 %collective-permute-start.22 = (bf16[64,512]{1,0:T(8,128)(2,1)S(1)}, bf16[64,512]{1,0:T(8,128)(2,1)S(1)}, u32[]{:S(2)}, u32[]{:S(2)}) collective-permute-start(bf16[64,512]{1,0:T(8,128)(2,1)S(1)} %get-tuple-element.44), channel_id=1, source_target_pairs={{0,1},{1,0},{2,3},{3,2},{4,5},{5,4},{6,7},{7,6},{8,9},{9,8},{10,11... | collective-permute-start | bytes 196616 | tf_op jit(solution)/shard_map/ppermute | solution.py:391
  58.1 2.5 %collective-permute-done.16.refs_3_ = bf16[64,1024]{1,0:T(8,128)(2,1)S(1)} collective-permute-done((bf16[64,1024]{1,0:T(8,128)(2,1)S(1)}, bf16[64,1024]{1,0:T(8,128)(2,1)S(1)}, u32[]{:S(2)}, u32[]{:S(2)}) %collective-permute-start.16) | collective-permute-done | bytes 131104 | tf_op jit(solution)/shard_map/ppermute | solution.py:388
  61.1 1.2 %collective-permute-start.20 = (bf16[64,512]{1,0:T(8,128)(2,1)S(1)}, bf16[64,512]{1,0:T(8,128)(2,1)S(1)}, u32[]{:S(2)}, u32[]{:S(2)}) collective-permute-start(bf16[64,512]{1,0:T(8,128)(2,1)S(1)} %get-tuple-element.46), channel_id=1, source_target_pairs={{0,1},{1,0},{2,3},{3,2},{4,5},{5,4},{6,7},{7,6},{8,9},{9,8},{10,11... | collective-permute-start | bytes 196616 | tf_op jit(solution)/shard_map/ppermute | solution.py:391
  62.3 2.0 %store.1 = (bf16[1,128,4096]{2,1,0:T(8,128)(2,1)}, bf16[1,128,4096]{2,1,0:T(8,128)(2,1)}, f32[8,128]{1,0:T(8,128)S(1)}) custom-call(bf16[64,1024]{1,0:T(8,128)(2,1)} %get-tuple-element.27.refs_0_, bf16[64,3072]{1,0:T(8,128)(2,1)S(1)} %get-tuple-element.23.refs_2_.refs_1_, bf16[64,1024]{1,0:T(8,128)(2,1)} %get-tuple-element.24.refs_2_, ...), custom_call_target="tpu_custom_call" | custom-call | tf_op jit(solution)/shard_map/store/pallas_call | solution.py:265
  64.4 3.7 %product.10 = (bf16[1,128,4096]{2,1,0:T(8,128)(2,1)}, bf16[1,128,4096]{2,1,0:T(8,128)(2,1)}, f32[8,128]{1,0:T(8,128)S(1)}) custom-call(s32[1,192]{1,0:T(1,128)S(1)} %get-tuple-element.57.refs_0_, bf16[64,512]{1,0:T(8,128)(2,1)S(1)} %collective-permute-done.18.refs_1_, ...), custom_call_target="tpu_custom_call", output_to_operand_aliasing={{0}: (6, {}), {1}: (7, {})} | custom-call | tf_op jit(solution)/shard_map/product/pallas_call | solution.py:265
  68.1 4.3 %product.11 = (bf16[1,128,4096]{2,1,0:T(8,128)(2,1)}, bf16[1,128,4096]{2,1,0:T(8,128)(2,1)}, f32[8,128]{1,0:T(8,128)}) custom-call(s32[1,192]{1,0:T(1,128)S(1)} %get-tuple-element.57.refs_0_, bf16[64,512]{1,0:T(8,128)(2,1)S(1)} %collective-permute-done.19.refs_1_, ...), custom_call_target="tpu_custom_call", output_to_operand_aliasing={{0}: (7, {}), {1}: (8, {})} | custom-call | tf_op jit(solution)/shard_map/product/pallas_call | solution.py:265
  (45 shorter events, 3.8 us)
Async XLA Ops:
  0.6 11.2 %copy-start.1 = (s32[1,192]{1,0:T(1,128)S(1)}, s32[1,192]{1,0:T(1,128)}, u32[]{:S(2)}) copy-start(s32[1,192]{1,0:T(1,128)} %param.11) | copy-start | bytes 2308
  3.3 7.9 %collective-permute-start.4 = (bf16[64,1024]{1,0:T(8,128)(2,1)}, bf16[64,1024]{1,0:T(8,128)(2,1)S(1)}, u32[]{:S(2)}, u32[]{:S(2)}) collective-permute-start(bf16[64,1024]{1,0:T(8,128)(2,1)} %get-tuple-element.27.refs_0_), channel_id=1, source_target_pairs={{0,8},{1,9},{2,10},{3,11},{4,12},{5,13},{6,14},{7,15},{8,0},{9,1},... | collective-permute-start | bytes 393224 | tf_op jit(solution)/shard_map/ppermute | solution.py:388
  6.7 13.0 %collective-permute-start.7 = (bf16[64,3072]{1,0:T(8,128)(2,1)S(1)}, bf16[64,3072]{1,0:T(8,128)(2,1)S(1)}, u32[]{:S(2)}, u32[]{:S(2)}) collective-permute-start(bf16[64,3072]{1,0:T(8,128)(2,1)S(1)} %get-tuple-element.23.refs_2_.refs_1_), channel_id=1, source_target_pairs={{0,8},{1,9},{2,10},{3,11},{4,12},{5,13},{6,14},{7,15},{8,0},{9,1},... | collective-permute-start | bytes 1179656 | tf_op jit(solution)/shard_map/ppermute | solution.py:388
  8.8 13.7 %collective-permute-start = (bf16[64,1024]{1,0:T(8,128)(2,1)}, bf16[64,1024]{1,0:T(8,128)(2,1)S(1)}, u32[]{:S(2)}, u32[]{:S(2)}) collective-permute-start(bf16[64,1024]{1,0:T(8,128)(2,1)} %get-tuple-element.24.refs_2_), channel_id=1, source_target_pairs={{0,8},{1,9},{2,10},{3,11},{4,12},{5,13},{6,14},{7,15},{8,0},{9,1},... | collective-permute-start | bytes 393224 | tf_op jit(solution)/shard_map/ppermute | solution.py:388
  11.1 19.1 %collective-permute-start.3 = (bf16[64,3072]{1,0:T(8,128)(2,1)S(1)}, bf16[64,3072]{1,0:T(8,128)(2,1)}, u32[]{:S(2)}, u32[]{:S(2)}) collective-permute-start(bf16[64,3072]{1,0:T(8,128)(2,1)S(1)} %get-tuple-element.25.refs_2_.refs_3_), channel_id=1, source_target_pairs={{0,8},{1,9},{2,10},{3,11},{4,12},{5,13},{6,14},{7,15},{8,0},{9,1},... | collective-permute-start | bytes 1179656 | tf_op jit(solution)/shard_map/ppermute | solution.py:388
  11.3 1.3 %collective-permute-start.5 = (bf16[64,512]{1,0:T(8,128)(2,1)S(1)}, bf16[64,512]{1,0:T(8,128)(2,1)S(1)}, u32[]{:S(2)}, u32[]{:S(2)}) collective-permute-start(bf16[64,512]{1,0:T(8,128)(2,1)S(1)} %get-tuple-element.53), channel_id=1, source_target_pairs={{0,1},{1,0},{2,3},{3,2},{4,5},{5,4},{6,7},{7,6},{8,15},{9,10},{10,... | collective-permute-start | bytes 196616 | tf_op jit(solution)/shard_map/ppermute | solution.py:399
  11.3 1.4 %collective-permute-start.6 = (bf16[64,512]{1,0:T(8,128)(2,1)S(1)}, bf16[64,512]{1,0:T(8,128)(2,1)S(1)}, u32[]{:S(2)}, u32[]{:S(2)}) collective-permute-start(bf16[64,512]{1,0:T(8,128)(2,1)S(1)} %get-tuple-element.52), channel_id=1, source_target_pairs={{0,1},{1,0},{2,3},{3,2},{4,5},{5,4},{6,7},{7,6},{8,9},{9,8},{10,11... | collective-permute-start | bytes 196616 | tf_op jit(solution)/shard_map/ppermute | solution.py:391
  20.2 2.8 %collective-permute-start.12 = (bf16[64,1024]{1,0:T(8,128)(2,1)S(1)}, bf16[64,1024]{1,0:T(8,128)(2,1)S(1)}, u32[]{:S(2)}, u32[]{:S(2)}) collective-permute-start(bf16[64,1024]{1,0:T(8,128)(2,1)S(1)} %get-tuple-element.32.refs_4_), channel_id=1, source_target_pairs={{0,1},{1,0},{2,3},{3,2},{4,5},{5,4},{6,7},{7,6},{8,16},{9,17},{10,... | collective-permute-start | bytes 393224 | tf_op jit(solution)/shard_map/ppermute | solution.py:388
  20.3 10.9 %collective-permute-start.15 = (bf16[64,3072]{1,0:T(8,128)(2,1)S(1)}, bf16[64,3072]{1,0:T(8,128)(2,1)S(1)}, u32[]{:S(2)}, u32[]{:S(2)}) collective-permute-start(bf16[64,3072]{1,0:T(8,128)(2,1)S(1)} %get-tuple-element.29.refs_7_.refs_5_), channel_id=1, source_target_pairs={{0,1},{1,0},{2,3},{3,2},{4,5},{5,4},{6,7},{7,6},{8,16},{9,17},{10,... | collective-permute-start | bytes 1179656 | tf_op jit(solution)/shard_map/ppermute | solution.py:388
  22.5 1.3 %collective-permute-start.1 = (bf16[64,512]{1,0:T(8,128)(2,1)S(1)}, bf16[64,512]{1,0:T(8,128)(2,1)S(1)}, u32[]{:S(2)}, u32[]{:S(2)}) collective-permute-start(bf16[64,512]{1,0:T(8,128)(2,1)S(1)} %get-tuple-element.55), channel_id=1, source_target_pairs={{0,1},{1,0},{2,3},{3,2},{4,5},{5,4},{6,7},{7,6},{8,15},{9,10},{10,... | collective-permute-start | bytes 196616 | tf_op jit(solution)/shard_map/ppermute | solution.py:399
  22.6 1.4 %collective-permute-start.2 = (bf16[64,512]{1,0:T(8,128)(2,1)S(1)}, bf16[64,512]{1,0:T(8,128)(2,1)S(1)}, u32[]{:S(2)}, u32[]{:S(2)}) collective-permute-start(bf16[64,512]{1,0:T(8,128)(2,1)S(1)} %get-tuple-element.54), channel_id=1, source_target_pairs={{0,1},{1,0},{2,3},{3,2},{4,5},{5,4},{6,7},{7,6},{8,9},{9,8},{10,11... | collective-permute-start | bytes 196616 | tf_op jit(solution)/shard_map/ppermute | solution.py:391
  23.1 8.1 %collective-permute-start.13 = (bf16[64,512]{1,0:T(8,128)(2,1)S(1)}, bf16[64,512]{1,0:T(8,128)(2,1)S(1)}, u32[]{:S(2)}, u32[]{:S(2)}) collective-permute-start(bf16[64,512]{1,0:T(8,128)(2,1)S(1)} %get-tuple-element.49), channel_id=1, source_target_pairs={{0,1},{1,0},{2,3},{3,2},{4,5},{5,4},{6,7},{7,6},{8,15},{9,10},{10,... | collective-permute-start | bytes 196616 | tf_op jit(solution)/shard_map/ppermute | solution.py:399
  23.8 7.4 %collective-permute-start.14 = (bf16[64,512]{1,0:T(8,128)(2,1)S(1)}, bf16[64,512]{1,0:T(8,128)(2,1)S(1)}, u32[]{:S(2)}, u32[]{:S(2)}) collective-permute-start(bf16[64,512]{1,0:T(8,128)(2,1)S(1)} %get-tuple-element.48), channel_id=1, source_target_pairs={{0,1},{1,0},{2,3},{3,2},{4,5},{5,4},{6,7},{7,6},{8,9},{9,8},{10,11... | collective-permute-start | bytes 196616 | tf_op jit(solution)/shard_map/ppermute | solution.py:391
  31.8 24.5 %collective-permute-start.17 = (bf16[64,4096]{1,0:T(8,128)(2,1)S(1)}, bf16[64,4096]{1,0:T(8,128)(2,1)S(1)}, u32[]{:S(2)}, u32[]{:S(2)}) collective-permute-start(bf16[64,4096]{1,0:T(8,128)(2,1)S(1)} %product.8.refs_2_.refs_8_), channel_id=1, source_target_pairs={{0,8},{1,9},{2,10},{3,11},{4,12},{5,13},{6,14},{7,15},{8,0},{9,1},... | collective-permute-start | bytes 1572872 | tf_op jit(solution)/shard_map/ppermute | solution.py:388
  40.5 1.3 %collective-permute-start.8 = (bf16[64,1024]{1,0:T(8,128)(2,1)S(1)}, bf16[64,1024]{1,0:T(8,128)(2,1)S(1)}, u32[]{:S(2)}, u32[]{:S(2)}) collective-permute-start(bf16[64,1024]{1,0:T(8,128)(2,1)S(1)} %get-tuple-element.30.refs_6_), channel_id=1, source_target_pairs={{0,1},{1,0},{2,3},{3,2},{4,5},{5,4},{6,7},{7,6},{8,16},{9,17},{10,... | collective-permute-start | bytes 393224 | tf_op jit(solution)/shard_map/ppermute | solution.py:388
  40.6 4.8 %collective-permute-start.11 = (bf16[64,3072]{1,0:T(8,128)(2,1)S(1)}, bf16[64,3072]{1,0:T(8,128)(2,1)S(1)}, u32[]{:S(2)}, u32[]{:S(2)}) collective-permute-start(bf16[64,3072]{1,0:T(8,128)(2,1)S(1)} %get-tuple-element.31.refs_7_), channel_id=1, source_target_pairs={{0,1},{1,0},{2,3},{3,2},{4,5},{5,4},{6,7},{7,6},{8,16},{9,17},{10,... | collective-permute-start | bytes 1179656 | tf_op jit(solution)/shard_map/ppermute | solution.py:388
  41.9 3.4 %collective-permute-start.10 = (bf16[64,512]{1,0:T(8,128)(2,1)S(1)}, bf16[64,512]{1,0:T(8,128)(2,1)S(1)}, u32[]{:S(2)}, u32[]{:S(2)}) collective-permute-start(bf16[64,512]{1,0:T(8,128)(2,1)S(1)} %get-tuple-element.50), channel_id=1, source_target_pairs={{0,1},{1,0},{2,3},{3,2},{4,5},{5,4},{6,7},{7,6},{8,9},{9,8},{10,11... | collective-permute-start | bytes 196616 | tf_op jit(solution)/shard_map/ppermute | solution.py:391
  42.1 3.2 %collective-permute-start.9 = (bf16[64,512]{1,0:T(8,128)(2,1)S(1)}, bf16[64,512]{1,0:T(8,128)(2,1)S(1)}, u32[]{:S(2)}, u32[]{:S(2)}) collective-permute-start(bf16[64,512]{1,0:T(8,128)(2,1)S(1)} %get-tuple-element.51), channel_id=1, source_target_pairs={{0,1},{1,0},{2,3},{3,2},{4,5},{5,4},{6,7},{7,6},{8,15},{9,10},{10,... | collective-permute-start | bytes 196616 | tf_op jit(solution)/shard_map/ppermute | solution.py:399
  45.9 14.6 %collective-permute-start.16 = (bf16[64,1024]{1,0:T(8,128)(2,1)S(1)}, bf16[64,1024]{1,0:T(8,128)(2,1)S(1)}, u32[]{:S(2)}, u32[]{:S(2)}) collective-permute-start(bf16[64,1024]{1,0:T(8,128)(2,1)S(1)} %get-tuple-element.33.refs_9_), channel_id=1, source_target_pairs={{0,8},{1,9},{2,10},{3,11},{4,12},{5,13},{6,14},{7,15},{8,0},{9,1},... | collective-permute-start | bytes 393224 | tf_op jit(solution)/shard_map/ppermute | solution.py:388
  56.3 11.8 %collective-permute-start.21 = (bf16[64,3072]{1,0:T(8,128)(2,1)S(1)}, bf16[64,3072]{1,0:T(8,128)(2,1)S(1)}, u32[]{:S(2)}, u32[]{:S(2)}) collective-permute-start(bf16[64,3072]{1,0:T(8,128)(2,1)S(1)} %get-tuple-element.35.refs_10_.refs_11_), channel_id=1, source_target_pairs={{0,8},{1,9},{2,10},{3,11},{4,12},{5,13},{6,14},{7,15},{8,0},{9,1},... | collective-permute-start | bytes 1179656 | tf_op jit(solution)/shard_map/ppermute | solution.py:388
  56.4 4.7 %collective-permute-start.18 = (bf16[64,512]{1,0:T(8,128)(2,1)S(1)}, bf16[64,512]{1,0:T(8,128)(2,1)S(1)}, u32[]{:S(2)}, u32[]{:S(2)}) collective-permute-start(bf16[64,512]{1,0:T(8,128)(2,1)S(1)} %get-tuple-element.45), channel_id=1, source_target_pairs={{0,7},{1,2},{2,1},{3,4},{4,3},{5,6},{6,5},{7,0},{8,9},{9,8},{10,11... | collective-permute-start | bytes 196616 | tf_op jit(solution)/shard_map/ppermute | solution.py:399
  56.5 7.9 %collective-permute-start.22 = (bf16[64,512]{1,0:T(8,128)(2,1)S(1)}, bf16[64,512]{1,0:T(8,128)(2,1)S(1)}, u32[]{:S(2)}, u32[]{:S(2)}) collective-permute-start(bf16[64,512]{1,0:T(8,128)(2,1)S(1)} %get-tuple-element.44), channel_id=1, source_target_pairs={{0,1},{1,0},{2,3},{3,2},{4,5},{5,4},{6,7},{7,6},{8,9},{9,8},{10,11... | collective-permute-start | bytes 196616 | tf_op jit(solution)/shard_map/ppermute | solution.py:391
  61.0 7.0 %collective-permute-start.19 = (bf16[64,512]{1,0:T(8,128)(2,1)S(1)}, bf16[64,512]{1,0:T(8,128)(2,1)S(1)}, u32[]{:S(2)}, u32[]{:S(2)}) collective-permute-start(bf16[64,512]{1,0:T(8,128)(2,1)S(1)} %get-tuple-element.47), channel_id=1, source_target_pairs={{0,7},{1,2},{2,1},{3,4},{4,3},{5,6},{6,5},{7,0},{8,9},{9,8},{10,11... | collective-permute-start | bytes 196616 | tf_op jit(solution)/shard_map/ppermute | solution.py:399
  61.1 7.0 %collective-permute-start.20 = (bf16[64,512]{1,0:T(8,128)(2,1)S(1)}, bf16[64,512]{1,0:T(8,128)(2,1)S(1)}, u32[]{:S(2)}, u32[]{:S(2)}) collective-permute-start(bf16[64,512]{1,0:T(8,128)(2,1)S(1)} %get-tuple-element.46), channel_id=1, source_target_pairs={{0,1},{1,0},{2,3},{3,2},{4,5},{5,4},{6,7},{7,6},{8,9},{9,8},{10,11... | collective-permute-start | bytes 196616 | tf_op jit(solution)/shard_map/ppermute | solution.py:391
  (1 other events, 11.2 us)

commit v5 on v4

--- a/solution.py
+++ b/solution.py
@@ -272,7 +272,7 @@
             compiler_params=params(mib),
             name=name,
         )(*ins)
-        token[:] = [out[-1]]
+        token[:] = [out[0 if name == "source" else -1]]
         return out
 
     def trace(rows, split):

time: 72.7 us -> 72.6 us (level)
  no operation moved by 1% of the time
where the time goes in v5:
time: 72.6 us; the launch traced here: 72.5 us
  starting transfers between devices  31.2 us (43%)
  waiting for transfers between devices  20 us (28%)
  Pallas kernels  19.7 us (27%)
  between operations  1.54 us (2%)
    ppermute x11, starting transfers between devices, hop(): return lax.ppermute(x, ('slab', 'cross'), route)  26.2 us
    pallas_call x12, Pallas kernels, launch(): pl.pallas_call(body, out_shape=out_shape, in_specs=in_specs, out_specs=ou...  19.7 us
    ppermute x11, waiting for transfers between devices, hop(): return lax.ppermute(x, ('slab', 'cross'), route)  18.2 us
    ppermute x6, starting transfers between devices, to_mate(): return lax.ppermute(x, 'cross', [(c, mate(c)) for c in range(cross)])  3.94 us
    ppermute x6, waiting for transfers between devices, to_next_chip(): return lax.ppermute(x, ('slab', 'cross'), route)  1.64 us
  transfers between devices with their start and end apart: 23, of which 10 were waited for; matrix products, arithmetic and copies ran while one was open for 0% of the time, Pallas kernels for 18%

profile of v5, /device:TPU:0, one launch (start us, length us, event | category | flops | bytes accessed | tf_op | source)
XLA Modules:
  0.0 72.5 jit_solution(16357377080331881851)
XLA Ops:
  1.3 2.1 %source.2 = (f32[64,4096]{1,0:T(8,128)S(1)}, bf16[64,1024]{1,0:T(8,128)(2,1)}, bf16[64,3072]{1,0:T(8,128)(2,1)S(1)}) custom-call(s32[1]{0:T(128)S(6)} %copy.16.refs_0_, bf16[4,128,4096]{2,1,0:T(8,128)(2,1)} %refs_1_.6), custom_call_target="tpu_custom_call" | custom-call | tf_op jit(solution)/shard_map/source/pallas_call | solution.py:265
  3.5 2.9 %collective-permute-start.4 = (bf16[64,1024]{1,0:T(8,128)(2,1)}, bf16[64,1024]{1,0:T(8,128)(2,1)S(1)}, u32[]{:S(2)}, u32[]{:S(2)}) collective-permute-start(bf16[64,1024]{1,0:T(8,128)(2,1)} %get-tuple-element.27.refs_0_), channel_id=1, source_target_pairs={{0,8},{1,9},{2,10},{3,11},{4,12},{5,13},{6,14},{7,15},{8,0},{9,1},... | collective-permute-start | bytes 393224 | tf_op jit(solution)/shard_map/ppermute | solution.py:388
  6.5 2.3 %source.3 = (f32[64,4096]{1,0:T(8,128)S(1)}, bf16[64,1024]{1,0:T(8,128)(2,1)}, bf16[64,3072]{1,0:T(8,128)(2,1)}) custom-call(s32[1]{0:T(128)S(6)} %copy.16.refs_0_, bf16[4,128,4096]{2,1,0:T(8,128)(2,1)} %refs_1_.6, f32[64,4096]{1,0:T(8,128)S(1)} %get-tuple-element.23.refs_2_.refs_6_.refs_5_), custom_call_target="tpu_custom_call" | custom-call | tf_op jit(solution)/shard_map/source/pallas_call | solution.py:265
  8.8 1.9 %collective-permute-start = (bf16[64,1024]{1,0:T(8,128)(2,1)}, bf16[64,1024]{1,0:T(8,128)(2,1)S(1)}, u32[]{:S(2)}, u32[]{:S(2)}) collective-permute-start(bf16[64,1024]{1,0:T(8,128)(2,1)} %get-tuple-element.24.refs_2_), channel_id=1, source_target_pairs={{0,8},{1,9},{2,10},{3,11},{4,12},{5,13},{6,14},{7,15},{8,0},{9,1},... | collective-permute-start | bytes 393224 | tf_op jit(solution)/shard_map/ppermute | solution.py:388
  11.6 0.7 collective-permute-done.5.refs_1_
  12.4 6.9 %collective-permute-done.7.refs_4_ = bf16[64,3072]{1,0:T(8,128)(2,1)S(1)} collective-permute-done((bf16[64,3072]{1,0:T(8,128)(2,1)S(1)}, bf16[64,3072]{1,0:T(8,128)(2,1)S(1)}, u32[]{:S(2)}, u32[]{:S(2)}) %collective-permute-start.7) | collective-permute-done | bytes 393248 | tf_op jit(solution)/shard_map/ppermute | solution.py:388
  19.4 0.6 product.6
  20.5 1.7 %collective-permute-done.refs_3_ = bf16[64,1024]{1,0:T(8,128)(2,1)S(1)} collective-permute-done((bf16[64,1024]{1,0:T(8,128)(2,1)}, bf16[64,1024]{1,0:T(8,128)(2,1)S(1)}, u32[]{:S(2)}, u32[]{:S(2)}) %collective-permute-start) | collective-permute-done | bytes 131104 | tf_op jit(solution)/shard_map/ppermute | solution.py:388
  22.9 0.6 collective-permute-done.1.refs_1_
  23.7 6.1 %collective-permute-done.3.refs_4_ = bf16[64,3072]{1,0:T(8,128)(2,1)S(1)} collective-permute-done((bf16[64,3072]{1,0:T(8,128)(2,1)}, bf16[64,3072]{1,0:T(8,128)(2,1)S(1)}, u32[]{:S(2)}, u32[]{:S(2)}) %collective-permute-start.3) | collective-permute-done | bytes 393248 | tf_op jit(solution)/shard_map/ppermute | solution.py:388
  29.8 0.6 product.7
  30.4 0.6 product.8.refs_2_.refs_8_
  30.9 9.8 %collective-permute-start.17 = (bf16[64,4096]{1,0:T(8,128)(2,1)S(1)}, bf16[64,4096]{1,0:T(8,128)(2,1)S(1)}, u32[]{:S(2)}, u32[]{:S(2)}) collective-permute-start(bf16[64,4096]{1,0:T(8,128)(2,1)S(1)} %product.8.refs_2_.refs_8_), channel_id=1, source_target_pairs={{0,8},{1,9},{2,10},{3,11},{4,12},{5,13},{6,14},{7,15},{8,0},{9,1},... | collective-permute-start | bytes 1572872 | tf_op jit(solution)/shard_map/ppermute | solution.py:388
  40.8 0.5 collective-permute-start.11
  41.3 0.8 %collective-permute-done.8.refs_3_ = bf16[64,1024]{1,0:T(8,128)(2,1)S(1)} collective-permute-done((bf16[64,1024]{1,0:T(8,128)(2,1)S(1)}, bf16[64,1024]{1,0:T(8,128)(2,1)S(1)}, u32[]{:S(2)}, u32[]{:S(2)}) %collective-permute-start.8) | collective-permute-done | bytes 131104 | tf_op jit(solution)/shard_map/ppermute | solution.py:388
  42.7 2.8 %fetch.5.refs_7_.refs_4_.refs_5_ = bf16[192,128,128]{2,1,0:T(8,128)(2,1)S(1)} custom-call(bf16[1,192,128,128]{3,2,1,0:T(8,128)(2,1)} %refs_0_.7, bf16[1,192,128,128]{3,2,1,0:T(8,128)(2,1)} %refs_1_.9, bf16[64,4096]{1,0:T(8,128)(2,1)S(1)} %product.8.refs_2_.refs_8_), custom_call_target="tpu_custom_call" | custom-call | tf_op jit(solution)/shard_map/fetch/pallas_call | solution.py:265
  45.5 0.6 product.9
  46.1 10.2 %collective-permute-start.16 = (bf16[64,1024]{1,0:T(8,128)(2,1)S(1)}, bf16[64,1024]{1,0:T(8,128)(2,1)S(1)}, u32[]{:S(2)}, u32[]{:S(2)}) collective-permute-start(bf16[64,1024]{1,0:T(8,128)(2,1)S(1)} %get-tuple-element.33.refs_9_), channel_id=1, source_target_pairs={{0,8},{1,9},{2,10},{3,11},{4,12},{5,13},{6,14},{7,15},{8,0},{9,1},... | collective-permute-start | bytes 393224 | tf_op jit(solution)/shard_map/ppermute | solution.py:388
  56.6 1.5 %collective-permute-start.22 = (bf16[64,512]{1,0:T(8,128)(2,1)S(1)}, bf16[64,512]{1,0:T(8,128)(2,1)S(1)}, u32[]{:S(2)}, u32[]{:S(2)}) collective-permute-start(bf16[64,512]{1,0:T(8,128)(2,1)S(1)} %get-tuple-element.44), channel_id=1, source_target_pairs={{0,1},{1,0},{2,3},{3,2},{4,5},{5,4},{6,7},{7,6},{8,9},{9,8},{10,11... | collective-permute-start | bytes 196616 | tf_op jit(solution)/shard_map/ppermute | solution.py:391
  58.0 2.6 %collective-permute-done.16.refs_3_ = bf16[64,1024]{1,0:T(8,128)(2,1)S(1)} collective-permute-done((bf16[64,1024]{1,0:T(8,128)(2,1)S(1)}, bf16[64,1024]{1,0:T(8,128)(2,1)S(1)}, u32[]{:S(2)}, u32[]{:S(2)}) %collective-permute-start.16) | collective-permute-done | bytes 131104 | tf_op jit(solution)/shard_map/ppermute | solution.py:388
  61.2 1.1 %collective-permute-start.20 = (bf16[64,512]{1,0:T(8,128)(2,1)S(1)}, bf16[64,512]{1,0:T(8,128)(2,1)S(1)}, u32[]{:S(2)}, u32[]{:S(2)}) collective-permute-start(bf16[64,512]{1,0:T(8,128)(2,1)S(1)} %get-tuple-element.46), channel_id=1, source_target_pairs={{0,1},{1,0},{2,3},{3,2},{4,5},{5,4},{6,7},{7,6},{8,9},{9,8},{10,11... | collective-permute-start | bytes 196616 | tf_op jit(solution)/shard_map/ppermute | solution.py:391
  62.3 2.2 %store.1 = (bf16[1,128,4096]{2,1,0:T(8,128)(2,1)}, bf16[1,128,4096]{2,1,0:T(8,128)(2,1)}, f32[8,128]{1,0:T(8,128)S(1)}) custom-call(bf16[64,1024]{1,0:T(8,128)(2,1)} %get-tuple-element.27.refs_0_, bf16[64,3072]{1,0:T(8,128)(2,1)S(1)} %get-tuple-element.28.refs_1_, bf16[64,1024]{1,0:T(8,128)(2,1)} %get-tuple-element.24.refs_2_, ...), custom_call_target="tpu_custom_call" | custom-call | tf_op jit(solution)/shard_map/store/pallas_call | solution.py:265
  64.5 3.7 %product.10 = (bf16[1,128,4096]{2,1,0:T(8,128)(2,1)}, bf16[1,128,4096]{2,1,0:T(8,128)(2,1)}, f32[8,128]{1,0:T(8,128)S(1)}) custom-call(s32[1,192]{1,0:T(1,128)S(1)} %get-tuple-element.57.refs_0_, bf16[64,512]{1,0:T(8,128)(2,1)S(1)} %collective-permute-done.18.refs_1_, ...), custom_call_target="tpu_custom_call", output_to_operand_aliasing={{0}: (6, {}), {1}: (7, {})} | custom-call | tf_op jit(solution)/shard_map/product/pallas_call | solution.py:265
  68.2 4.3 %product.11 = (bf16[1,128,4096]{2,1,0:T(8,128)(2,1)}, bf16[1,128,4096]{2,1,0:T(8,128)(2,1)}, f32[8,128]{1,0:T(8,128)}) custom-call(s32[1,192]{1,0:T(1,128)S(1)} %get-tuple-element.57.refs_0_, bf16[64,512]{1,0:T(8,128)(2,1)S(1)} %collective-permute-done.19.refs_1_, ...), custom_call_target="tpu_custom_call", output_to_operand_aliasing={{0}: (7, {}), {1}: (8, {})} | custom-call | tf_op jit(solution)/shard_map/product/pallas_call | solution.py:265
  (45 shorter events, 4.2 us)
Async XLA Ops:
  0.6 10.9 %copy-start.1 = (s32[1,192]{1,0:T(1,128)S(1)}, s32[1,192]{1,0:T(1,128)}, u32[]{:S(2)}) copy-start(s32[1,192]{1,0:T(1,128)} %param.11) | copy-start | bytes 2308
  3.5 7.5 %collective-permute-start.4 = (bf16[64,1024]{1,0:T(8,128)(2,1)}, bf16[64,1024]{1,0:T(8,128)(2,1)S(1)}, u32[]{:S(2)}, u32[]{:S(2)}) collective-permute-start(bf16[64,1024]{1,0:T(8,128)(2,1)} %get-tuple-element.27.refs_0_), channel_id=1, source_target_pairs={{0,8},{1,9},{2,10},{3,11},{4,12},{5,13},{6,14},{7,15},{8,0},{9,1},... | collective-permute-start | bytes 393224 | tf_op jit(solution)/shard_map/ppermute | solution.py:388
  6.4 13.0 %collective-permute-start.7 = (bf16[64,3072]{1,0:T(8,128)(2,1)S(1)}, bf16[64,3072]{1,0:T(8,128)(2,1)S(1)}, u32[]{:S(2)}, u32[]{:S(2)}) collective-permute-start(bf16[64,3072]{1,0:T(8,128)(2,1)S(1)} %get-tuple-element.28.refs_1_), channel_id=1, source_target_pairs={{0,8},{1,9},{2,10},{3,11},{4,12},{5,13},{6,14},{7,15},{8,0},{9,1},... | collective-permute-start | bytes 1179656 | tf_op jit(solution)/shard_map/ppermute | solution.py:388
  8.8 13.4 %collective-permute-start = (bf16[64,1024]{1,0:T(8,128)(2,1)}, bf16[64,1024]{1,0:T(8,128)(2,1)S(1)}, u32[]{:S(2)}, u32[]{:S(2)}) collective-permute-start(bf16[64,1024]{1,0:T(8,128)(2,1)} %get-tuple-element.24.refs_2_), channel_id=1, source_target_pairs={{0,8},{1,9},{2,10},{3,11},{4,12},{5,13},{6,14},{7,15},{8,0},{9,1},... | collective-permute-start | bytes 393224 | tf_op jit(solution)/shard_map/ppermute | solution.py:388
  10.6 19.1 %collective-permute-start.3 = (bf16[64,3072]{1,0:T(8,128)(2,1)}, bf16[64,3072]{1,0:T(8,128)(2,1)S(1)}, u32[]{:S(2)}, u32[]{:S(2)}) collective-permute-start(bf16[64,3072]{1,0:T(8,128)(2,1)} %get-tuple-element.25.refs_3_), channel_id=1, source_target_pairs={{0,8},{1,9},{2,10},{3,11},{4,12},{5,13},{6,14},{7,15},{8,0},{9,1},... | collective-permute-start | bytes 1179656 | tf_op jit(solution)/shard_map/ppermute | solution.py:388
  10.9 1.3 %collective-permute-start.5 = (bf16[64,512]{1,0:T(8,128)(2,1)S(1)}, bf16[64,512]{1,0:T(8,128)(2,1)S(1)}, u32[]{:S(2)}, u32[]{:S(2)}) collective-permute-start(bf16[64,512]{1,0:T(8,128)(2,1)S(1)} %get-tuple-element.53), channel_id=1, source_target_pairs={{0,1},{1,0},{2,3},{3,2},{4,5},{5,4},{6,7},{7,6},{8,15},{9,10},{10,... | collective-permute-start | bytes 196616 | tf_op jit(solution)/shard_map/ppermute | solution.py:399
  11.0 1.4 %collective-permute-start.6 = (bf16[64,512]{1,0:T(8,128)(2,1)S(1)}, bf16[64,512]{1,0:T(8,128)(2,1)S(1)}, u32[]{:S(2)}, u32[]{:S(2)}) collective-permute-start(bf16[64,512]{1,0:T(8,128)(2,1)S(1)} %get-tuple-element.52), channel_id=1, source_target_pairs={{0,1},{1,0},{2,3},{3,2},{4,5},{5,4},{6,7},{7,6},{8,9},{9,8},{10,11... | collective-permute-start | bytes 196616 | tf_op jit(solution)/shard_map/ppermute | solution.py:391
  19.9 2.8 %collective-permute-start.12 = (bf16[64,1024]{1,0:T(8,128)(2,1)S(1)}, bf16[64,1024]{1,0:T(8,128)(2,1)S(1)}, u32[]{:S(2)}, u32[]{:S(2)}) collective-permute-start(bf16[64,1024]{1,0:T(8,128)(2,1)S(1)} %get-tuple-element.32.refs_4_), channel_id=1, source_target_pairs={{0,1},{1,0},{2,3},{3,2},{4,5},{5,4},{6,7},{7,6},{8,16},{9,17},{10,... | collective-permute-start | bytes 393224 | tf_op jit(solution)/shard_map/ppermute | solution.py:388
  20.0 10.4 %collective-permute-start.15 = (bf16[64,3072]{1,0:T(8,128)(2,1)S(1)}, bf16[64,3072]{1,0:T(8,128)(2,1)S(1)}, u32[]{:S(2)}, u32[]{:S(2)}) collective-permute-start(bf16[64,3072]{1,0:T(8,128)(2,1)S(1)} %get-tuple-element.29.refs_7_.refs_5_), channel_id=1, source_target_pairs={{0,1},{1,0},{2,3},{3,2},{4,5},{5,4},{6,7},{7,6},{8,16},{9,17},{10,... | collective-permute-start | bytes 1179656 | tf_op jit(solution)/shard_map/ppermute | solution.py:388
  22.2 1.3 %collective-permute-start.1 = (bf16[64,512]{1,0:T(8,128)(2,1)S(1)}, bf16[64,512]{1,0:T(8,128)(2,1)S(1)}, u32[]{:S(2)}, u32[]{:S(2)}) collective-permute-start(bf16[64,512]{1,0:T(8,128)(2,1)S(1)} %get-tuple-element.55), channel_id=1, source_target_pairs={{0,1},{1,0},{2,3},{3,2},{4,5},{5,4},{6,7},{7,6},{8,15},{9,10},{10,... | collective-permute-start | bytes 196616 | tf_op jit(solution)/shard_map/ppermute | solution.py:399
  22.3 1.4 %collective-permute-start.2 = (bf16[64,512]{1,0:T(8,128)(2,1)S(1)}, bf16[64,512]{1,0:T(8,128)(2,1)S(1)}, u32[]{:S(2)}, u32[]{:S(2)}) collective-permute-start(bf16[64,512]{1,0:T(8,128)(2,1)S(1)} %get-tuple-element.54), channel_id=1, source_target_pairs={{0,1},{1,0},{2,3},{3,2},{4,5},{5,4},{6,7},{7,6},{8,9},{9,8},{10,11... | collective-permute-start | bytes 196616 | tf_op jit(solution)/shard_map/ppermute | solution.py:391
  22.8 7.6 %collective-permute-start.13 = (bf16[64,512]{1,0:T(8,128)(2,1)S(1)}, bf16[64,512]{1,0:T(8,128)(2,1)S(1)}, u32[]{:S(2)}, u32[]{:S(2)}) collective-permute-start(bf16[64,512]{1,0:T(8,128)(2,1)S(1)} %get-tuple-element.49), channel_id=1, source_target_pairs={{0,1},{1,0},{2,3},{3,2},{4,5},{5,4},{6,7},{7,6},{8,15},{9,10},{10,... | collective-permute-start | bytes 196616 | tf_op jit(solution)/shard_map/ppermute | solution.py:399
  23.5 6.8 %collective-permute-start.14 = (bf16[64,512]{1,0:T(8,128)(2,1)S(1)}, bf16[64,512]{1,0:T(8,128)(2,1)S(1)}, u32[]{:S(2)}, u32[]{:S(2)}) collective-permute-start(bf16[64,512]{1,0:T(8,128)(2,1)S(1)} %get-tuple-element.48), channel_id=1, source_target_pairs={{0,1},{1,0},{2,3},{3,2},{4,5},{5,4},{6,7},{7,6},{8,9},{9,8},{10,11... | collective-permute-start | bytes 196616 | tf_op jit(solution)/shard_map/ppermute | solution.py:391
  30.9 25.4 %collective-permute-start.17 = (bf16[64,4096]{1,0:T(8,128)(2,1)S(1)}, bf16[64,4096]{1,0:T(8,128)(2,1)S(1)}, u32[]{:S(2)}, u32[]{:S(2)}) collective-permute-start(bf16[64,4096]{1,0:T(8,128)(2,1)S(1)} %product.8.refs_2_.refs_8_), channel_id=1, source_target_pairs={{0,8},{1,9},{2,10},{3,11},{4,12},{5,13},{6,14},{7,15},{8,0},{9,1},... | collective-permute-start | bytes 1572872 | tf_op jit(solution)/shard_map/ppermute | solution.py:388
  40.8 1.3 %collective-permute-start.8 = (bf16[64,1024]{1,0:T(8,128)(2,1)S(1)}, bf16[64,1024]{1,0:T(8,128)(2,1)S(1)}, u32[]{:S(2)}, u32[]{:S(2)}) collective-permute-start(bf16[64,1024]{1,0:T(8,128)(2,1)S(1)} %get-tuple-element.30.refs_6_), channel_id=1, source_target_pairs={{0,1},{1,0},{2,3},{3,2},{4,5},{5,4},{6,7},{7,6},{8,16},{9,17},{10,... | collective-permute-start | bytes 393224 | tf_op jit(solution)/shard_map/ppermute | solution.py:388
  40.8 4.8 %collective-permute-start.11 = (bf16[64,3072]{1,0:T(8,128)(2,1)S(1)}, bf16[64,3072]{1,0:T(8,128)(2,1)S(1)}, u32[]{:S(2)}, u32[]{:S(2)}) collective-permute-start(bf16[64,3072]{1,0:T(8,128)(2,1)S(1)} %get-tuple-element.31.refs_7_), channel_id=1, source_target_pairs={{0,1},{1,0},{2,3},{3,2},{4,5},{5,4},{6,7},{7,6},{8,16},{9,17},{10,... | collective-permute-start | bytes 1179656 | tf_op jit(solution)/shard_map/ppermute | solution.py:388
  42.1 3.4 %collective-permute-start.10 = (bf16[64,512]{1,0:T(8,128)(2,1)S(1)}, bf16[64,512]{1,0:T(8,128)(2,1)S(1)}, u32[]{:S(2)}, u32[]{:S(2)}) collective-permute-start(bf16[64,512]{1,0:T(8,128)(2,1)S(1)} %get-tuple-element.50), channel_id=1, source_target_pairs={{0,1},{1,0},{2,3},{3,2},{4,5},{5,4},{6,7},{7,6},{8,9},{9,8},{10,11... | collective-permute-start | bytes 196616 | tf_op jit(solution)/shard_map/ppermute | solution.py:391
  42.3 3.2 %collective-permute-start.9 = (bf16[64,512]{1,0:T(8,128)(2,1)S(1)}, bf16[64,512]{1,0:T(8,128)(2,1)S(1)}, u32[]{:S(2)}, u32[]{:S(2)}) collective-permute-start(bf16[64,512]{1,0:T(8,128)(2,1)S(1)} %get-tuple-element.51), channel_id=1, source_target_pairs={{0,1},{1,0},{2,3},{3,2},{4,5},{5,4},{6,7},{7,6},{8,15},{9,10},{10,... | collective-permute-start | bytes 196616 | tf_op jit(solution)/shard_map/ppermute | solution.py:399
  46.1 14.5 %collective-permute-start.16 = (bf16[64,1024]{1,0:T(8,128)(2,1)S(1)}, bf16[64,1024]{1,0:T(8,128)(2,1)S(1)}, u32[]{:S(2)}, u32[]{:S(2)}) collective-permute-start(bf16[64,1024]{1,0:T(8,128)(2,1)S(1)} %get-tuple-element.33.refs_9_), channel_id=1, source_target_pairs={{0,8},{1,9},{2,10},{3,11},{4,12},{5,13},{6,14},{7,15},{8,0},{9,1},... | collective-permute-start | bytes 393224 | tf_op jit(solution)/shard_map/ppermute | solution.py:388
  56.3 12.0 %collective-permute-start.21 = (bf16[64,3072]{1,0:T(8,128)(2,1)S(1)}, bf16[64,3072]{1,0:T(8,128)(2,1)S(1)}, u32[]{:S(2)}, u32[]{:S(2)}) collective-permute-start(bf16[64,3072]{1,0:T(8,128)(2,1)S(1)} %get-tuple-element.35.refs_10_.refs_11_), channel_id=1, source_target_pairs={{0,8},{1,9},{2,10},{3,11},{4,12},{5,13},{6,14},{7,15},{8,0},{9,1},... | collective-permute-start | bytes 1179656 | tf_op jit(solution)/shard_map/ppermute | solution.py:388
  56.4 4.7 %collective-permute-start.18 = (bf16[64,512]{1,0:T(8,128)(2,1)S(1)}, bf16[64,512]{1,0:T(8,128)(2,1)S(1)}, u32[]{:S(2)}, u32[]{:S(2)}) collective-permute-start(bf16[64,512]{1,0:T(8,128)(2,1)S(1)} %get-tuple-element.45), channel_id=1, source_target_pairs={{0,7},{1,2},{2,1},{3,4},{4,3},{5,6},{6,5},{7,0},{8,9},{9,8},{10,11... | collective-permute-start | bytes 196616 | tf_op jit(solution)/shard_map/ppermute | solution.py:399
  56.6 8.0 %collective-permute-start.22 = (bf16[64,512]{1,0:T(8,128)(2,1)S(1)}, bf16[64,512]{1,0:T(8,128)(2,1)S(1)}, u32[]{:S(2)}, u32[]{:S(2)}) collective-permute-start(bf16[64,512]{1,0:T(8,128)(2,1)S(1)} %get-tuple-element.44), channel_id=1, source_target_pairs={{0,1},{1,0},{2,3},{3,2},{4,5},{5,4},{6,7},{7,6},{8,9},{9,8},{10,11... | collective-permute-start | bytes 196616 | tf_op jit(solution)/shard_map/ppermute | solution.py:391
  61.0 7.2 %collective-permute-start.19 = (bf16[64,512]{1,0:T(8,128)(2,1)S(1)}, bf16[64,512]{1,0:T(8,128)(2,1)S(1)}, u32[]{:S(2)}, u32[]{:S(2)}) collective-permute-start(bf16[64,512]{1,0:T(8,128)(2,1)S(1)} %get-tuple-element.47), channel_id=1, source_target_pairs={{0,7},{1,2},{2,1},{3,4},{4,3},{5,6},{6,5},{7,0},{8,9},{9,8},{10,11... | collective-permute-start | bytes 196616 | tf_op jit(solution)/shard_map/ppermute | solution.py:399
  61.2 7.0 %collective-permute-start.20 = (bf16[64,512]{1,0:T(8,128)(2,1)S(1)}, bf16[64,512]{1,0:T(8,128)(2,1)S(1)}, u32[]{:S(2)}, u32[]{:S(2)}) collective-permute-start(bf16[64,512]{1,0:T(8,128)(2,1)S(1)} %get-tuple-element.46), channel_id=1, source_target_pairs={{0,1},{1,0},{2,3},{3,2},{4,5},{5,4},{6,7},{7,6},{8,9},{9,8},{10,11... | collective-permute-start | bytes 196616 | tf_op jit(solution)/shard_map/ppermute | solution.py:391
  (1 other events, 10.9 us)
